TPU v7x, 32 devices: a whole 2x2x4 slice. The times are simulated.
32 devices in a mesh: comp: 4 (over z), tile: 8 (over y, x, core).
Axes of the slice: x: 2, y: 2, z: 4, core: 2. Of those that a mesh axis runs over, the one named last changes fastest.
Arguments:
- atmos_state: float32 [4, 32, 32, 1024], P(None, None, 'comp', 'tile'), may hold values from -6 to 6
- ocean_state: float32 [4, 8, 64, 1024], P(None, None, 'comp', 'tile'), may hold values from -6 to 6
- flux_coef: float32 [4], replicated, may hold values from 0.5 to 2
- remap_weight: bfloat16 [384, 128, 128], P(('comp', 'tile')), may hold values from -0.5 to 0.5
- source_row: int32 [384], P(('comp', 'tile')), may hold values from 0 to 7
- target_device: int32 [384, 1], P(('comp', 'tile')), may hold values from 0 to 7; in each aligned block of 12 rows (0 to 11, 12 to 23, ...) at most 3 rows name the same one
- target_row: int32 [384], P(('comp', 'tile')), may hold values from 0 to 15
Outputs:
- atmos_next: float32 [4, 32, 32, 1024], P(None, None, 'comp', 'tile')
- ocean_next: float32 [4, 8, 64, 1024], P(None, None, 'comp', 'tile')
Inputs may be any that keep to these rules, and one draw needn't show every extreme that they name: `target_device`: among the items of one device no target device is named more than 3 times, and some target device is named exactly 3 times.
All inputs are finite; a program needn't handle non-finite values.
Results may differ from a plain program's by a relative error of at most 0.0024.
Values sent between devices are 32-bit elements; how exact they have to be, the bound alone decides.
No kernel may reach another device: no remote copies, remote signals or barrier semaphores. Data moves between devices by JAX's collectives and lax.ppermute only.
A program may use at most 64 MiB of HBM per device.

v0:
```python
import jax
import jax.numpy as jnp
from jax import lax
from jax.sharding import PartitionSpec as P

viscosity = 0.01
diffusion = 0.2
mixing_rate = 0.1
forcing_step = 0.5


def with_halo(cells, sides, width, closed):
    for axis, dim in sides:
        count = lax.axis_size(axis)
        ends = count if closed else count - 1
        head = lax.slice_in_dim(cells, 0, width, axis=dim)
        tail = lax.slice_in_dim(cells, cells.shape[dim] - width, cells.shape[dim], axis=dim)
        cells = jnp.concatenate(
            [
                lax.ppermute(tail, axis, [(i, (i + 1) % count) for i in range(ends)]),
                cells,
                lax.ppermute(head, axis, [((i + 1) % count, i) for i in range(ends)]),
            ],
            axis=dim,
        )
    return cells


def gll_second():
    nodes = [-1.0, -(0.2**0.5), 0.2**0.5, 1.0]
    derivative = []
    for outer_pos in range(4):
        entries = []
        for inner_pos in range(4):
            if outer_pos == inner_pos:
                value = sum(
                    (
                        1.0 / (nodes[outer_pos] - nodes[other])
                        for other in range(4)
                        if other != outer_pos
                    )
                )
            else:
                numerator = 1.0
                for other in range(4):
                    if other != outer_pos and other != inner_pos:
                        numerator = numerator * (nodes[outer_pos] - nodes[other])
                denominator = 1.0
                for other in range(4):
                    if other != inner_pos:
                        denominator = denominator * (nodes[inner_pos] - nodes[other])
                value = numerator / denominator
            entries.append(value)
        derivative.append(entries)
    squared = []
    for outer_pos in range(4):
        squared.append(
            [
                sum(
                    (
                        derivative[outer_pos][middle] * derivative[middle][inner_pos]
                        for middle in range(4)
                    )
                )
                for inner_pos in range(4)
            ]
        )
    return squared


def block_matrix(length, table):
    rows_at = lax.broadcasted_iota(jnp.int32, (length, length), 0)
    cols_at = lax.broadcasted_iota(jnp.int32, (length, length), 1)
    inside = rows_at // 4 == cols_at // 4
    matrix = jnp.zeros((length, length), jnp.float32)
    for outer_pos in range(4):
        for inner_pos in range(4):
            picked = inside & (rows_at % 4 == outer_pos) & (cols_at % 4 == inner_pos)
            matrix = jnp.where(picked, table[outer_pos][inner_pos], matrix)
    return matrix


def body(atmos_state, ocean_state, flux_coef, remap_weight, source_row, target_device, target_row):
    highest = lax.Precision.HIGHEST
    fields, levels, atmos_rows, columns = atmos_state.shape
    ocean_rows = ocean_state.shape[2]
    item_count = remap_weight.shape[0]
    width_all = fields * columns
    surface = (flux_coef[:, None, None] * atmos_state[:, 0]).astype(jnp.bfloat16)
    chosen = (
        source_row[:, None] == lax.broadcasted_iota(jnp.int32, (item_count, atmos_rows), 1)
    ).astype(jnp.bfloat16)
    picked_rows = jnp.einsum(
        "ir,frx->ifx", chosen, surface, preferred_element_type=jnp.float32
    ).astype(jnp.bfloat16)
    shares = jnp.einsum(
        "ifk,ikj->ifj", picked_rows, remap_weight, preferred_element_type=jnp.float32
    )
    flat_shares = shares.reshape(item_count, width_all)
    destination = target_device[:, 0]
    global_row = destination * ocean_rows + target_row
    wanted = lax.broadcasted_iota(jnp.int32, (lax.axis_size("tile") * ocean_rows, item_count), 0)
    hitting = (global_row[None, :] == wanted).astype(jnp.float32)
    landed = lax.psum_scatter(
        jnp.dot(hitting, flat_shares, precision=highest), "tile", scatter_dimension=0, tiled=True
    )
    forcing = landed.reshape(ocean_rows, fields, columns).transpose(1, 0, 2)
    table = gll_second()
    flipped = [[table[inner_pos][outer_pos] for inner_pos in range(4)] for outer_pos in range(4)]
    second_x = jnp.dot(
        atmos_state.reshape(-1, columns), block_matrix(columns, flipped), precision=highest
    ).reshape(atmos_state.shape)
    second_y = jnp.einsum(
        "yk,flkx->flyx", block_matrix(atmos_rows, table), atmos_state, precision=highest
    )
    laplace = second_x + second_y
    widened = with_halo(laplace, (("comp", 2), ("tile", 3)), 1, True)
    col_pos = lax.broadcasted_iota(jnp.int32, (1, 1, 1, columns), 3) % 4
    middle_cols = widened[:, :, :, 1:-1]
    across = jnp.where(
        col_pos == 3,
        (middle_cols + widened[:, :, :, 2:]) * 0.5,
        jnp.where(col_pos == 0, (middle_cols + widened[:, :, :, :-2]) * 0.5, middle_cols),
    )
    row_pos = lax.broadcasted_iota(jnp.int32, (1, 1, atmos_rows, 1), 2) % 4
    middle_rows = across[:, :, 1:-1]
    smoothed = jnp.where(
        row_pos == 3,
        (middle_rows + across[:, :, 2:]) * 0.5,
        jnp.where(row_pos == 0, (middle_rows + across[:, :, :-2]) * 0.5, middle_rows),
    )
    atmos_next = atmos_state + viscosity * smoothed
    padded = with_halo(ocean_state, (("comp", 2), ("tile", 3)), 1, False)
    planar = (
        padded[:, :, 2:, 1:-1]
        + padded[:, :, :-2, 1:-1]
        + padded[:, :, 1:-1, 2:]
        + padded[:, :, 1:-1, :-2]
        - 4.0 * ocean_state
    )
    upper = jnp.concatenate([ocean_state[:, :1], ocean_state[:, :-1]], axis=1)
    lower = jnp.concatenate([ocean_state[:, 1:], ocean_state[:, -1:]], axis=1)
    vertical = upper + lower - 2.0 * ocean_state
    ocean_next = ocean_state + diffusion * planar + mixing_rate * vertical
    ocean_next = ocean_next.at[:, 0].add(forcing_step * forcing)
    return (atmos_next, ocean_next)


def solution(mesh):
    return jax.shard_map(
        body,
        mesh=mesh,
        in_specs=(
            P(None, None, "comp", "tile"),
            P(None, None, "comp", "tile"),
            P(),
            P(("comp", "tile"), None, None),
            P(("comp", "tile")),
            P(("comp", "tile"), None),
            P(("comp", "tile")),
        ),
        out_specs=(P(None, None, "comp", "tile"), P(None, None, "comp", "tile")),
        check_vma=False,
    )
```

profile of v0, /device:TPU:0, one launch (start us, length us, event | category | flops | bytes accessed | tf_op | source)
XLA Modules:
  0.0 65.1 jit_solution(2508827802086557240)
XLA Ops:
  7.3 1.9 %convolution_bitcast_fusion.1 = f32[1024,128]{0,1:T(8,128)S(1)} fusion(f32[1024,128]{1,0:T(8,128)} %bitcast.47, s32[128]{0:T(128)S(1)} %get-tuple-element.29, s32[128]{0:T(128)S(1)} %get-tuple-element.31, s32[128]{0:T(128)S(1)} %get-tuple-element.28, s32[128]{0:T(128)S(1)} %get-tuple-element.30, pred[128]{0:T(512)(128)(4,1)S(1)} %get-tuple-element.27, ...), kind=kOutput, calls=%fused_computation.1 | convolution fusion | flops 202129408 | bytes 1050880 | tf_op jit(solution)/shard_map/dot_general | solution.py:110
  9.4 0.8 %copy-done.2 = f32[4,32,8,128]{3,2,1,0:T(8,128)S(1)} copy-done((f32[4,32,8,128]{3,2,1,0:T(8,128)S(1)}, f32[4,32,8,128]{3,2,1,0:T(8,128)}, u32[]{:S(2)}) %copy-start.2) | copy-done | bytes 524312
  10.2 0.6 fusion
  11.0 3.1 %collective-permute-start = (f32[4,32,1,128]{3,2,1,0:T(1,128)S(1)}, f32[4,32,1,128]{3,2,1,0:T(1,128)S(1)}, u32[]{:S(2)}, u32[]{:S(2)}) collective-permute-start(f32[4,32,1,128]{3,2,1,0:T(1,128)S(1)} %get-tuple-element.16), channel_id=1, source_target_pairs={{0,8},{8,16},{16,24},{24,0},{1,9},{9,17},{17,25},{25,1},{2,10},{10... | collective-permute-start | bytes 196616 | tf_op jit(solution)/shard_map/ppermute | solution.py:20
  14.0 2.1 %collective-permute-start.1 = (f32[4,32,1,128]{3,2,1,0:T(1,128)S(1)}, f32[4,32,1,128]{3,2,1,0:T(1,128)S(1)}, u32[]{:S(2)}, u32[]{:S(2)}) collective-permute-start(f32[4,32,1,128]{3,2,1,0:T(1,128)S(1)} %get-tuple-element.17), channel_id=1, source_target_pairs={{8,0},{16,8},{24,16},{0,24},{9,1},{17,9},{25,17},{1,25},{10,2},{18... | collective-permute-start | bytes 196616 | tf_op jit(solution)/shard_map/ppermute | solution.py:22
  16.2 1.3 %collective-permute-start.4 = (f32[4,8,1,128]{3,2,1,0:T(1,128)S(1)}, f32[4,8,1,128]{3,2,1,0:T(1,128)S(1)}, u32[]{:S(2)}, u32[]{:S(2)}) collective-permute-start(f32[4,8,1,128]{3,2,1,0:T(1,128)S(1)} %get-tuple-element.25), channel_id=1, source_target_pairs={{8,0},{16,8},{24,16},{9,1},{17,9},{25,17},{10,2},{18,10},{26,18},{... | collective-permute-start | bytes 49160 | tf_op jit(solution)/shard_map/ppermute | solution.py:22
  17.5 4.5 %collective-permute-start.5 = (f32[4,8,1,128]{3,2,1,0:T(1,128)S(1)}, f32[4,8,1,128]{3,2,1,0:T(1,128)S(1)}, u32[]{:S(2)}, u32[]{:S(2)}) collective-permute-start(f32[4,8,1,128]{3,2,1,0:T(1,128)S(1)} %get-tuple-element.24), channel_id=1, source_target_pairs={{0,8},{8,16},{16,24},{1,9},{9,17},{17,25},{2,10},{10,18},{18,26},{... | collective-permute-start | bytes 49160 | tf_op jit(solution)/shard_map/ppermute | solution.py:20
  22.5 0.6 copy-done.19
  23.2 0.9 %fusion.54 = f32[128,512]{1,0:T(8,128)} fusion(f32[12,512]{1,0:T(8,128)S(1)} %bitcast.49, s32[12]{0:T(128)S(1)} %bitcast_add_fusion), kind=kOutput, calls=%fused_computation.86 | convolution fusion | flops 9438720 | bytes 286768 | tf_op jit(solution)/shard_map/dot_general | solution.py:105
  24.1 0.6 broadcast_compare_fusion
  24.7 0.7 %fusion.228 = (f32[4,7,16,128]{3,2,1,0:T(8,128)S(1)}, f32[4,7,16,128]{3,2,1,0:T(8,128)}) fusion(f32[4,8,16,128]{3,2,1,0:T(8,128)S(1)} %copy-done.1), kind=kLoop, calls=%fused_computation.250 | loop fusion | bytes 917504 | tf_op jit(solution)/shard_map/slice | solution.py:142
  25.5 0.6 fusion.229
  26.1 0.6 broadcast_compare_fusion.2
  26.7 0.5 copy-done.11
  27.3 1.0 %fusion.227 = (f32[4,8,18,1]{3,2,1,0:T(8,128)}, f32[4,8,18,1]{3,2,1,0:T(8,128)}) fusion(f32[4,8,18,128]{3,2,1,0:T(8,128)S(1)} %pad_maximum_fusion.7), kind=kLoop, calls=%fused_computation.249 | loop fusion | bytes 9216 | tf_op jit(solution)/shard_map/slice | solution.py:16
  28.2 1.3 %collective-permute-start.6 = (f32[4,8,18,1]{3,2,1,0:T(8,128)}, f32[4,8,18,1]{3,2,1,0:T(8,128)}, u32[]{:S(2)}, u32[]{:S(2)}) collective-permute-start(f32[4,8,18,1]{3,2,1,0:T(8,128)} %get-tuple-element.18), channel_id=1, source_target_pairs={{1,0},{2,1},{3,2},{4,3},{5,4},{6,5},{7,6},{9,8},{10,9},{11,10},{12... | collective-permute-start | bytes 6920 | tf_op jit(solution)/shard_map/ppermute | solution.py:22
  29.5 3.8 %collective-permute-start.7 = (f32[4,8,18,1]{3,2,1,0:T(8,128)}, f32[4,8,18,1]{3,2,1,0:T(8,128)}, u32[]{:S(2)}, u32[]{:S(2)}) collective-permute-start(f32[4,8,18,1]{3,2,1,0:T(8,128)} %get-tuple-element.19), channel_id=1, source_target_pairs={{0,1},{1,2},{2,3},{3,4},{4,5},{5,6},{6,7},{8,9},{9,10},{10,11},{11... | collective-permute-start | bytes 6920 | tf_op jit(solution)/shard_map/ppermute | solution.py:20
  33.3 0.6 copy-done.6
  33.9 0.6 copy-done.8
  35.1 1.0 %copy.14 = f32[4,32,10,1]{1,0,3,2:T(4,128)} copy(f32[4,32,10,1]{3,2,1,0:T(8,128)S(1)} %get-tuple-element.14) | data formatting | bytes 10240 | tf_op jit(solution)/shard_map/slice | solution.py:16
  36.1 1.6 %collective-permute-start.2 = (f32[4,32,10,1]{1,0,3,2:T(4,128)}, f32[4,32,10,1]{1,0,3,2:T(4,128)S(1)}, u32[]{:S(2)}, u32[]{:S(2)}) collective-permute-start(f32[4,32,10,1]{1,0,3,2:T(4,128)} %copy.14), channel_id=1, source_target_pairs={{1,0},{2,1},{3,2},{4,3},{5,4},{6,5},{7,6},{0,7},{9,8},{10,9},{11,1... | collective-permute-start | bytes 15368 | tf_op jit(solution)/shard_map/ppermute | solution.py:22
  38.6 1.5 %fusion.17 = f32[4,8,16,128]{3,2,1,0:T(8,128)S(1)} fusion(f32[4,8,16,128]{3,2,1,0:T(8,128)S(1)} %copy-done.1, f32[4,8,18,1]{3,2,1,0:T(8,128)} %collective-permute-done.7, f32[4,8,1,128]{3,2,1,0:T(1,128)S(1)} %collective-permute-done.4, f32[4,8,1,128]{3,2,1,0:T(1,128)S(1)} %copy-done.12, f32[4,8,18,1]{3,2,1,0:T(8,128)} %collective-permute-done.6, ...), kind=kLoop, calls=%fused_computation.31 | loop fusion | flops 1441792 | bytes 1085952 | tf_op jit(solution)/shard_map/add | solution.py:144
  40.1 0.5 copy.15
  40.7 1.7 %collective-permute-done.3 = f32[4,32,10,1]{1,0,3,2:T(4,128)} collective-permute-done((f32[4,32,10,1]{1,0,3,2:T(4,128)S(1)}, f32[4,32,10,1]{1,0,3,2:T(4,128)}, u32[]{:S(2)}, u32[]{:S(2)}) %collective-permute-start.3) | collective-permute-done | bytes 5152 | tf_op jit(solution)/shard_map/ppermute | solution.py:20
  42.3 1.2 %copy.17 = f32[4,32,10,1]{3,2,1,0:T(8,128)S(1)} copy(f32[4,32,10,1]{1,0,3,2:T(4,128)} %collective-permute-done.3) | data formatting | bytes 10240 | tf_op jit(solution)/shard_map/ppermute | solution.py:20
  43.6 0.6 copy-done.15
  44.3 1.4 %fusion.4 = f32[4,32,10,128]{3,2,1,0:T(8,128)S(1)} fusion(f32[4,32,10,1]{3,2,1,0:T(8,128)S(1)} %copy.17, f32[4,32,1,128]{3,2,1,0:T(1,128)S(1)} %copy-done.9, f32[4,32,8,128]{3,2,1,0:T(8,128)S(1)} %fusion, f32[4,32,1,128]{3,2,1,0:T(1,128)S(1)} %copy-done.7, f32[4,32,10,1]{3,2,1,0:T(8,128)S(1)} %copy.15, pred[128]{0:T(512)(128)(4,1)S(1)} %copy-done.15, ...), kind=kLoop, calls=%fused_computation.8 | loop fusion | flops 2293760 | bytes 1321216 | tf_op jit(solution)/shard_map/jit(_where)/select_n | solution.py:120
  45.7 0.6 copy-done.17
  46.4 1.0 %fusion.11 = f32[4,32,8,128]{3,2,1,0:T(8,128)} fusion(f32[4,32,8,128]{3,2,1,0:T(8,128)S(1)} %copy-done.3, f32[4,32,10,128]{3,2,1,0:T(8,128)S(1)} %fusion.4, pred[8]{0:T(512)(128)(4,1)S(1)} %copy-done.17, pred[8]{0:T(512)(128)(4,1)S(1)} %copy-done.18), kind=kLoop, calls=%fused_computation.22 | loop fusion | flops 1048576 | bytes 2621456 | tf_op jit(solution)/shard_map/add | solution.py:132
  47.4 9.4 %reduce-scatter.2.cloned.1.call-done = f32[16,512]{1,0:T(8,128)} async-done(((f32[128,512]{1,0:T(8,128)}), f32[16,512]{1,0:T(8,128)}) %reduce-scatter.2.cloned.1.call-update) | async-done | bytes 32784 | tf_op jit(solution)/shard_map/reduce_scatter | solution.py:104
  56.8 0.8 %fusion.80 = f32[4,8,16,128]{3,2,1,0:T(8,128)S(1)} fusion(f32[4,8,16,128]{3,2,1,0:T(8,128)S(1)} %fusion.17, f32[16,512]{1,0:T(8,128)} %reduce-scatter.2.cloned.1.call-done), kind=kLoop, calls=%fused_computation.93 | loop fusion | flops 16384 | bytes 98304 | tf_op jit(solution)/shard_map/scatter-add | solution.py:145
  57.5 0.7 %copy-done.5 = f32[4,8,16,128]{3,2,1,0:T(8,128)} copy-done((f32[4,8,16,128]{3,2,1,0:T(8,128)}, f32[4,8,16,128]{3,2,1,0:T(8,128)S(1)}, u32[]{:S(2)}) %copy-start.5) | copy-done | bytes 262168
  (62 shorter events, 2.6 us)
Async XLA Ops:
  7.2 15.1 %copy-start = (bf16[12,128,128]{2,1,0:T(8,128)(2,1)S(1)}, bf16[12,128,128]{2,1,0:T(8,128)(2,1)}, u32[]{:S(2)}) copy-start(bf16[12,128,128]{2,1,0:T(8,128)(2,1)} %param.12) | copy-start | bytes 1179652
  7.2 49.6 %reduce-scatter.2.cloned.1.call-start = ((), (), s32[]{:S(2)}) async-start(), calls=%async_computation.1 | async-start | bytes 294912 | tf_op jit(solution)/shard_map/reduce_scatter | solution.py:104
  9.2 1.0 %copy-start.2 = (f32[4,32,8,128]{3,2,1,0:T(8,128)S(1)}, f32[4,32,8,128]{3,2,1,0:T(8,128)}, u32[]{:S(2)}) copy-start(f32[4,32,8,128]{3,2,1,0:T(8,128)} %param.9) | copy-start | bytes 1572868
  10.9 5.3 %copy-start.1 = (f32[4,8,16,128]{3,2,1,0:T(8,128)S(1)}, f32[4,8,16,128]{3,2,1,0:T(8,128)}, u32[]{:S(2)}) copy-start(f32[4,8,16,128]{3,2,1,0:T(8,128)} %param.10) | copy-start | bytes 786436
  11.0 22.4 %collective-permute-start = (f32[4,32,1,128]{3,2,1,0:T(1,128)S(1)}, f32[4,32,1,128]{3,2,1,0:T(1,128)S(1)}, u32[]{:S(2)}, u32[]{:S(2)}) collective-permute-start(f32[4,32,1,128]{3,2,1,0:T(1,128)S(1)} %get-tuple-element.16), channel_id=1, source_target_pairs={{0,8},{8,16},{16,24},{24,0},{1,9},{9,17},{17,25},{25,1},{2,10},{10... | collective-permute-start | bytes 196616 | tf_op jit(solution)/shard_map/ppermute | solution.py:20
  14.0 19.3 %collective-permute-start.1 = (f32[4,32,1,128]{3,2,1,0:T(1,128)S(1)}, f32[4,32,1,128]{3,2,1,0:T(1,128)S(1)}, u32[]{:S(2)}, u32[]{:S(2)}) collective-permute-start(f32[4,32,1,128]{3,2,1,0:T(1,128)S(1)} %get-tuple-element.17), channel_id=1, source_target_pairs={{8,0},{16,8},{24,16},{0,24},{9,1},{17,9},{25,17},{1,25},{10,2},{18... | collective-permute-start | bytes 196616 | tf_op jit(solution)/shard_map/ppermute | solution.py:22
  16.2 5.9 %copy-start.13 = (f32[4]{0:T(128)S(1)}, f32[4]{0:T(128)}, u32[]{:S(2)}) copy-start(f32[4]{0:T(128)} %param.11) | copy-start | bytes 52
  16.2 5.9 %copy-start.14 = (s32[12]{0:T(128)S(1)}, s32[12]{0:T(128)}, u32[]{:S(2)}) copy-start(s32[12]{0:T(128)} %param.13) | copy-start | bytes 148
  16.2 10.5 %collective-permute-start.4 = (f32[4,8,1,128]{3,2,1,0:T(1,128)S(1)}, f32[4,8,1,128]{3,2,1,0:T(1,128)S(1)}, u32[]{:S(2)}, u32[]{:S(2)}) collective-permute-start(f32[4,8,1,128]{3,2,1,0:T(1,128)S(1)} %get-tuple-element.25), channel_id=1, source_target_pairs={{8,0},{16,8},{24,16},{9,1},{17,9},{25,17},{10,2},{18,10},{26,18},{... | collective-permute-start | bytes 49160 | tf_op jit(solution)/shard_map/ppermute | solution.py:22
  17.5 9.2 %collective-permute-start.5 = (f32[4,8,1,128]{3,2,1,0:T(1,128)S(1)}, f32[4,8,1,128]{3,2,1,0:T(1,128)S(1)}, u32[]{:S(2)}, u32[]{:S(2)}) collective-permute-start(f32[4,8,1,128]{3,2,1,0:T(1,128)S(1)} %get-tuple-element.24), channel_id=1, source_target_pairs={{0,8},{8,16},{16,24},{1,9},{9,17},{17,25},{2,10},{10,18},{18,26},{... | collective-permute-start | bytes 49160 | tf_op jit(solution)/shard_map/ppermute | solution.py:20
  22.5 0.7 %copy-start.19 = (s32[12]{0:T(128)S(1)}, s32[12]{0:T(128)}, u32[]{:S(2)}) copy-start(s32[12]{0:T(128)} %param.15) | copy-start | bytes 148
  22.5 0.7 %copy-start.20 = (s32[12,1]{0,1:T(1,128)S(1)}, s32[12,1]{0,1:T(1,128)}, u32[]{:S(2)}) copy-start(s32[12,1]{0,1:T(1,128)} %param.14) | copy-start | bytes 148
  26.7 0.6 copy-start.11
  28.2 9.9 %collective-permute-start.6 = (f32[4,8,18,1]{3,2,1,0:T(8,128)}, f32[4,8,18,1]{3,2,1,0:T(8,128)}, u32[]{:S(2)}, u32[]{:S(2)}) collective-permute-start(f32[4,8,18,1]{3,2,1,0:T(8,128)} %get-tuple-element.18), channel_id=1, source_target_pairs={{1,0},{2,1},{3,2},{4,3},{5,4},{6,5},{7,6},{9,8},{10,9},{11,10},{12... | collective-permute-start | bytes 6920 | tf_op jit(solution)/shard_map/ppermute | solution.py:22
  29.5 8.6 %collective-permute-start.7 = (f32[4,8,18,1]{3,2,1,0:T(8,128)}, f32[4,8,18,1]{3,2,1,0:T(8,128)}, u32[]{:S(2)}, u32[]{:S(2)}) collective-permute-start(f32[4,8,18,1]{3,2,1,0:T(8,128)} %get-tuple-element.19), channel_id=1, source_target_pairs={{0,1},{1,2},{2,3},{3,4},{4,5},{5,6},{6,7},{8,9},{9,10},{10,11},{11... | collective-permute-start | bytes 6920 | tf_op jit(solution)/shard_map/ppermute | solution.py:20
  33.3 0.6 copy-start.6
  33.9 0.6 copy-start.8
  36.1 4.0 %collective-permute-start.2 = (f32[4,32,10,1]{1,0,3,2:T(4,128)}, f32[4,32,10,1]{1,0,3,2:T(4,128)S(1)}, u32[]{:S(2)}, u32[]{:S(2)}) collective-permute-start(f32[4,32,10,1]{1,0,3,2:T(4,128)} %copy.14), channel_id=1, source_target_pairs={{1,0},{2,1},{3,2},{4,3},{5,4},{6,5},{7,6},{0,7},{9,8},{10,9},{11,1... | collective-permute-start | bytes 15368 | tf_op jit(solution)/shard_map/ppermute | solution.py:22
  37.7 0.9 %copy-start.4 = (f32[4,7,16,128]{3,2,1,0:T(8,128)S(1)}, f32[4,7,16,128]{3,2,1,0:T(8,128)}, u32[]{:S(2)}) copy-start(f32[4,7,16,128]{3,2,1,0:T(8,128)} %get-tuple-element.21) | copy-start | bytes 688132
  37.7 0.9 %copy-start.10 = (f32[4,1,16,128]{3,2,1,0:T(8,128)S(1)}, f32[4,1,16,128]{3,2,1,0:T(8,128)}, u32[]{:S(2)}) copy-start(f32[4,1,16,128]{3,2,1,0:T(8,128)} %get-tuple-element.23) | copy-start | bytes 98308
  37.7 0.9 %copy-start.12 = (f32[4,8,1,128]{3,2,1,0:T(1,128)S(1)}, f32[4,8,1,128]{3,2,1,0:T(1,128)}, u32[]{:S(2)}) copy-start(f32[4,8,1,128]{3,2,1,0:T(1,128)} %copy-done.11) | copy-start | bytes 49156
  38.1 4.2 %collective-permute-start.3 = (f32[4,32,10,1]{1,0,3,2:T(4,128)S(1)}, f32[4,32,10,1]{1,0,3,2:T(4,128)}, u32[]{:S(2)}, u32[]{:S(2)}) collective-permute-start(f32[4,32,10,1]{1,0,3,2:T(4,128)S(1)} %copy.16), channel_id=1, source_target_pairs={{0,1},{1,2},{2,3},{3,4},{4,5},{5,6},{6,7},{7,0},{8,9},{9,10},{10,1... | collective-permute-start | bytes 15368 | tf_op jit(solution)/shard_map/ppermute | solution.py:20
  40.7 3.0 %copy-start.7 = (f32[4,32,1,128]{3,2,1,0:T(1,128)S(1)}, f32[4,32,1,128]{3,2,1,0:T(1,128)}, u32[]{:S(2)}) copy-start(f32[4,32,1,128]{3,2,1,0:T(1,128)} %copy-done.6) | copy-start | bytes 196612
  40.7 3.0 %copy-start.9 = (f32[4,32,1,128]{3,2,1,0:T(1,128)S(1)}, f32[4,32,1,128]{3,2,1,0:T(1,128)}, u32[]{:S(2)}) copy-start(f32[4,32,1,128]{3,2,1,0:T(1,128)} %copy-done.8) | copy-start | bytes 196612
  43.6 0.6 copy-start.15
  43.6 0.7 %copy-start.16 = (pred[128]{0:T(512)(128)(4,1)S(1)}, pred[128]{0:T(512)(128)(4,1)}, u32[]{:S(2)}) copy-start(pred[128]{0:T(512)(128)(4,1)} %get-tuple-element.39) | copy-start | bytes 388
  44.3 1.4 %copy-start.3 = (f32[4,32,8,128]{3,2,1,0:T(8,128)S(1)}, f32[4,32,8,128]{3,2,1,0:T(8,128)}, u32[]{:S(2)}) copy-start(f32[4,32,8,128]{3,2,1,0:T(8,128)} %param.9) | copy-start | bytes 1572868
  45.7 0.6 copy-start.17
  45.7 0.7 %copy-start.18 = (pred[8]{0:T(512)(128)(4,1)S(1)}, pred[8]{0:T(512)(128)(4,1)}, u32[]{:S(2)}) copy-start(pred[8]{0:T(512)(128)(4,1)} %get-tuple-element.41) | copy-start | bytes 28
  57.5 0.7 %copy-start.5 = (f32[4,8,16,128]{3,2,1,0:T(8,128)}, f32[4,8,16,128]{3,2,1,0:T(8,128)S(1)}, u32[]{:S(2)}) copy-start(f32[4,8,16,128]{3,2,1,0:T(8,128)S(1)} %fusion.80) | copy-start | bytes 786436
Sparse Core Ops, SparseCore 0:
  24.3 32.4 reduce-scatter.1
where the time goes:
time: 65.5 us; the launch traced here: 65.1 us
  starting transfers between devices  17.7 us (27%)
  between operations  14.4 us (22%)
  local copies, waits for them, and re-layouts  11.9 us (18%)
  waiting for transfers between devices  11.1 us (17%)
  other arithmetic  6.12 us (9%)
  matrix products  3.86 us (6%)
    ppermute x4, starting transfers between devices, with_halo(): lax.ppermute(tail, axis, [(i, (i + 1) % count) for i in range(ends)])  11.4 us
    reduce_scatter x1, waiting for transfers between devices, body(): lax.psum_scatter(jnp.dot(hitting, flat_shares, precision=highest), 'tile'...  9.36 us
    ppermute x4, starting transfers between devices, with_halo(): lax.ppermute(head, axis, [((i + 1) % count, i) for i in range(ends)])  6.27 us
    unnamed x44, local copies, waits for them, and re-layouts  5.78 us
    slice x3, local copies, waits for them, and re-layouts, with_halo(): head = lax.slice_in_dim(cells, 0, width, axis=dim)  2.32 us
    dot_general x1, matrix products, body(): jnp.dot(atmos_state.reshape(-1, columns), block_matrix(columns, flipped),...  1.86 us
    ppermute x4, waiting for transfers between devices, with_halo(): lax.ppermute(tail, axis, [(i, (i + 1) % count) for i in range(ends)])  1.67 us
    add x1, other arithmetic, body(): ocean_next = ocean_state + diffusion * planar + mixing_rate * vertical  1.46 us
  transfers between devices with their start and end apart: 9, of which 2 were waited for; matrix products, arithmetic and copies ran while one was open for 19% of the time, Pallas kernels for 0%

commit v1 on v0

v1 whole, which is shorter than its diff:
```python
import functools

import jax
import jax.numpy as jnp
import numpy as np
from jax import lax
from jax.experimental import pallas as pl
from jax.experimental.pallas import tpu as pltpu
from jax.sharding import PartitionSpec as P

viscosity = 0.01
diffusion = 0.2
mixing_rate = 0.1
forcing_step = 0.5
SLOTS = 3
GROUP = 4
BLOCK = (SLOTS + 1) * GROUP
HALO = 16


def gll_second():
    nodes = np.array([-1.0, -(0.2**0.5), 0.2**0.5, 1.0])
    derivative = np.zeros((4, 4))
    for i in range(4):
        for j in range(4):
            if i == j:
                derivative[i, j] = sum(1.0 / (nodes[i] - nodes[k]) for k in range(4) if k != i)
            else:
                top = np.prod([nodes[i] - nodes[k] for k in range(4) if k not in (i, j)])
                derivative[i, j] = top / np.prod([nodes[j] - nodes[k] for k in range(4) if k != j])
    return derivative @ derivative


def tables(columns):
    second = gll_second()
    along = np.kron(np.eye(columns // 4), second)
    seam = np.eye(columns)
    for x in range(0, columns, 4):
        for edge, other in ((x, x - 1), (x + 3, x + 4)):
            seam[edge, edge] = 0.5
            if 0 <= other < columns:
                seam[edge, other] = 0.5
    inner = (seam @ along).T
    first, last = np.eye(columns)[0], np.eye(columns)[-1]
    edge_atmos = np.zeros((16, 8 * columns))
    for k in range(8):
        for side, unit, row in ((0, first, along[0]), (8, last, along[-1])):
            edge_atmos[side + k, k * columns : (k + 1) * columns] += row
            for j in range(4):
                m = k // 4 * 4 + j
                edge_atmos[side + k, m * columns : (m + 1) * columns] += second[k % 4, j] * unit
    edge_ocean = np.zeros((16, 4 * columns))
    place_atmos = np.zeros((8, 16, columns))
    place_ocean = np.zeros((4, 16, columns))
    for c in range(4):
        edge_ocean[c, c * columns : (c + 1) * columns] = first
        edge_ocean[4 + c, c * columns : (c + 1) * columns] = last
        for part in (0, 8):
            place_ocean[c, part + c] = last
            place_ocean[c, part + 4 + c] = first
    for k in range(8):
        place_atmos[k, k] = 0.5 * first
        place_atmos[k, 8 + k] = 0.5 * last
    bf = lambda a: jnp.asarray(a.astype(np.float32)).astype(jnp.bfloat16)
    return (
        bf(np.concatenate([inner, seam.T])),
        bf(np.concatenate([edge_atmos, edge_ocean], axis=1)),
        bf(np.concatenate([place_atmos.reshape(-1, columns), place_ocean.reshape(-1, columns)])),
    )


def dot(a, b):
    return jnp.dot(a, b, preferred_element_type=jnp.float32)


def dot_nt(a, b):
    return lax.dot_general(a, b, (((1,), (1,)), ((), ())), preferred_element_type=jnp.float32)


def dot_tn(a, b):
    return lax.dot_general(a, b, (((0,), (0,)), ((), ())), preferred_element_type=jnp.float32)


def split(v):
    high = v.astype(jnp.bfloat16)
    return high, (v - high.astype(jnp.float32)).astype(jnp.bfloat16)


def row_of(ref, k, count, stride):
    return ref[pl.ds(k, count, stride=stride), :]


def along_y(rows, k):
    second = gll_second()
    base = k // 4 * 4
    return sum(float(second[k % 4, j]) * rows[base + j] for j in range(4))


def pack_kernel(
    n, fields, levels, olev, oy,
    coef, source, target, target_row, atmos, ocean, weight, mix, edge,
    blocks, far, edges, surf, counts,
):
    planes, cells = fields * levels, fields * olev
    ay = atmos.shape[0] // planes
    columns = atmos.shape[1]
    items = weight.shape[0]
    me = lax.axis_index("tile")
    even = me % 2 == 0
    rows = [row_of(atmos, k, planes, ay) for k in range(ay)]
    halves = [r.astype(jnp.bfloat16) for r in rows]
    inner, seam = mix[:columns, :], mix[columns:, :]
    for slot, k in ((0, 0), (1, ay - 1)):
        edges[slot, :planes, :] = dot(halves[k], inner) + dot(along_y(rows, k).astype(jnp.bfloat16), seam)
    cell_rows = [row_of(ocean, y, cells, oy) for y in range(oy)]
    edges[0, planes:, :] = cell_rows[0]
    edges[1, planes:, :] = cell_rows[oy - 1]
    width = ay * columns
    atmos_cols = dot_nt(edge[:, :width], jnp.concatenate(halves, axis=1))
    chunks = [jnp.concatenate(cell_rows[4 * c : 4 * c + 4], axis=0) for c in range(oy // 4)]
    parts = [split(c) for c in chunks]
    ocean_cols = dot_nt(edge[:, width:], jnp.concatenate([p[0] for p in parts], axis=1)) + dot_nt(
        edge[:, width:], jnp.concatenate([p[1] for p in parts], axis=1)
    )
    left, right = atmos_cols[:ay], atmos_cols[ay:]
    near = jnp.where(even, right, left)
    far[:ay, :] = jnp.where(even, left, right)
    far[ay:, :] = ocean_cols[:8]
    base = n * (SLOTS + 1)
    for g in range(2):
        blocks[base + g] = near[g * GROUP : (g + 1) * GROUP]
        blocks[base + 2 + g] = ocean_cols[g * GROUP : (g + 1) * GROUP]
    blocks[:base] = jnp.full((base, GROUP, columns), -1.0, jnp.float32)
    for y in range(ay):
        surf[y, fields:, :] = jnp.zeros((8 - fields, columns), jnp.float32)
    for f in range(fields):
        plane = atmos[f * levels * ay : f * levels * ay + ay, :] * coef[f]
        for y in range(ay):
            surf[y, f : f + 1, :] = plane[y : y + 1]

    @pl.loop(0, n)
    def _(i):
        counts[i] = 0

    def one(i, carry):
        to = target[i]
        slot = counts[to]
        counts[to] = slot + 1
        offset = to ^ me
        at = ((offset % 2) * (n // 2) + offset // 2) * (SLOTS + 1)
        share = dot(surf[source[i]].astype(jnp.bfloat16), weight[i])
        blocks[at + slot] = share[:fields]
        blocks[at + SLOTS, pl.ds(slot, 1), :] = jnp.full((1, columns), target_row[i].astype(jnp.float32))
        return carry

    lax.fori_loop(0, items, one, 0, unroll=items <= 16)


def corner_kernel(planes, ay, near, far, edges, place, first, second):
    even_tile = lax.axis_index("tile") % 2 == 0
    even_comp = lax.axis_index("comp") % 2 == 0
    halos = side_halos(even_tile, near[:ay, :], far[:ay, :])
    top = edges[0, :planes, :] + dot_tn(halos, place[:16, :])
    low = edges[1, :planes, :] + dot_tn(halos, place[(ay - 1) * 16 : ay * 16, :])
    first[:planes, :] = jnp.where(even_comp, low, top)
    second[:planes, :] = jnp.where(even_comp, top, low)
    first[planes:, :] = jnp.where(even_comp, edges[1, planes:, :], edges[0, planes:, :])
    second[planes:, :] = jnp.where(even_comp, edges[0, planes:, :], edges[1, planes:, :])


def side_halos(even_tile, near, far):
    left = jnp.where(even_tile, far, near)
    right = jnp.where(even_tile, near, far)
    return jnp.concatenate([left, right], axis=0).astype(jnp.bfloat16)


def finish_kernel(
    n, bands, fields, levels, olev, oy,
    atmos, ocean, near, far, first, second, shares, mix, place,
    atmos_out, ocean_out,
):
    planes, cells = fields * levels, fields * olev
    ay = atmos.shape[0] // planes
    columns = atmos.shape[1]
    me, band = lax.axis_index("tile"), lax.axis_index("comp")
    even_tile, even_comp = me % 2 == 0, band % 2 == 0
    up_all = jnp.where(even_comp, second[...], first[...])
    down_all = jnp.where(even_comp, first[...], second[...])
    rows = [row_of(atmos, k, planes, ay) for k in range(ay)]
    inner, seam = mix[:columns, :], mix[columns:, :]
    halos = side_halos(even_tile, near[:ay, :], far[:ay, :])
    across = [
        dot(rows[k].astype(jnp.bfloat16), inner)
        + dot(along_y(rows, k).astype(jnp.bfloat16), seam)
        + dot_tn(halos, place[k * 16 : (k + 1) * 16, :])
        for k in range(ay)
    ]
    for k in range(ay):
        if k % 4 == 0:
            smooth = (across[k] + (across[k - 1] if k else up_all[:planes])) * 0.5
        elif k % 4 == 3:
            smooth = (across[k] + (across[k + 1] if k + 1 < ay else down_all[:planes])) * 0.5
        else:
            smooth = across[k]
        atmos_out[pl.ds(k, planes, stride=ay), :] = rows[k] + viscosity * smooth
    lane = lax.broadcasted_iota(jnp.int32, (1, columns), 1)
    row_id = lax.broadcasted_iota(jnp.int32, (oy * cells, columns), 0)
    remapped = jnp.zeros((oy * cells, columns), jnp.float32)
    per = columns // BLOCK
    for group in range(n // per):
        ids = jnp.full((1, columns), -1.0, jnp.float32)
        for p in range(per):
            at = (group * per + p) * BLOCK
            for slot in range(SLOTS):
                here = lane // GROUP == (p * BLOCK) // GROUP + slot
                ids = jnp.where(here, shares[at + SLOTS * GROUP + slot : at + SLOTS * GROUP + slot + 1, :], ids)
        wanted = ids.astype(jnp.int32) * cells + lane % GROUP * olev
        hitting = jnp.where(row_id == wanted, 1.0, 0.0).astype(jnp.bfloat16)
        high, low = split(shares[group * columns : (group + 1) * columns, :])
        remapped = remapped + dot(hitting, high) + dot(hitting, low)
    col = lax.broadcasted_iota(jnp.int32, (cells, columns), 1)
    level = lax.broadcasted_iota(jnp.int32, (cells, columns), 0) % olev
    side = lax.broadcasted_iota(jnp.int32, (8, columns), 0)
    near_ocean, far_ocean = near[ay:, :], far[ay:, :]
    right_first = jnp.where(
        side < 4,
        jnp.where(me == n - 1, 0.0, jnp.where(even_tile, near_ocean, far_ocean)),
        jnp.where(me == 0, 0.0, jnp.where(even_tile, far_ocean, near_ocean)),
    )
    sides = jnp.concatenate(split(right_first), axis=0)
    sides_at = [dot_tn(sides, place[(ay + c) * 16 : (ay + c + 1) * 16, :]) for c in range(oy // 4)]
    cell_rows = [row_of(ocean, y, cells, oy) for y in range(oy)]
    north = jnp.where(band == 0, 0.0, up_all[planes:])
    south = jnp.where(band == bands - 1, 0.0, down_all[planes:])
    for y in range(oy):
        v = cell_rows[y]
        rolled = jnp.where(col == 0, 0.0, pltpu.roll(v, 1, 1)) + jnp.where(
            col == columns - 1, 0.0, pltpu.roll(v, columns - 1, 1)
        )
        beside = rolled + sides_at[y // 4][y % 4 * cells : (y % 4 + 1) * cells]
        above = cell_rows[y - 1] if y else north
        below = cell_rows[y + 1] if y + 1 < oy else south
        planar = below + above + beside - 4.0 * v
        upper = jnp.where(level == 0, v, pltpu.roll(v, 1, 0))
        lower = jnp.where(level == olev - 1, v, pltpu.roll(v, cells - 1, 0))
        vertical = upper + lower - 2.0 * v
        ocean_out[pl.ds(y, cells, stride=oy), :] = (
            v
            + diffusion * planar
            + mixing_rate * vertical
            + forcing_step * remapped[y * cells : (y + 1) * cells]
        )


def pair_up(count):
    return [(i, i ^ 1) for i in range(count)]


def pair_over(count):
    return [(i, (i + 1) % count if i % 2 else (i - 1) % count) for i in range(count)]


def body(mesh, atmos_state, ocean_state, flux_coef, remap_weight, source_row, target_device, target_row):
    n, bands = mesh.shape["tile"], mesh.shape["comp"]
    fields, levels, ay, columns = atmos_state.shape
    olev, oy = ocean_state.shape[1:3]
    planes, cells = fields * levels, fields * olev
    f32 = jnp.float32
    vmem = pl.BlockSpec(memory_space=pltpu.VMEM)
    smem = pl.BlockSpec(memory_space=pltpu.SMEM)
    mix, edge, place = tables(columns)
    atmos = atmos_state.reshape(planes * ay, columns)
    ocean = ocean_state.reshape(cells * oy, columns)
    params = pltpu.CompilerParams(vmem_limit_bytes=32 * 1024 * 1024)
    blocks, far_out, edges = pl.pallas_call(
        functools.partial(pack_kernel, n, fields, levels, olev, oy),
        out_shape=(
            jax.ShapeDtypeStruct((n * (SLOTS + 1) + HALO // GROUP, GROUP, columns), f32),
            jax.ShapeDtypeStruct((HALO, columns), f32),
            jax.ShapeDtypeStruct((2, planes + cells, columns), f32),
        ),
        in_specs=[smem] * 4 + [vmem] * 5,
        out_specs=(vmem, vmem, vmem),
        scratch_shapes=[pltpu.VMEM((ay, 8, columns), f32), pltpu.SMEM((n,), jnp.int32)],
        compiler_params=params,
        name="pack",
    )(flux_coef, source_row, target_device.reshape(-1), target_row, atmos, ocean, remap_weight, mix, edge)
    flat = blocks.reshape(-1, columns)
    half = n // 2 * BLOCK
    got = lax.ppermute(flat[half:], "tile", pair_up(n))
    far = lax.ppermute(far_out, "tile", pair_over(n))
    near = got[half:]
    state = jnp.concatenate(
        [flat[:half].reshape(n // 2, 1, BLOCK, columns), got[:half].reshape(n // 2, 1, BLOCK, columns)], axis=1
    )
    bit = 2
    while bit < n:
        pairs = state.reshape(state.shape[0] // 2, 2, state.shape[1], BLOCK, columns)
        came = lax.ppermute(
            pairs[:, 1].reshape(-1, columns), "tile", [(i, i ^ bit) for i in range(n)]
        ).reshape(pairs[:, 1].shape)
        state = jnp.concatenate([pairs[:, 0], came], axis=1)
        bit *= 2
    shares = state.reshape(n * BLOCK, columns)
    row_shape = jax.ShapeDtypeStruct((planes + cells, columns), f32)
    first_out, second_out = pl.pallas_call(
        functools.partial(corner_kernel, planes, ay),
        out_shape=(row_shape, row_shape),
        in_specs=[vmem] * 4,
        out_specs=(vmem, vmem),
        compiler_params=params,
        name="corners",
    )(near, far, edges, place)
    first = lax.ppermute(first_out, "comp", pair_up(bands))
    second = lax.ppermute(second_out, "comp", pair_over(bands))
    atmos_next, ocean_next = pl.pallas_call(
        functools.partial(finish_kernel, n, bands, fields, levels, olev, oy),
        out_shape=(
            jax.ShapeDtypeStruct(atmos.shape, f32),
            jax.ShapeDtypeStruct(ocean.shape, f32),
        ),
        in_specs=[vmem] * 9,
        out_specs=(vmem, vmem),
        compiler_params=params,
        name="finish",
    )(atmos, ocean, near, far, first, second, shares, mix, place)
    return atmos_next.reshape(atmos_state.shape), ocean_next.reshape(ocean_state.shape)


def solution(mesh):
    return jax.shard_map(
        functools.partial(body, mesh),
        mesh=mesh,
        in_specs=(
            P(None, None, "comp", "tile"),
            P(None, None, "comp", "tile"),
            P(),
            P(("comp", "tile"), None, None),
            P(("comp", "tile")),
            P(("comp", "tile"), None),
            P(("comp", "tile")),
        ),
        out_specs=(P(None, None, "comp", "tile"), P(None, None, "comp", "tile")),
        check_vma=False,
    )
```

time: 65.5 us -> 29.4 us (0.45)
  between operations: 14.4 us -> 0.73 us
  starting transfers between devices: 17.7 us -> 9.65 us
  local copies, waits for them, and re-layouts: 11.9 us -> 5.34 us
  other arithmetic: 6.12 us -> 0.02 us
  matrix products: 3.86 us -> 0 us
  Pallas kernels: 0 us -> 2.8 us
    reduce_scatter x1 -> x0, waiting for transfers between devices: 9.36 us -> none  [body(): lax.psum_scatter(jnp.dot(hitting, flat_shares, precision=highest), 'tile'...]
    ppermute x8 -> x6, waiting for transfers between devices: 1.68 us -> 10.5 us  [the longest x1 3.97 us: body(): far = lax.ppermute(far_out, 'tile', pair_over(n))]
    ppermute x8 -> x6, starting transfers between devices: 17.7 us -> 9.65 us  [the longest x2 5.01 us: body(): lax.ppermute(pairs[:, 1].reshape(-1, columns), 'tile', [(i, i ^ bit) for...]
    slice x8 -> x4, local copies, waits for them, and re-layouts: 4.15 us -> 0.01 us  [the longest x1 0.01 us: body(): got = lax.ppermute(flat[half:], 'tile', pair_up(n))]
    dot_general x5 -> x0, matrix products: 3.86 us -> none  [the longest x1 1.86 us: body(): jnp.dot(atmos_state.reshape(-1, columns), block_matrix(columns, flipped),...]
    pallas_call x0 -> x3, Pallas kernels: none -> 2.8 us  [the longest x1 1.46 us: body(): pl.pallas_call(functools.partial(finish_kernel, n, bands, fields, levels,...]
    add x3 -> x0, other arithmetic: 2.49 us -> none  [the longest x1 1.46 us: body(): ocean_next = ocean_state + diffusion * planar + mixing_rate * vertical]
    ppermute x2 -> x0, local copies, waits for them, and re-layouts: 1.78 us -> none  [the longest x1 1.25 us: with_halo(): lax.ppermute(tail, axis, [(i, (i + 1) % count) for i in range(ends)])]
  transfers between devices with their start and end apart: 9 -> 6, of which waited for: 2 -> 5; matrix products, arithmetic and copies ran while one was open for 19% -> 0% of each run, Pallas kernels for 0% -> 1%
where the time goes in v1:
time: 29.4 us; the launch traced here: 29 us
  waiting for transfers between devices  10.5 us (36%)
  starting transfers between devices  9.65 us (33%)
  local copies, waits for them, and re-layouts  5.34 us (18%)
  Pallas kernels  2.8 us (10%)
  between operations  0.73 us (2%)
    unnamed x28, local copies, waits for them, and re-layouts  5.32 us
    ppermute x2, starting transfers between devices, body(): lax.ppermute(pairs[:, 1].reshape(-1, columns), 'tile', [(i, i ^ bit) for...  5.01 us
    ppermute x1, waiting for transfers between devices, body(): far = lax.ppermute(far_out, 'tile', pair_over(n))  3.97 us
    ppermute x1, waiting for transfers between devices, body(): second = lax.ppermute(second_out, 'comp', pair_over(bands))  3.37 us
    ppermute x1, starting transfers between devices, body(): second = lax.ppermute(second_out, 'comp', pair_over(bands))  2.47 us
    ppermute x2, waiting for transfers between devices, body(): lax.ppermute(pairs[:, 1].reshape(-1, columns), 'tile', [(i, i ^ bit) for...  1.89 us
    ppermute x1, starting transfers between devices, body(): first = lax.ppermute(first_out, 'comp', pair_up(bands))  1.64 us
    pallas_call x1, Pallas kernels, body(): pl.pallas_call(functools.partial(finish_kernel, n, bands, fields, levels,...  1.46 us
  transfers between devices with their start and end apart: 6, of which 5 were waited for; matrix products, arithmetic and copies ran while one was open for 0% of the time, Pallas kernels for 1%

profile of v1, /device:TPU:0, one launch (start us, length us, event | category | flops | bytes accessed | tf_op | source)
XLA Modules:
  0.0 29.0 jit_solution(3627502725273274450)
XLA Ops:
  0.6 0.0 copy-start.12
  0.6 0.0 copy-start.9
  0.7 0.0 copy-start.10
  0.7 0.0 copy-start.11
  0.7 0.6 %copy-done.12 = s32[12]{0:T(128)S(1)} copy-done((s32[12]{0:T(128)S(1)}, s32[12]{0:T(128)}, u32[]{:S(2)}) %copy-start.12) | copy-done | bytes 72
  1.3 0.0 copy-done.9
  1.3 0.0 copy-done.10
  1.3 0.0 copy-done.11
  1.3 1.0 %copy-done = f32[4,32,8,128]{3,2,1,0:T(8,128)S(1)} copy-done((f32[4,32,8,128]{3,2,1,0:T(8,128)S(1)}, f32[4,32,8,128]{3,2,1,0:T(8,128)}, u32[]{:S(2)}) %copy-start) | copy-done | bytes 524312
  2.4 0.9 %copy-done.2 = f32[4,8,16,128]{3,2,1,0:T(8,128)S(1)} copy-done((f32[4,8,16,128]{3,2,1,0:T(8,128)S(1)}, f32[4,8,16,128]{3,2,1,0:T(8,128)}, u32[]{:S(2)}) %copy-start.2) | copy-done | bytes 262168
  3.3 1.0 %copy-done.4 = bf16[12,128,128]{2,1,0:T(8,128)(2,1)S(1)} copy-done((bf16[12,128,128]{2,1,0:T(8,128)(2,1)S(1)}, bf16[12,128,128]{2,1,0:T(8,128)(2,1)}, u32[]{:S(2)}) %copy-start.4) | copy-done | bytes 393240
  4.3 0.8 %copy-done.5 = bf16[256,128]{1,0:T(8,128)(2,1)S(1)} copy-done((bf16[256,128]{1,0:T(8,128)(2,1)S(1)}, bf16[256,128]{1,0:T(8,128)(2,1)}, u32[]{:S(2)}) %copy-start.5) | copy-done | bytes 65560
  5.2 0.8 %copy-done.8 = bf16[16,1536]{1,0:T(8,128)(2,1)S(1)} copy-done((bf16[16,1536]{1,0:T(8,128)(2,1)S(1)}, bf16[16,1536]{1,0:T(8,128)(2,1)}, u32[]{:S(2)}) %copy-start.8) | copy-done | bytes 49176
  6.0 1.1 %pack.1 = (f32[36,4,128]{2,1,0:T(4,128)S(1)}, f32[16,128]{1,0:T(8,128)S(1)}, f32[2,160,128]{2,1,0:T(8,128)S(1)}) custom-call(f32[4]{0:T(128)S(1)} %copy-done.9, s32[12]{0:T(128)S(1)} %copy-done.10, s32[12]{0:T(128)S(1)} %bitcast.25, s32[12]{0:T(128)S(1)} %copy-done.12, f32[1024,128]{1,0:T(8,128)S(1)} %bitcast.20, f32[512,128]{1,0:T(8,128)S(1)} %bitcast.22, ...), custom_call_target="tpu_custom_call" | custom-call | tf_op jit(solution)/shard_map/pack/pallas_call | solution.py:275
  7.1 0.0 copy-start.1
  7.1 0.5 %collective-permute-start = (f32[80,128]{1,0:T(8,128)S(1)}, f32[80,128]{1,0:T(8,128)S(1)}, u32[]{:S(2)}, u32[]{:S(2)}) collective-permute-start(f32[80,128]{1,0:T(8,128)S(1)} %bitcast.29), channel_id=1, source_target_pairs={{0,1},{1,0},{2,3},{3,2},{4,5},{5,4},{6,7},{7,6},{8,9},{9,8},{10,11... | collective-permute-start | bytes 122888 | tf_op jit(solution)/shard_map/ppermute | solution.py:290
  7.7 0.9 %collective-permute-done = f32[80,128]{1,0:T(8,128)S(1)} collective-permute-done((f32[80,128]{1,0:T(8,128)S(1)}, f32[80,128]{1,0:T(8,128)S(1)}, u32[]{:S(2)}, u32[]{:S(2)}) %collective-permute-start) | collective-permute-done | bytes 40992 | tf_op jit(solution)/shard_map/ppermute | solution.py:290
  8.5 2.9 %collective-permute-start.4 = (f32[64,128]{1,0:T(8,128)S(1)}, f32[64,128]{1,0:T(8,128)S(1)}, u32[]{:S(2)}, u32[]{:S(2)}) collective-permute-start(f32[64,128]{1,0:T(8,128)S(1)} %bitcast.30), channel_id=1, source_target_pairs={{0,2},{1,3},{2,0},{3,1},{4,6},{5,7},{6,4},{7,5},{8,10},{9,11},{10,... | collective-permute-start | bytes 98312 | tf_op jit(solution)/shard_map/ppermute | solution.py:299
  11.4 1.9 %collective-permute-done.4 = f32[64,128]{1,0:T(8,128)S(1)} collective-permute-done((f32[64,128]{1,0:T(8,128)S(1)}, f32[64,128]{1,0:T(8,128)S(1)}, u32[]{:S(2)}, u32[]{:S(2)}) %collective-permute-start.4) | collective-permute-done | bytes 32800 | tf_op jit(solution)/shard_map/ppermute | solution.py:299
  13.3 0.0 copy-start.3
  13.4 2.1 %collective-permute-start.5 = (f32[64,128]{1,0:T(8,128)S(1)}, f32[64,128]{1,0:T(8,128)S(1)}, u32[]{:S(2)}, u32[]{:S(2)}) collective-permute-start(f32[64,128]{1,0:T(8,128)S(1)} %bitcast.31), channel_id=1, source_target_pairs={{0,4},{1,5},{2,6},{3,7},{4,0},{5,1},{6,2},{7,3},{8,12},{9,13},{10,... | collective-permute-start | bytes 98312 | tf_op jit(solution)/shard_map/ppermute | solution.py:299
  15.5 0.0 collective-permute-start.1
  15.5 4.0 %collective-permute-done.1.far = f32[16,128]{1,0:T(8,128)S(1)} collective-permute-done((f32[16,128]{1,0:T(8,128)S(1)}, f32[16,128]{1,0:T(8,128)S(1)}, u32[]{:S(2)}, u32[]{:S(2)}) %collective-permute-start.1) | collective-permute-done | bytes 8224 | tf_op jit(solution)/shard_map/ppermute | solution.py:291
  19.5 0.0 copy-done.7
  19.5 0.2 corners.1
  19.7 1.6 %collective-permute-start.2 = (f32[160,128]{1,0:T(8,128)S(1)}, f32[160,128]{1,0:T(8,128)S(1)}, u32[]{:S(2)}, u32[]{:S(2)}) collective-permute-start(f32[160,128]{1,0:T(8,128)S(1)} %get-tuple-element.12), channel_id=1, source_target_pairs={{0,8},{8,0},{16,24},{24,16},{1,9},{9,1},{17,25},{25,17},{2,10},{10... | collective-permute-start | bytes 245768 | tf_op jit(solution)/shard_map/ppermute | solution.py:314
  21.3 2.5 %collective-permute-start.3 = (f32[160,128]{1,0:T(8,128)S(1)}, f32[160,128]{1,0:T(8,128)S(1)}, u32[]{:S(2)}, u32[]{:S(2)}) collective-permute-start(f32[160,128]{1,0:T(8,128)S(1)} %get-tuple-element.13), channel_id=1, source_target_pairs={{0,24},{8,16},{16,8},{24,0},{1,25},{9,17},{17,9},{25,1},{2,26},{10... | collective-permute-start | bytes 245768 | tf_op jit(solution)/shard_map/ppermute | solution.py:315
  23.8 0.0 collective-permute-done.5
  23.8 0.4 %collective-permute-done.2.first = f32[160,128]{1,0:T(8,128)S(1)} collective-permute-done((f32[160,128]{1,0:T(8,128)S(1)}, f32[160,128]{1,0:T(8,128)S(1)}, u32[]{:S(2)}, u32[]{:S(2)}) %collective-permute-start.2) | collective-permute-done | bytes 81952 | tf_op jit(solution)/shard_map/ppermute | solution.py:314
  24.2 3.4 %collective-permute-done.3.second = f32[160,128]{1,0:T(8,128)S(1)} collective-permute-done((f32[160,128]{1,0:T(8,128)S(1)}, f32[160,128]{1,0:T(8,128)S(1)}, u32[]{:S(2)}, u32[]{:S(2)}) %collective-permute-start.3) | collective-permute-done | bytes 81952 | tf_op jit(solution)/shard_map/ppermute | solution.py:315
  27.6 0.0 copy-done.6
  27.6 1.5 %finish.1 = (f32[1024,128]{1,0:T(8,128)}, f32[512,128]{1,0:T(8,128)}) custom-call(f32[1024,128]{1,0:T(8,128)S(1)} %bitcast.21, f32[512,128]{1,0:T(8,128)S(1)} %bitcast.23, f32[16,128]{1,0:T(8,128)S(1)} %slice.37.near, f32[16,128]{1,0:T(8,128)S(1)} %collective-permute-done.1.far, f32[160,128]{1,0:T(8,128)S(1)} %collective-permute-done.2.first, ...), custom_call_target="tpu_custom_call" | custom-call | tf_op jit(solution)/shard_map/finish/pallas_call | solution.py:316
  (19 shorter events, 0.1 us)
Async XLA Ops:
  0.6 0.7 %copy-start.12 = (s32[12]{0:T(128)S(1)}, s32[12]{0:T(128)}, u32[]{:S(2)}) copy-start(s32[12]{0:T(128)} %target_row.1) | copy-start | bytes 148
  0.6 0.7 %copy-start.9 = (f32[4]{0:T(128)S(1)}, f32[4]{0:T(128)}, u32[]{:S(2)}) copy-start(f32[4]{0:T(128)} %coef.1) | copy-start | bytes 52
  0.7 0.7 %copy-start.10 = (s32[12]{0:T(128)S(1)}, s32[12]{0:T(128)}, u32[]{:S(2)}) copy-start(s32[12]{0:T(128)} %source.1) | copy-start | bytes 148
  0.7 0.7 %copy-start.11 = (s32[12,1]{0,1:T(1,128)S(1)}, s32[12,1]{0,1:T(1,128)}, u32[]{:S(2)}) copy-start(s32[12,1]{0,1:T(1,128)} %param.15) | copy-start | bytes 148
  1.3 1.0 %copy-start = (f32[4,32,8,128]{3,2,1,0:T(8,128)S(1)}, f32[4,32,8,128]{3,2,1,0:T(8,128)}, u32[]{:S(2)}) copy-start(f32[4,32,8,128]{3,2,1,0:T(8,128)} %param.10) | copy-start | bytes 1572868
  2.4 0.9 %copy-start.2 = (f32[4,8,16,128]{3,2,1,0:T(8,128)S(1)}, f32[4,8,16,128]{3,2,1,0:T(8,128)}, u32[]{:S(2)}) copy-start(f32[4,8,16,128]{3,2,1,0:T(8,128)} %param.11) | copy-start | bytes 786436
  3.3 1.0 %copy-start.4 = (bf16[12,128,128]{2,1,0:T(8,128)(2,1)S(1)}, bf16[12,128,128]{2,1,0:T(8,128)(2,1)}, u32[]{:S(2)}) copy-start(bf16[12,128,128]{2,1,0:T(8,128)(2,1)} %weight.1) | copy-start | bytes 1179652
  4.3 0.8 %copy-start.5 = (bf16[256,128]{1,0:T(8,128)(2,1)S(1)}, bf16[256,128]{1,0:T(8,128)(2,1)}, u32[]{:S(2)}) copy-start(bf16[256,128]{1,0:T(8,128)(2,1)} %constant.13.mix) | copy-start | bytes 196612
  5.2 0.8 %copy-start.8 = (bf16[16,1536]{1,0:T(8,128)(2,1)S(1)}, bf16[16,1536]{1,0:T(8,128)(2,1)}, u32[]{:S(2)}) copy-start(bf16[16,1536]{1,0:T(8,128)(2,1)} %constant.14.edge) | copy-start | bytes 147460
  7.1 20.4 %copy-start.1 = (f32[4,32,8,128]{3,2,1,0:T(8,128)S(1)}, f32[4,32,8,128]{3,2,1,0:T(8,128)}, u32[]{:S(2)}) copy-start(f32[4,32,8,128]{3,2,1,0:T(8,128)} %param.10) | copy-start | bytes 1572868
  7.1 1.4 %collective-permute-start = (f32[80,128]{1,0:T(8,128)S(1)}, f32[80,128]{1,0:T(8,128)S(1)}, u32[]{:S(2)}, u32[]{:S(2)}) collective-permute-start(f32[80,128]{1,0:T(8,128)S(1)} %bitcast.29), channel_id=1, source_target_pairs={{0,1},{1,0},{2,3},{3,2},{4,5},{5,4},{6,7},{7,6},{8,9},{9,8},{10,11... | collective-permute-start | bytes 122888 | tf_op jit(solution)/shard_map/ppermute | solution.py:290
  8.5 4.8 %collective-permute-start.4 = (f32[64,128]{1,0:T(8,128)S(1)}, f32[64,128]{1,0:T(8,128)S(1)}, u32[]{:S(2)}, u32[]{:S(2)}) collective-permute-start(f32[64,128]{1,0:T(8,128)S(1)} %bitcast.30), channel_id=1, source_target_pairs={{0,2},{1,3},{2,0},{3,1},{4,6},{5,7},{6,4},{7,5},{8,10},{9,11},{10,... | collective-permute-start | bytes 98312 | tf_op jit(solution)/shard_map/ppermute | solution.py:299
  13.3 6.1 %copy-start.7 = (bf16[192,128]{1,0:T(8,128)(2,1)S(1)}, bf16[192,128]{1,0:T(8,128)(2,1)}, u32[]{:S(2)}) copy-start(bf16[192,128]{1,0:T(8,128)(2,1)} %constant.15.place) | copy-start | bytes 147460
  13.3 14.2 %copy-start.3 = (f32[4,8,16,128]{3,2,1,0:T(8,128)S(1)}, f32[4,8,16,128]{3,2,1,0:T(8,128)}, u32[]{:S(2)}) copy-start(f32[4,8,16,128]{3,2,1,0:T(8,128)} %param.11) | copy-start | bytes 786436
  13.4 10.4 %collective-permute-start.5 = (f32[64,128]{1,0:T(8,128)S(1)}, f32[64,128]{1,0:T(8,128)S(1)}, u32[]{:S(2)}, u32[]{:S(2)}) collective-permute-start(f32[64,128]{1,0:T(8,128)S(1)} %bitcast.31), channel_id=1, source_target_pairs={{0,4},{1,5},{2,6},{3,7},{4,0},{5,1},{6,2},{7,3},{8,12},{9,13},{10,... | collective-permute-start | bytes 98312 | tf_op jit(solution)/shard_map/ppermute | solution.py:299
  15.5 4.0 %collective-permute-start.1 = (f32[16,128]{1,0:T(8,128)S(1)}, f32[16,128]{1,0:T(8,128)S(1)}, u32[]{:S(2)}, u32[]{:S(2)}) collective-permute-start(f32[16,128]{1,0:T(8,128)S(1)} %get-tuple-element.10), channel_id=1, source_target_pairs={{0,7},{1,2},{2,1},{3,4},{4,3},{5,6},{6,5},{7,0},{8,15},{9,10},{10,... | collective-permute-start | bytes 24584 | tf_op jit(solution)/shard_map/ppermute | solution.py:291
  19.7 4.5 %collective-permute-start.2 = (f32[160,128]{1,0:T(8,128)S(1)}, f32[160,128]{1,0:T(8,128)S(1)}, u32[]{:S(2)}, u32[]{:S(2)}) collective-permute-start(f32[160,128]{1,0:T(8,128)S(1)} %get-tuple-element.12), channel_id=1, source_target_pairs={{0,8},{8,0},{16,24},{24,16},{1,9},{9,1},{17,25},{25,17},{2,10},{10... | collective-permute-start | bytes 245768 | tf_op jit(solution)/shard_map/ppermute | solution.py:314
  21.3 6.2 %collective-permute-start.3 = (f32[160,128]{1,0:T(8,128)S(1)}, f32[160,128]{1,0:T(8,128)S(1)}, u32[]{:S(2)}, u32[]{:S(2)}) collective-permute-start(f32[160,128]{1,0:T(8,128)S(1)} %get-tuple-element.13), channel_id=1, source_target_pairs={{0,24},{8,16},{16,8},{24,0},{1,25},{9,17},{17,9},{25,1},{2,26},{10... | collective-permute-start | bytes 245768 | tf_op jit(solution)/shard_map/ppermute | solution.py:315
  23.8 3.8 %copy-start.6 = (bf16[256,128]{1,0:T(8,128)(2,1)S(1)}, bf16[256,128]{1,0:T(8,128)(2,1)}, u32[]{:S(2)}) copy-start(bf16[256,128]{1,0:T(8,128)(2,1)} %constant.13.mix) | copy-start | bytes 196612

commit v2 on v1

--- a/solution.py
+++ b/solution.py
@@ -15,6 +15,7 @@
 SLOTS = 3
 GROUP = 4
 BLOCK = (SLOTS + 1) * GROUP
+ROOMLESS = 55096 * 1024
 HALO = 16
 
 
@@ -64,7 +65,7 @@
     bf = lambda a: jnp.asarray(a.astype(np.float32)).astype(jnp.bfloat16)
     return (
         bf(np.concatenate([inner, seam.T])),
-        bf(np.concatenate([edge_atmos, edge_ocean], axis=1)),
+        bf(np.pad(np.concatenate([edge_atmos, edge_ocean], axis=1), ((0, 112), (0, 0)))),
         bf(np.concatenate([place_atmos.reshape(-1, columns), place_ocean.reshape(-1, columns)])),
     )
 
@@ -96,41 +97,49 @@
     return sum(float(second[k % 4, j]) * rows[base + j] for j in range(4))
 
 
-def pack_kernel(
-    n, fields, levels, olev, oy,
-    coef, source, target, target_row, atmos, ocean, weight, mix, edge,
-    blocks, far, edges, surf, counts,
+def edge_kernel(
+    fields, levels, olev, oy, atmos_at, ocean_at, edge_at, near, far, atmos, ocean, edge, sems
 ):
     planes, cells = fields * levels, fields * olev
     ay = atmos.shape[0] // planes
     columns = atmos.shape[1]
-    items = weight.shape[0]
-    me = lax.axis_index("tile")
-    even = me % 2 == 0
-    rows = [row_of(atmos, k, planes, ay) for k in range(ay)]
-    halves = [r.astype(jnp.bfloat16) for r in rows]
-    inner, seam = mix[:columns, :], mix[columns:, :]
-    for slot, k in ((0, 0), (1, ay - 1)):
-        edges[slot, :planes, :] = dot(halves[k], inner) + dot(along_y(rows, k).astype(jnp.bfloat16), seam)
+    copies = [
+        pltpu.make_async_copy(atmos_at, atmos, sems.at[0]),
+        pltpu.make_async_copy(edge_at.at[pl.ds(0, 16), :], edge, sems.at[1]),
+        pltpu.make_async_copy(ocean_at, ocean, sems.at[2]),
+    ]
+    for copy in copies:
+        copy.start()
+    even = lax.axis_index("tile") % 2 == 0
+    width = ay * columns
+    copies[0].wait()
+    copies[1].wait()
+    halves = [row_of(atmos, k, planes, ay).astype(jnp.bfloat16) for k in range(ay)]
+    atmos_cols = dot_nt(edge[:, :width], jnp.concatenate(halves, axis=1))
+    copies[2].wait()
     cell_rows = [row_of(ocean, y, cells, oy) for y in range(oy)]
-    edges[0, planes:, :] = cell_rows[0]
-    edges[1, planes:, :] = cell_rows[oy - 1]
-    width = ay * columns
-    atmos_cols = dot_nt(edge[:, :width], jnp.concatenate(halves, axis=1))
     chunks = [jnp.concatenate(cell_rows[4 * c : 4 * c + 4], axis=0) for c in range(oy // 4)]
     parts = [split(c) for c in chunks]
     ocean_cols = dot_nt(edge[:, width:], jnp.concatenate([p[0] for p in parts], axis=1)) + dot_nt(
         edge[:, width:], jnp.concatenate([p[1] for p in parts], axis=1)
     )
     left, right = atmos_cols[:ay], atmos_cols[ay:]
-    near = jnp.where(even, right, left)
+    near[:ay, :] = jnp.where(even, right, left)
     far[:ay, :] = jnp.where(even, left, right)
+    near[ay:, :] = ocean_cols[:8]
     far[ay:, :] = ocean_cols[:8]
-    base = n * (SLOTS + 1)
-    for g in range(2):
-        blocks[base + g] = near[g * GROUP : (g + 1) * GROUP]
-        blocks[base + 2 + g] = ocean_cols[g * GROUP : (g + 1) * GROUP]
-    blocks[:base] = jnp.full((base, GROUP, columns), -1.0, jnp.float32)
+
+
+def share_kernel(
+    n, fields, levels, coef, source, target, target_row, atmos, weight, near,
+    keep, send, surf, blocks, counts,
+):
+    ay = atmos.shape[0] // (fields * levels)
+    columns = atmos.shape[1]
+    items = weight.shape[0]
+    half = n // 2 * (SLOTS + 1)
+    me = lax.axis_index("tile")
+    blocks[...] = jnp.full(blocks.shape, -1.0, jnp.float32)
     for y in range(ay):
         surf[y, fields:, :] = jnp.zeros((8 - fields, columns), jnp.float32)
     for f in range(fields):
@@ -154,18 +163,38 @@
         return carry
 
     lax.fori_loop(0, items, one, 0, unroll=items <= 16)
-
-
-def corner_kernel(planes, ay, near, far, edges, place, first, second):
+    keep[...] = blocks[:half]
+    send[:half] = blocks[half:]
+    for g in range(HALO // GROUP):
+        send[half + g] = near[g * GROUP : (g + 1) * GROUP, :]
+
+
+def corner_kernel(
+    fields, levels, olev, oy, atmos, ocean, near, far, mix, place, later_in, first, second, later
+):
+    planes, cells = fields * levels, fields * olev
+    ay = atmos.shape[0] // planes
+    columns = atmos.shape[1]
+    later[...] = later_in[...]
     even_tile = lax.axis_index("tile") % 2 == 0
     even_comp = lax.axis_index("comp") % 2 == 0
     halos = side_halos(even_tile, near[:ay, :], far[:ay, :])
-    top = edges[0, :planes, :] + dot_tn(halos, place[:16, :])
-    low = edges[1, :planes, :] + dot_tn(halos, place[(ay - 1) * 16 : ay * 16, :])
+    rows = [row_of(atmos, k, planes, ay) for k in range(ay)]
+    top, low = [across_row(rows, k, mix, halos, place) for k in (0, ay - 1)]
     first[:planes, :] = jnp.where(even_comp, low, top)
     second[:planes, :] = jnp.where(even_comp, top, low)
-    first[planes:, :] = jnp.where(even_comp, edges[1, planes:, :], edges[0, planes:, :])
-    second[planes:, :] = jnp.where(even_comp, edges[0, planes:, :], edges[1, planes:, :])
+    top, low = row_of(ocean, 0, cells, oy), row_of(ocean, oy - 1, cells, oy)
+    first[planes:, :] = jnp.where(even_comp, low, top)
+    second[planes:, :] = jnp.where(even_comp, top, low)
+
+
+def across_row(rows, k, mix, halos, place):
+    columns = mix.shape[1]
+    return (
+        dot(rows[k].astype(jnp.bfloat16), mix[:columns, :])
+        + dot(along_y(rows, k).astype(jnp.bfloat16), mix[columns:, :])
+        + dot_tn(halos, place[k * 16 : (k + 1) * 16, :])
+    )
 
 
 def side_halos(even_tile, near, far):
@@ -176,8 +205,8 @@
 
 def finish_kernel(
     n, bands, fields, levels, olev, oy,
-    atmos, ocean, near, far, first, second, shares, mix, place,
-    atmos_out, ocean_out,
+    atmos, ocean, near, far, first, second, kept, came, mix, place,
+    atmos_out, ocean_out, shares,
 ):
     planes, cells = fields * levels, fields * olev
     ay = atmos.shape[0] // planes
@@ -186,15 +215,11 @@
     even_tile, even_comp = me % 2 == 0, band % 2 == 0
     up_all = jnp.where(even_comp, second[...], first[...])
     down_all = jnp.where(even_comp, first[...], second[...])
+    shares[: kept.shape[0], :] = kept[...]
+    shares[kept.shape[0] :, :] = came[...]
     rows = [row_of(atmos, k, planes, ay) for k in range(ay)]
-    inner, seam = mix[:columns, :], mix[columns:, :]
     halos = side_halos(even_tile, near[:ay, :], far[:ay, :])
-    across = [
-        dot(rows[k].astype(jnp.bfloat16), inner)
-        + dot(along_y(rows, k).astype(jnp.bfloat16), seam)
-        + dot_tn(halos, place[k * 16 : (k + 1) * 16, :])
-        for k in range(ay)
-    ]
+    across = [across_row(rows, k, mix, halos, place) for k in range(ay)]
     for k in range(ay):
         if k % 4 == 0:
             smooth = (across[k] + (across[k - 1] if k else up_all[:planes])) * 0.5
@@ -272,58 +297,78 @@
     atmos = atmos_state.reshape(planes * ay, columns)
     ocean = ocean_state.reshape(cells * oy, columns)
     params = pltpu.CompilerParams(vmem_limit_bytes=32 * 1024 * 1024)
-    blocks, far_out, edges = pl.pallas_call(
-        functools.partial(pack_kernel, n, fields, levels, olev, oy),
+    near_out, far_out = pl.pallas_call(
+        functools.partial(edge_kernel, fields, levels, olev, oy),
+        out_shape=(jax.ShapeDtypeStruct((HALO, columns), f32),) * 2,
+        in_specs=[pl.BlockSpec(memory_space=pltpu.HBM)] * 3,
+        out_specs=(vmem, vmem),
+        scratch_shapes=[
+            pltpu.VMEM(atmos.shape, f32),
+            pltpu.VMEM(ocean.shape, f32),
+            pltpu.VMEM((16, edge.shape[1]), jnp.bfloat16),
+            pltpu.SemaphoreType.DMA((3,)),
+        ],
+        compiler_params=pltpu.CompilerParams(vmem_limit_bytes=ROOMLESS),
+        name="edges",
+    )(atmos, ocean, edge)
+    far = lax.ppermute(far_out, "tile", pair_over(n))
+    half = n // 2 * BLOCK
+    kept, send = pl.pallas_call(
+        functools.partial(share_kernel, n, fields, levels),
         out_shape=(
-            jax.ShapeDtypeStruct((n * (SLOTS + 1) + HALO // GROUP, GROUP, columns), f32),
-            jax.ShapeDtypeStruct((HALO, columns), f32),
-            jax.ShapeDtypeStruct((2, planes + cells, columns), f32),
+            jax.ShapeDtypeStruct((n // 2 * (SLOTS + 1), GROUP, columns), f32),
+            jax.ShapeDtypeStruct((n // 2 * (SLOTS + 1) + HALO // GROUP, GROUP, columns), f32),
         ),
-        in_specs=[smem] * 4 + [vmem] * 5,
-        out_specs=(vmem, vmem, vmem),
-        scratch_shapes=[pltpu.VMEM((ay, 8, columns), f32), pltpu.SMEM((n,), jnp.int32)],
+        in_specs=[smem] * 4 + [vmem] * 3,
+        out_specs=(vmem, vmem),
+        scratch_shapes=[
+            pltpu.VMEM((ay, 8, columns), f32),
+            pltpu.VMEM((n * (SLOTS + 1), GROUP, columns), f32),
+            pltpu.SMEM((n,), jnp.int32),
+        ],
         compiler_params=params,
-        name="pack",
-    )(flux_coef, source_row, target_device.reshape(-1), target_row, atmos, ocean, remap_weight, mix, edge)
-    flat = blocks.reshape(-1, columns)
-    half = n // 2 * BLOCK
-    got = lax.ppermute(flat[half:], "tile", pair_up(n))
-    far = lax.ppermute(far_out, "tile", pair_over(n))
+        name="shares",
+    )(flux_coef, source_row, target_device.reshape(-1), target_row, atmos, remap_weight, near_out)
+    got = lax.ppermute(send.reshape(-1, columns), "tile", pair_up(n))
     near = got[half:]
+    row_shape = jax.ShapeDtypeStruct((planes + cells, columns), f32)
     state = jnp.concatenate(
-        [flat[:half].reshape(n // 2, 1, BLOCK, columns), got[:half].reshape(n // 2, 1, BLOCK, columns)], axis=1
+        [kept.reshape(n // 2, 1, BLOCK, columns), got[:half].reshape(n // 2, 1, BLOCK, columns)], axis=1
     )
     bit = 2
     while bit < n:
         pairs = state.reshape(state.shape[0] // 2, 2, state.shape[1], BLOCK, columns)
-        came = lax.ppermute(
-            pairs[:, 1].reshape(-1, columns), "tile", [(i, i ^ bit) for i in range(n)]
-        ).reshape(pairs[:, 1].shape)
-        state = jnp.concatenate([pairs[:, 0], came], axis=1)
+        keep, send = pairs[:, 0], pairs[:, 1]
+        if bit == 2:
+            came = lax.ppermute(send.reshape(-1, columns), "tile", [(i, i ^ bit) for i in range(n)])
+            first_out, second_out, keep = pl.pallas_call(
+                functools.partial(corner_kernel, fields, levels, olev, oy),
+                out_shape=(row_shape, row_shape, jax.ShapeDtypeStruct((n // 2 * BLOCK, columns), f32)),
+                in_specs=[vmem] * 7,
+                out_specs=(vmem, vmem, vmem),
+                compiler_params=params,
+                name="corners",
+            )(atmos, ocean, near, far, mix, place, keep.reshape(-1, columns))
+            keep = keep.reshape(send.shape)
+            first = lax.ppermute(first_out, "comp", pair_up(bands))
+            second = lax.ppermute(second_out, "comp", pair_over(bands))
+        else:
+            came = lax.ppermute(send.reshape(-1, columns), "tile", [(i, i ^ bit) for i in range(n)])
+        came = came.reshape(send.shape)
+        state = jnp.concatenate([keep, came], axis=1)
         bit *= 2
-    shares = state.reshape(n * BLOCK, columns)
-    row_shape = jax.ShapeDtypeStruct((planes + cells, columns), f32)
-    first_out, second_out = pl.pallas_call(
-        functools.partial(corner_kernel, planes, ay),
-        out_shape=(row_shape, row_shape),
-        in_specs=[vmem] * 4,
-        out_specs=(vmem, vmem),
-        compiler_params=params,
-        name="corners",
-    )(near, far, edges, place)
-    first = lax.ppermute(first_out, "comp", pair_up(bands))
-    second = lax.ppermute(second_out, "comp", pair_over(bands))
     atmos_next, ocean_next = pl.pallas_call(
         functools.partial(finish_kernel, n, bands, fields, levels, olev, oy),
         out_shape=(
             jax.ShapeDtypeStruct(atmos.shape, f32),
             jax.ShapeDtypeStruct(ocean.shape, f32),
         ),
-        in_specs=[vmem] * 9,
+        in_specs=[vmem] * 10,
         out_specs=(vmem, vmem),
+        scratch_shapes=[pltpu.VMEM((n * BLOCK, columns), f32)],
         compiler_params=params,
         name="finish",
-    )(atmos, ocean, near, far, first, second, shares, mix, place)
+    )(atmos, ocean, near, far, first, second, keep.reshape(-1, columns), came.reshape(-1, columns), mix, place)
     return atmos_next.reshape(atmos_state.shape), ocean_next.reshape(ocean_state.shape)
 
 

time: 29.4 us -> 22.2 us (0.76)
  local copies, waits for them, and re-layouts: 5.34 us -> 0.68 us
  waiting for transfers between devices: 10.5 us -> 6.26 us
  Pallas kernels: 2.8 us -> 4.25 us
  starting transfers between devices: 9.65 us -> 10.1 us
    unnamed x28 -> x20, local copies, waits for them, and re-layouts: 5.32 us -> 0.67 us
    ppermute x1, waiting for transfers between devices: 3.37 us -> 0.01 us  [body(): second = lax.ppermute(second_out, 'comp', pair_over(bands))]
    pallas_call x2 -> x3, Pallas kernels: 1.34 us -> 2.77 us  [the longest x1 1.66 us: body(): pl.pallas_call(functools.partial(edge_kernel, fields, levels, olev, oy),...]
    ppermute x1, waiting for transfers between devices: 3.97 us -> 2.99 us  [body(): far = lax.ppermute(far_out, 'tile', pair_over(n))]
    ppermute x1, starting transfers between devices: 0.01 us -> 0.98 us  [body(): far = lax.ppermute(far_out, 'tile', pair_over(n))]
    ppermute x3, starting transfers between devices: 5.53 us -> 5 us  [the longest x2 4.49 us: body(): lax.ppermute(send.reshape(-1, columns), 'tile', [(i, i ^ bit) for i in ra...]
    ppermute x3, waiting for transfers between devices: 2.76 us -> 3.27 us  [the longest x2 2.4 us: body(): lax.ppermute(send.reshape(-1, columns), 'tile', [(i, i ^ bit) for i in ra...]
    ppermute x1, waiting for transfers between devices: 0.37 us -> 0.01 us  [body(): first = lax.ppermute(first_out, 'comp', pair_up(bands))]
  transfers between devices with their start and end apart: 6 -> 6, of which waited for: 5 -> 3; matrix products, arithmetic and copies ran while one was open for 0% -> 0% of each run, Pallas kernels for 1% -> 1%
where the time goes in v2:
time: 22.2 us; the launch traced here: 22.1 us
  starting transfers between devices  10.1 us (45%)
  waiting for transfers between devices  6.26 us (28%)
  Pallas kernels  4.25 us (19%)
  between operations  0.77 us (3%)
  local copies, waits for them, and re-layouts  0.68 us (3%)
    ppermute x2, starting transfers between devices, body(): lax.ppermute(send.reshape(-1, columns), 'tile', [(i, i ^ bit) for i in ra...  4.49 us
    ppermute x1, waiting for transfers between devices, body(): far = lax.ppermute(far_out, 'tile', pair_over(n))  2.99 us
    ppermute x1, starting transfers between devices, body(): second = lax.ppermute(second_out, 'comp', pair_over(bands))  2.48 us
    ppermute x2, waiting for transfers between devices, body(): lax.ppermute(send.reshape(-1, columns), 'tile', [(i, i ^ bit) for i in ra...  2.4 us
    pallas_call x1, Pallas kernels, body(): pl.pallas_call(functools.partial(edge_kernel, fields, levels, olev, oy),...  1.66 us
    ppermute x1, starting transfers between devices, body(): first = lax.ppermute(first_out, 'comp', pair_up(bands))  1.64 us
    pallas_call x1, Pallas kernels, body(): pl.pallas_call(functools.partial(finish_kernel, n, bands, fields, levels,...  1.48 us
    ppermute x1, starting transfers between devices, body(): far = lax.ppermute(far_out, 'tile', pair_over(n))  0.98 us
  transfers between devices with their start and end apart: 6, of which 3 were waited for; matrix products, arithmetic and copies ran while one was open for 0% of the time, Pallas kernels for 1%

profile of v2, /device:TPU:0, one launch (start us, length us, event | category | flops | bytes accessed | tf_op | source)
XLA Modules:
  0.0 22.1 jit_solution(17521255888773406093)
XLA Ops:
  0.6 0.0 copy-start
  0.6 0.0 copy-start.2
  0.6 0.0 copy-start.8
  0.7 1.7 %edges.1 = (f32[16,128]{1,0:T(8,128)S(1)}, f32[16,128]{1,0:T(8,128)S(1)}) custom-call(f32[1024,128]{1,0:T(8,128)} %bitcast.16, f32[512,128]{1,0:T(8,128)} %bitcast.20, bf16[128,1536]{1,0:T(8,128)(2,1)} %constant.13.edge_at), custom_call_target="tpu_custom_call" | custom-call | tf_op jit(solution)/shard_map/edges/pallas_call | solution.py:300
  2.3 0.0 copy-start.5
  2.3 0.0 copy-start.6
  2.4 0.0 copy-start.7
  2.4 0.0 copy-done
  2.4 0.0 copy-done.2
  2.4 0.0 copy-done.8
  2.4 0.6 %copy-done.5 = f32[4]{0:T(128)S(1)} copy-done((f32[4]{0:T(128)S(1)}, f32[4]{0:T(128)}, u32[]{:S(2)}) %copy-start.5) | copy-done | bytes 40
  3.0 0.0 copy-done.6
  3.0 0.0 copy-done.7
  3.0 0.8 %shares.1 = (f32[16,4,128]{2,1,0:T(4,128)S(1)}, f32[20,4,128]{2,1,0:T(4,128)S(1)}) custom-call(f32[4]{0:T(128)S(1)} %copy-done.5, s32[12]{0:T(128)S(1)} %copy-done.6, s32[12]{0:T(128)S(1)} %bitcast.27, s32[12]{0:T(128)S(1)} %copy-done.8, f32[1024,128]{1,0:T(8,128)S(1)} %bitcast.17, bf16[12,128,128]{2,1,0:T(8,128)(2,1)S(1)} %copy-done.2, ...), custom_call_target="tpu_custom_call" | custom-call | tf_op jit(solution)/shard_map/shares/pallas_call | solution.py:316
  3.9 0.0 copy-start.1
  3.9 0.5 %collective-permute-start = (f32[80,128]{1,0:T(8,128)S(1)}, f32[80,128]{1,0:T(8,128)S(1)}, u32[]{:S(2)}, u32[]{:S(2)}) collective-permute-start(f32[80,128]{1,0:T(8,128)S(1)} %bitcast.28), channel_id=1, source_target_pairs={{0,1},{1,0},{2,3},{3,2},{4,5},{5,4},{6,7},{7,6},{8,9},{9,8},{10,11... | collective-permute-start | bytes 122888 | tf_op jit(solution)/shard_map/ppermute | solution.py:332
  4.4 0.9 %collective-permute-done = f32[80,128]{1,0:T(8,128)S(1)} collective-permute-done((f32[80,128]{1,0:T(8,128)S(1)}, f32[80,128]{1,0:T(8,128)S(1)}, u32[]{:S(2)}, u32[]{:S(2)}) %collective-permute-start) | collective-permute-done | bytes 40992 | tf_op jit(solution)/shard_map/ppermute | solution.py:332
  5.3 0.0 copy-start.3
  5.3 2.9 %collective-permute-start.4 = (f32[64,128]{1,0:T(8,128)S(1)}, f32[64,128]{1,0:T(8,128)S(1)}, u32[]{:S(2)}, u32[]{:S(2)}) collective-permute-start(f32[64,128]{1,0:T(8,128)S(1)} %bitcast.30), channel_id=1, source_target_pairs={{0,2},{1,3},{2,0},{3,1},{4,6},{5,7},{6,4},{7,5},{8,10},{9,11},{10,... | collective-permute-start | bytes 98312 | tf_op jit(solution)/shard_map/ppermute | solution.py:343
  8.2 1.0 %collective-permute-start.1 = (f32[16,128]{1,0:T(8,128)S(1)}, f32[16,128]{1,0:T(8,128)S(1)}, u32[]{:S(2)}, u32[]{:S(2)}) collective-permute-start(f32[16,128]{1,0:T(8,128)S(1)} %get-tuple-element.13), channel_id=1, source_target_pairs={{0,7},{1,2},{2,1},{3,4},{4,3},{5,6},{6,5},{7,0},{8,15},{9,10},{10,... | collective-permute-start | bytes 24584 | tf_op jit(solution)/shard_map/ppermute | solution.py:314
  9.2 3.0 %collective-permute-done.1.far = f32[16,128]{1,0:T(8,128)S(1)} collective-permute-done((f32[16,128]{1,0:T(8,128)S(1)}, f32[16,128]{1,0:T(8,128)S(1)}, u32[]{:S(2)}, u32[]{:S(2)}) %collective-permute-start.1) | collective-permute-done | bytes 8224 | tf_op jit(solution)/shard_map/ppermute | solution.py:314
  12.2 0.0 copy-done.4
  12.2 0.0 copy-done.1
  12.2 0.3 %corners.1 = (f32[160,128]{1,0:T(8,128)S(1)}, f32[160,128]{1,0:T(8,128)S(1)}, f32[64,128]{1,0:T(8,128)S(1)}) custom-call(f32[1024,128]{1,0:T(8,128)S(1)} %bitcast.18, f32[512,128]{1,0:T(8,128)S(1)} %bitcast.21, f32[16,128]{1,0:T(8,128)S(1)} %slice.24.near, f32[16,128]{1,0:T(8,128)S(1)} %collective-permute-done.1.far, bf16[256,128]{1,0:T(8,128)(2,1)S(1)} %copy-done.3, ...), custom_call_target="tpu_custom_call" | custom-call | tf_op jit(solution)/shard_map/corners/pallas_call | solution.py:344
  12.5 1.6 %collective-permute-start.2 = (f32[160,128]{1,0:T(8,128)S(1)}, f32[160,128]{1,0:T(8,128)S(1)}, u32[]{:S(2)}, u32[]{:S(2)}) collective-permute-start(f32[160,128]{1,0:T(8,128)S(1)} %get-tuple-element.15), channel_id=1, source_target_pairs={{0,8},{8,0},{16,24},{24,16},{1,9},{9,1},{17,25},{25,17},{2,10},{10... | collective-permute-start | bytes 245768 | tf_op jit(solution)/shard_map/ppermute | solution.py:353
  14.1 2.5 %collective-permute-start.3 = (f32[160,128]{1,0:T(8,128)S(1)}, f32[160,128]{1,0:T(8,128)S(1)}, u32[]{:S(2)}, u32[]{:S(2)}) collective-permute-start(f32[160,128]{1,0:T(8,128)S(1)} %get-tuple-element.16), channel_id=1, source_target_pairs={{0,24},{8,16},{16,8},{24,0},{1,25},{9,17},{17,9},{25,1},{2,26},{10... | collective-permute-start | bytes 245768 | tf_op jit(solution)/shard_map/ppermute | solution.py:354
  16.6 0.0 collective-permute-done.4
  16.6 1.6 %collective-permute-start.5 = (f32[64,128]{1,0:T(8,128)S(1)}, f32[64,128]{1,0:T(8,128)S(1)}, u32[]{:S(2)}, u32[]{:S(2)}) collective-permute-start(f32[64,128]{1,0:T(8,128)S(1)} %bitcast.32), channel_id=1, source_target_pairs={{0,4},{1,5},{2,6},{3,7},{4,0},{5,1},{6,2},{7,3},{8,12},{9,13},{10,... | collective-permute-start | bytes 98312 | tf_op jit(solution)/shard_map/ppermute | solution.py:356
  18.2 2.4 %collective-permute-done.5.came = f32[64,128]{1,0:T(8,128)S(1)} collective-permute-done((f32[64,128]{1,0:T(8,128)S(1)}, f32[64,128]{1,0:T(8,128)S(1)}, u32[]{:S(2)}, u32[]{:S(2)}) %collective-permute-start.5) | collective-permute-done | bytes 32800 | tf_op jit(solution)/shard_map/ppermute | solution.py:356
  20.6 0.0 collective-permute-done.2.first
  20.6 0.0 collective-permute-done.3.second
  20.6 1.5 %finish.1 = (f32[1024,128]{1,0:T(8,128)}, f32[512,128]{1,0:T(8,128)}) custom-call(f32[1024,128]{1,0:T(8,128)S(1)} %bitcast.19, f32[512,128]{1,0:T(8,128)S(1)} %bitcast.22, f32[16,128]{1,0:T(8,128)S(1)} %slice.24.near, f32[16,128]{1,0:T(8,128)S(1)} %collective-permute-done.1.far, f32[160,128]{1,0:T(8,128)S(1)} %collective-permute-done.2.first, ...), custom_call_target="tpu_custom_call" | custom-call | tf_op jit(solution)/shard_map/finish/pallas_call | solution.py:360
  (9 shorter events, 0.0 us)
Async XLA Ops:
  0.6 1.7 %copy-start = (f32[4,32,8,128]{3,2,1,0:T(8,128)S(1)}, f32[4,32,8,128]{3,2,1,0:T(8,128)}, u32[]{:S(2)}) copy-start(f32[4,32,8,128]{3,2,1,0:T(8,128)} %param.10) | copy-start | bytes 1572868
  0.6 1.7 %copy-start.2 = (bf16[12,128,128]{2,1,0:T(8,128)(2,1)S(1)}, bf16[12,128,128]{2,1,0:T(8,128)(2,1)}, u32[]{:S(2)}) copy-start(bf16[12,128,128]{2,1,0:T(8,128)(2,1)} %weight.1) | copy-start | bytes 1179652
  0.6 1.7 %copy-start.8 = (s32[12]{0:T(128)S(1)}, s32[12]{0:T(128)}, u32[]{:S(2)}) copy-start(s32[12]{0:T(128)} %target_row.1) | copy-start | bytes 148
  2.3 0.7 %copy-start.5 = (f32[4]{0:T(128)S(1)}, f32[4]{0:T(128)}, u32[]{:S(2)}) copy-start(f32[4]{0:T(128)} %coef.1) | copy-start | bytes 52
  2.3 0.7 %copy-start.6 = (s32[12]{0:T(128)S(1)}, s32[12]{0:T(128)}, u32[]{:S(2)}) copy-start(s32[12]{0:T(128)} %source.1) | copy-start | bytes 148
  2.4 0.7 %copy-start.7 = (s32[12,1]{0,1:T(1,128)S(1)}, s32[12,1]{0,1:T(1,128)}, u32[]{:S(2)}) copy-start(s32[12,1]{0,1:T(1,128)} %param.15) | copy-start | bytes 148
  3.0 9.2 %copy-start.4 = (bf16[192,128]{1,0:T(8,128)(2,1)S(1)}, bf16[192,128]{1,0:T(8,128)(2,1)}, u32[]{:S(2)}) copy-start(bf16[192,128]{1,0:T(8,128)(2,1)} %constant.15.place) | copy-start | bytes 147460
  3.9 8.3 %copy-start.1 = (f32[4,8,16,128]{3,2,1,0:T(8,128)S(1)}, f32[4,8,16,128]{3,2,1,0:T(8,128)}, u32[]{:S(2)}) copy-start(f32[4,8,16,128]{3,2,1,0:T(8,128)} %param.11) | copy-start | bytes 786436
  3.9 1.4 %collective-permute-start = (f32[80,128]{1,0:T(8,128)S(1)}, f32[80,128]{1,0:T(8,128)S(1)}, u32[]{:S(2)}, u32[]{:S(2)}) collective-permute-start(f32[80,128]{1,0:T(8,128)S(1)} %bitcast.28), channel_id=1, source_target_pairs={{0,1},{1,0},{2,3},{3,2},{4,5},{5,4},{6,7},{7,6},{8,9},{9,8},{10,11... | collective-permute-start | bytes 122888 | tf_op jit(solution)/shard_map/ppermute | solution.py:332
  5.3 6.9 %copy-start.3 = (bf16[256,128]{1,0:T(8,128)(2,1)S(1)}, bf16[256,128]{1,0:T(8,128)(2,1)}, u32[]{:S(2)}) copy-start(bf16[256,128]{1,0:T(8,128)(2,1)} %constant.14.mix) | copy-start | bytes 196612
  5.3 11.3 %collective-permute-start.4 = (f32[64,128]{1,0:T(8,128)S(1)}, f32[64,128]{1,0:T(8,128)S(1)}, u32[]{:S(2)}, u32[]{:S(2)}) collective-permute-start(f32[64,128]{1,0:T(8,128)S(1)} %bitcast.30), channel_id=1, source_target_pairs={{0,2},{1,3},{2,0},{3,1},{4,6},{5,7},{6,4},{7,5},{8,10},{9,11},{10,... | collective-permute-start | bytes 98312 | tf_op jit(solution)/shard_map/ppermute | solution.py:343
  8.2 4.0 %collective-permute-start.1 = (f32[16,128]{1,0:T(8,128)S(1)}, f32[16,128]{1,0:T(8,128)S(1)}, u32[]{:S(2)}, u32[]{:S(2)}) collective-permute-start(f32[16,128]{1,0:T(8,128)S(1)} %get-tuple-element.13), channel_id=1, source_target_pairs={{0,7},{1,2},{2,1},{3,4},{4,3},{5,6},{6,5},{7,0},{8,15},{9,10},{10,... | collective-permute-start | bytes 24584 | tf_op jit(solution)/shard_map/ppermute | solution.py:314
  12.5 8.1 %collective-permute-start.2 = (f32[160,128]{1,0:T(8,128)S(1)}, f32[160,128]{1,0:T(8,128)S(1)}, u32[]{:S(2)}, u32[]{:S(2)}) collective-permute-start(f32[160,128]{1,0:T(8,128)S(1)} %get-tuple-element.15), channel_id=1, source_target_pairs={{0,8},{8,0},{16,24},{24,16},{1,9},{9,1},{17,25},{25,17},{2,10},{10... | collective-permute-start | bytes 245768 | tf_op jit(solution)/shard_map/ppermute | solution.py:353
  14.1 6.5 %collective-permute-start.3 = (f32[160,128]{1,0:T(8,128)S(1)}, f32[160,128]{1,0:T(8,128)S(1)}, u32[]{:S(2)}, u32[]{:S(2)}) collective-permute-start(f32[160,128]{1,0:T(8,128)S(1)} %get-tuple-element.16), channel_id=1, source_target_pairs={{0,24},{8,16},{16,8},{24,0},{1,25},{9,17},{17,9},{25,1},{2,26},{10... | collective-permute-start | bytes 245768 | tf_op jit(solution)/shard_map/ppermute | solution.py:354
  16.6 4.0 %collective-permute-start.5 = (f32[64,128]{1,0:T(8,128)S(1)}, f32[64,128]{1,0:T(8,128)S(1)}, u32[]{:S(2)}, u32[]{:S(2)}) collective-permute-start(f32[64,128]{1,0:T(8,128)S(1)} %bitcast.32), channel_id=1, source_target_pairs={{0,4},{1,5},{2,6},{3,7},{4,0},{5,1},{6,2},{7,3},{8,12},{9,13},{10,... | collective-permute-start | bytes 98312 | tf_op jit(solution)/shard_map/ppermute | solution.py:356

commit v3 on v2

v3 whole, which is shorter than its diff:
```python
import functools
import math

import jax
import jax.numpy as jnp
import numpy as np
from jax import lax
from jax.experimental import pallas as pl
from jax.experimental.pallas import tpu as pltpu
from jax.sharding import PartitionSpec as P

viscosity = 0.01
diffusion = 0.2
mixing_rate = 0.1
forcing_step = 0.5
SLOTS = 3
GROUP = 4
BLOCK = (SLOTS + 1) * GROUP
ROOMLESS = 55096 * 1024
HALO = 16


def gll_second():
    nodes = np.array([-1.0, -(0.2**0.5), 0.2**0.5, 1.0])
    derivative = np.zeros((4, 4))
    for i in range(4):
        for j in range(4):
            if i == j:
                derivative[i, j] = sum(1.0 / (nodes[i] - nodes[k]) for k in range(4) if k != i)
            else:
                top = np.prod([nodes[i] - nodes[k] for k in range(4) if k not in (i, j)])
                derivative[i, j] = top / np.prod([nodes[j] - nodes[k] for k in range(4) if k != j])
    return derivative @ derivative


def tables(columns):
    second = gll_second()
    along = np.kron(np.eye(columns // 4), second)
    seam = np.eye(columns)
    for x in range(0, columns, 4):
        for edge, other in ((x, x - 1), (x + 3, x + 4)):
            seam[edge, edge] = 0.5
            if 0 <= other < columns:
                seam[edge, other] = 0.5
    inner = (seam @ along).T
    first, last = np.eye(columns)[0], np.eye(columns)[-1]
    edge_atmos = np.zeros((16, 8 * columns))
    for k in range(8):
        for side, unit, row in ((0, first, along[0]), (8, last, along[-1])):
            edge_atmos[side + k, k * columns : (k + 1) * columns] += row
            for j in range(4):
                m = k // 4 * 4 + j
                edge_atmos[side + k, m * columns : (m + 1) * columns] += second[k % 4, j] * unit
    edge_ocean = np.zeros((16, 4 * columns))
    place_atmos = np.zeros((8, 16, columns))
    place_ocean = np.zeros((4, 16, columns))
    for c in range(4):
        edge_ocean[c, c * columns : (c + 1) * columns] = first
        edge_ocean[4 + c, c * columns : (c + 1) * columns] = last
        for part in (0, 8):
            place_ocean[c, part + c] = last
            place_ocean[c, part + 4 + c] = first
    for k in range(8):
        place_atmos[k, k] = 0.5 * first
        place_atmos[k, 8 + k] = 0.5 * last
    bf = lambda a: jnp.asarray(a.astype(np.float32)).astype(jnp.bfloat16)
    return (
        bf(np.concatenate([inner, seam.T])),
        bf(np.pad(np.concatenate([edge_atmos, edge_ocean], axis=1), ((0, 112), (0, 0)))),
        bf(np.concatenate([place_atmos.reshape(-1, columns), place_ocean.reshape(-1, columns)])),
    )


def dot(a, b):
    return jnp.dot(a, b, preferred_element_type=jnp.float32)


def dot_nt(a, b):
    return lax.dot_general(a, b, (((1,), (1,)), ((), ())), preferred_element_type=jnp.float32)


def dot_tn(a, b):
    return lax.dot_general(a, b, (((0,), (0,)), ((), ())), preferred_element_type=jnp.float32)


def split(v):
    high = v.astype(jnp.bfloat16)
    return high, (v - high.astype(jnp.float32)).astype(jnp.bfloat16)


def row_of(ref, k, count, stride):
    return ref[pl.ds(k, count, stride=stride), :]


def along_y(rows, k):
    second = gll_second()
    base = k // 4 * 4
    return sum(float(second[k % 4, j]) * rows[base + j] for j in range(4))


def edge_kernel(
    fields, levels, olev, oy, atmos_at, ocean_at, edge_at, near, far, ground, atmos, ocean, edge, sems
):
    planes, cells = fields * levels, fields * olev
    ay = atmos.shape[0] // planes
    columns = atmos.shape[1]
    copies = [
        pltpu.make_async_copy(atmos_at, atmos, sems.at[0]),
        pltpu.make_async_copy(edge_at.at[pl.ds(0, 16), :], edge, sems.at[1]),
        pltpu.make_async_copy(ocean_at, ocean, sems.at[2]),
    ]
    for copy in copies:
        copy.start()
    even = lax.axis_index("tile") % 2 == 0
    width = ay * columns
    copies[0].wait()
    copies[1].wait()
    halves = [row_of(atmos, k, planes, ay).astype(jnp.bfloat16) for k in range(ay)]
    atmos_cols = dot_nt(edge[:, :width], jnp.concatenate(halves, axis=1))
    for f in range(fields):
        ground[f * ay : (f + 1) * ay, :] = atmos[f * levels * ay : f * levels * ay + ay, :]
    copies[2].wait()
    cell_rows = [row_of(ocean, y, cells, oy) for y in range(oy)]
    chunks = [jnp.concatenate(cell_rows[4 * c : 4 * c + 4], axis=0) for c in range(oy // 4)]
    parts = [split(c) for c in chunks]
    ocean_cols = dot_nt(edge[:, width:], jnp.concatenate([p[0] for p in parts], axis=1)) + dot_nt(
        edge[:, width:], jnp.concatenate([p[1] for p in parts], axis=1)
    )
    left, right = atmos_cols[:ay], atmos_cols[ay:]
    near[:ay, :] = jnp.where(even, right, left)
    far[:ay, :] = jnp.where(even, left, right)
    near[ay:, :] = ocean_cols[:8]
    far[ay:, :] = ocean_cols[:8]


def share_kernel(
    n, fields, coef_in, source_in, target_in, target_row_in, ground, weight, near,
    keep, send, coef, source, target, target_row, surf, blocks, counts, sems,
):
    copies = [
        pltpu.make_async_copy(src, dst, sems.at[place])
        for place, (src, dst) in enumerate(
            ((coef_in, coef), (source_in, source), (target_in, target), (target_row_in, target_row))
        )
    ]
    for copy in copies:
        copy.start()
    ay = ground.shape[0] // fields
    columns = ground.shape[1]
    items = weight.shape[0]
    half = n // 2 * (SLOTS + 1)
    me = lax.axis_index("tile")
    blocks[...] = jnp.full(blocks.shape, -1.0, jnp.float32)
    for y in range(ay):
        surf[y, fields:, :] = jnp.zeros((8 - fields, columns), jnp.float32)
    for copy in copies:
        copy.wait()
    for f in range(fields):
        plane = ground[f * ay : (f + 1) * ay, :] * coef[f]
        for y in range(ay):
            surf[y, f : f + 1, :] = plane[y : y + 1]

    @pl.loop(0, n)
    def _(i):
        counts[i] = 0

    def some(first, many):
        results = [
            dot(surf[source[first + i]].astype(jnp.bfloat16), weight[first + i]) for i in range(many)
        ]
        for i in range(many):
            to = target[first + i]
            slot = counts[to]
            counts[to] = slot + 1
            offset = to ^ me
            at = ((offset % 2) * (n // 2) + offset // 2) * (SLOTS + 1)
            blocks[at + slot] = results[i][:fields]
            blocks[at + SLOTS, pl.ds(slot, 1), :] = jnp.full(
                (1, columns), target_row[first + i].astype(jnp.float32)
            )

    many = math.gcd(items, 12)

    if items == many:
        some(0, many)
    else:

        @pl.loop(0, items // many)
        def _(part):
            some(part * many, many)

    keep[...] = blocks[:half]
    send[:half] = blocks[half:]
    for g in range(HALO // GROUP):
        send[half + g] = near[g * GROUP : (g + 1) * GROUP, :]


def inner_kernel(fields, levels, olev, oy, atmos, ocean, mix, atmos_part, ends, ocean_part):
    planes, cells = fields * levels, fields * olev
    ay = atmos.shape[0] // planes
    columns = atmos.shape[1]
    rows = [row_of(atmos, k, planes, ay) for k in range(ay)]
    across = [
        dot(rows[k].astype(jnp.bfloat16), mix[:columns, :])
        + dot(along_y(rows, k).astype(jnp.bfloat16), mix[columns:, :])
        for k in range(ay)
    ]
    ends[:planes, :] = across[0]
    ends[planes:, :] = across[ay - 1]
    for k in range(ay):
        smooth = sum(share * across[j] for j, share in seam_rows(ay, k))
        atmos_part[k * planes : (k + 1) * planes, :] = rows[k] + viscosity * smooth
    col = lax.broadcasted_iota(jnp.int32, (cells, columns), 1)
    level = lax.broadcasted_iota(jnp.int32, (cells, columns), 0) % olev
    cell_rows = [row_of(ocean, y, cells, oy) for y in range(oy)]
    for y in range(oy):
        v = cell_rows[y]
        planar = (
            jnp.where(col == 0, 0.0, pltpu.roll(v, 1, 1))
            + jnp.where(col == columns - 1, 0.0, pltpu.roll(v, columns - 1, 1))
            - 4.0 * v
        )
        if y:
            planar = planar + cell_rows[y - 1]
        if y + 1 < oy:
            planar = planar + cell_rows[y + 1]
        upper = jnp.where(level == 0, v, pltpu.roll(v, 1, 0))
        lower = jnp.where(level == olev - 1, v, pltpu.roll(v, cells - 1, 0))
        vertical = upper + lower - 2.0 * v
        ocean_part[y * cells : (y + 1) * cells, :] = v + diffusion * planar + mixing_rate * vertical


def seam_rows(ay, k):
    if k % 4 == 0:
        return [(k, 0.5)] + ([(k - 1, 0.5)] if k else [])
    if k % 4 == 3:
        return [(k, 0.5)] + ([(k + 1, 0.5)] if k + 1 < ay else [])
    return [(k, 1.0)]


def corner_kernel(fields, olev, oy, ocean, near, far, ends, place, later_in, first, second, later):
    cells = fields * olev
    planes = ends.shape[0] // 2
    ay = near.shape[0] - 8
    later[...] = later_in[...]
    even_tile = lax.axis_index("tile") % 2 == 0
    even_comp = lax.axis_index("comp") % 2 == 0
    halos = side_halos(even_tile, near[:ay, :], far[:ay, :])
    top = ends[:planes, :] + dot_tn(halos, place[:16, :])
    low = ends[planes:, :] + dot_tn(halos, place[(ay - 1) * 16 : ay * 16, :])
    first[:planes, :] = jnp.where(even_comp, low, top)
    second[:planes, :] = jnp.where(even_comp, top, low)
    top, low = row_of(ocean, 0, cells, oy), row_of(ocean, oy - 1, cells, oy)
    first[planes:, :] = jnp.where(even_comp, low, top)
    second[planes:, :] = jnp.where(even_comp, top, low)


def side_kernel(n, ay, oy, near, far, atmos_in, ocean_in, place, atmos_part, ocean_part):
    columns = near.shape[1]
    planes, cells = atmos_in.shape[0] // ay, ocean_in.shape[0] // oy
    me = lax.axis_index("tile")
    even_tile = me % 2 == 0
    halos = side_halos(even_tile, near[:ay, :], far[:ay, :])
    sides = [dot_tn(halos, place[k * 16 : (k + 1) * 16, :]) for k in range(ay)]
    for k in range(ay):
        here = slice(k * planes, (k + 1) * planes)
        smooth = sum(share * sides[j] for j, share in seam_rows(ay, k))
        atmos_part[here, :] = atmos_in[here, :] + viscosity * smooth
    side = lax.broadcasted_iota(jnp.int32, (8, columns), 0)
    near_ocean, far_ocean = near[ay:, :], far[ay:, :]
    right_first = jnp.where(
        side < 4,
        jnp.where(me == n - 1, 0.0, jnp.where(even_tile, near_ocean, far_ocean)),
        jnp.where(me == 0, 0.0, jnp.where(even_tile, far_ocean, near_ocean)),
    )
    parts = jnp.concatenate(split(right_first), axis=0)
    for c in range(oy // 4):
        here = slice(c * 4 * cells, (c + 1) * 4 * cells)
        four = ocean_in[here, :] + diffusion * dot_tn(
            parts, place[(ay + c) * 16 : (ay + c + 1) * 16, :]
        )
        for j in range(4):
            ocean_part[pl.ds(4 * c + j, cells, stride=oy), :] = four[j * cells : (j + 1) * cells]


def side_halos(even_tile, near, far):
    left = jnp.where(even_tile, far, near)
    right = jnp.where(even_tile, near, far)
    return jnp.concatenate([left, right], axis=0).astype(jnp.bfloat16)


def finish_kernel(
    bands, fields, levels, first, second, kept, came, atmos_part, ocean_part,
    atmos_out, ocean_out, rims, cells_out, sems,
):
    columns = atmos_part.shape[1]
    planes = fields * levels
    ay = atmos_part.shape[0] // planes
    cells = first.shape[0] - planes
    oy = ocean_part.shape[0] // cells
    olev = cells // fields
    band = lax.axis_index("comp")
    even_comp = band % 2 == 0
    copies = []

    def send(src, dst):
        copies.append(pltpu.make_async_copy(src, dst, sems.at[len(copies)]))
        copies[-1].start()

    for k in range(1, ay - 1):
        send(atmos_part.at[pl.ds(k * planes, planes), :], atmos_out.at[:, k, :])
    up = jnp.where(even_comp, second[...], first[...])
    down = jnp.where(even_comp, first[...], second[...])
    for slot, k, beyond in ((0, 0, up), (1, ay - 1, down)):
        rims[slot] = atmos_part[k * planes : (k + 1) * planes, :] + (0.5 * viscosity) * beyond[:planes]
        send(rims.at[slot], atmos_out.at[:, k, :])
    cells_out[...] = ocean_part[...]
    for y, beyond in (
        (0, jnp.where(band == 0, 0.0, up[planes:])),
        (oy - 1, jnp.where(band == bands - 1, 0.0, down[planes:])),
    ):
        row = pl.ds(y, cells, stride=oy)
        cells_out[row, :] = cells_out[row, :] + diffusion * beyond
    for f in range(fields):
        deep = pl.ds((f * olev + 1) * oy, (olev - 1) * oy)
        send(cells_out.at[deep, :], ocean_out.at[deep, :])
    lane = lax.broadcasted_iota(jnp.int32, (1, columns), 1)
    row_id = lax.broadcasted_iota(jnp.int32, (fields * oy, columns), 0)
    remapped = jnp.zeros((fields * oy, columns), jnp.float32)
    for blocks in (kept, came):
        rows = blocks.shape[0]
        for start in range(0, rows, columns):
            count = min(columns, rows - start)
            ids = jnp.full((1, columns), -float(fields * oy), jnp.float32)
            for p in range(count // BLOCK):
                at = start + p * BLOCK + SLOTS * GROUP
                for slot in range(SLOTS):
                    here = lane // GROUP == (p * BLOCK) // GROUP + slot
                    ids = jnp.where(here, blocks[at + slot : at + slot + 1, :], ids)
            wanted = jnp.where(ids < 0, -1, ids.astype(jnp.int32) + lane % GROUP * oy)
            hitting = jnp.where(row_id == wanted, forcing_step, 0.0).astype(jnp.bfloat16)[:, :count]
            high, low = split(blocks[start : start + count, :])
            remapped = remapped + dot(hitting, high) + dot(hitting, low)
    for f in range(fields):
        top = pl.ds(f * olev * oy, oy)
        cells_out[top, :] = cells_out[top, :] + remapped[f * oy : (f + 1) * oy]
        send(cells_out.at[top, :], ocean_out.at[top, :])
    for copy in copies:
        copy.wait()


def cost(flops):
    return pl.CostEstimate(flops=flops, bytes_accessed=10**6, transcendentals=0)


def pair_up(count):
    return [(i, i ^ 1) for i in range(count)]


def pair_over(count):
    return [(i, (i + 1) % count if i % 2 else (i - 1) % count) for i in range(count)]


def body(mesh, atmos_state, ocean_state, flux_coef, remap_weight, source_row, target_device, target_row):
    n, bands = mesh.shape["tile"], mesh.shape["comp"]
    fields, levels, ay, columns = atmos_state.shape
    olev, oy = ocean_state.shape[1:3]
    planes, cells = fields * levels, fields * olev
    f32 = jnp.float32
    vmem = pl.BlockSpec(memory_space=pltpu.VMEM)
    smem = pl.BlockSpec(memory_space=pltpu.SMEM)
    mix, edge, place = tables(columns)
    atmos = atmos_state.reshape(planes * ay, columns)
    ocean = ocean_state.reshape(cells * oy, columns)
    params = pltpu.CompilerParams(vmem_limit_bytes=32 * 1024 * 1024)
    near_out, far_out, ground = pl.pallas_call(
        functools.partial(edge_kernel, fields, levels, olev, oy),
        out_shape=(
            jax.ShapeDtypeStruct((HALO, columns), f32),
            jax.ShapeDtypeStruct((HALO, columns), f32),
            jax.ShapeDtypeStruct((fields * ay, columns), f32),
        ),
        in_specs=[pl.BlockSpec(memory_space=pltpu.HBM)] * 3,
        out_specs=(vmem, vmem, vmem),
        scratch_shapes=[
            pltpu.VMEM(atmos.shape, f32),
            pltpu.VMEM(ocean.shape, f32),
            pltpu.VMEM((16, edge.shape[1]), jnp.bfloat16),
            pltpu.SemaphoreType.DMA((3,)),
        ],
        compiler_params=pltpu.CompilerParams(vmem_limit_bytes=ROOMLESS),
        name="edges",
    )(atmos, ocean, edge)
    far = lax.ppermute(far_out, "tile", pair_over(n))
    half = n // 2 * BLOCK
    kept, send = pl.pallas_call(
        functools.partial(share_kernel, n, fields),
        out_shape=(
            jax.ShapeDtypeStruct((n // 2 * (SLOTS + 1), GROUP, columns), f32),
            jax.ShapeDtypeStruct((n // 2 * (SLOTS + 1) + HALO // GROUP, GROUP, columns), f32),
        ),
        in_specs=[vmem] * 7,
        out_specs=(vmem, vmem),
        scratch_shapes=[
            pltpu.SMEM(flux_coef.shape, f32),
            pltpu.SMEM(source_row.shape, jnp.int32),
            pltpu.SMEM(source_row.shape, jnp.int32),
            pltpu.SMEM(source_row.shape, jnp.int32),
            pltpu.VMEM((ay, 8, columns), f32),
            pltpu.VMEM((n * (SLOTS + 1), GROUP, columns), f32),
            pltpu.SMEM((n,), jnp.int32),
            pltpu.SemaphoreType.DMA((4,)),
        ],
        compiler_params=params,
        name="shares",
    )(flux_coef, source_row, target_device.reshape(-1), target_row, ground, remap_weight, near_out)
    got = lax.ppermute(send.reshape(-1, columns), "tile", pair_up(n))
    near = got[half:]
    row_shape = jax.ShapeDtypeStruct((planes + cells, columns), f32)
    part_shapes = jax.ShapeDtypeStruct(atmos.shape, f32), jax.ShapeDtypeStruct(ocean.shape, f32)
    atmos_part, ends, ocean_part = pl.pallas_call(
        functools.partial(inner_kernel, fields, levels, olev, oy),
        out_shape=(part_shapes[0], jax.ShapeDtypeStruct((2 * planes, columns), f32), part_shapes[1]),
        in_specs=[vmem] * 3,
        out_specs=(vmem,) * 3,
        compiler_params=params,
        cost_estimate=cost(10**9),
        name="inner",
    )(atmos, ocean, mix)
    state = jnp.concatenate(
        [kept.reshape(n // 2, 1, BLOCK, columns), got[:half].reshape(n // 2, 1, BLOCK, columns)], axis=1
    )
    bit = 2
    while bit < n:
        pairs = state.reshape(state.shape[0] // 2, 2, state.shape[1], BLOCK, columns)
        keep, send = pairs[:, 0].reshape(-1, columns), pairs[:, 1].reshape(-1, columns)
        came = lax.ppermute(send, "tile", [(i, i ^ bit) for i in range(n)])
        if bit == 2:
            first_out, second_out, keep = pl.pallas_call(
                functools.partial(corner_kernel, fields, olev, oy),
                out_shape=(
                    row_shape,
                    row_shape,
                    jax.ShapeDtypeStruct(keep.shape, f32),
                ),
                in_specs=[vmem] * 6,
                out_specs=(vmem,) * 3,
                compiler_params=params,
                cost_estimate=cost(10**9),
                name="corners",
            )(ocean, near, far, ends, place, keep)
            second = lax.ppermute(second_out, "comp", pair_over(bands))
            first = lax.ppermute(first_out, "comp", pair_up(bands))
            atmos_part, ocean_part = pl.pallas_call(
                functools.partial(side_kernel, n, ay, oy),
                out_shape=part_shapes,
                in_specs=[vmem] * 5,
                out_specs=(vmem,) * 2,
                input_output_aliases={2: 0},
                compiler_params=params,
                cost_estimate=cost(10**8),
                name="sides",
            )(near, far, atmos_part, ocean_part, place)
        state = jnp.concatenate(
            [keep.reshape(pairs[:, 0].shape), came.reshape(pairs[:, 0].shape)], axis=1
        )
        bit *= 2
    hbm = pl.BlockSpec(memory_space=pltpu.HBM)
    atmos_next, ocean_next = pl.pallas_call(
        functools.partial(finish_kernel, bands, fields, levels),
        out_shape=(jax.ShapeDtypeStruct((planes, ay, columns), f32), part_shapes[1]),
        in_specs=[vmem] * 6,
        out_specs=(hbm, hbm),
        scratch_shapes=[
            pltpu.VMEM((2, planes, columns), f32),
            pltpu.VMEM(ocean.shape, f32),
            pltpu.SemaphoreType.DMA((ay + 2 * fields,)),
        ],
        compiler_params=params,
        name="finish",
    )(first, second, keep, came, atmos_part, ocean_part)
    return atmos_next.reshape(atmos_state.shape), ocean_next.reshape(ocean_state.shape)


def solution(mesh):
    return jax.shard_map(
        functools.partial(body, mesh),
        mesh=mesh,
        in_specs=(
            P(None, None, "comp", "tile"),
            P(None, None, "comp", "tile"),
            P(),
            P(("comp", "tile"), None, None),
            P(("comp", "tile")),
            P(("comp", "tile"), None),
            P(("comp", "tile")),
        ),
        out_specs=(P(None, None, "comp", "tile"), P(None, None, "comp", "tile")),
        check_vma=False,
    )
```

time: 22.2 us -> 18.6 us (0.84)
  waiting for transfers between devices: 6.26 us -> 2.83 us
  local copies, waits for them, and re-layouts: 0.68 us -> 0.07 us
  Pallas kernels: 4.25 us -> 4.65 us
    ppermute x2, starting transfers between devices: 4.49 us -> 1.65 us  [body(): came = lax.ppermute(send, 'tile', [(i, i ^ bit) for i in range(n)])]
    ppermute x1, starting transfers between devices: 0.98 us -> 3.56 us  [body(): far = lax.ppermute(far_out, 'tile', pair_over(n))]
    ppermute x1, waiting for transfers between devices: 2.99 us -> 0.69 us  [body(): far = lax.ppermute(far_out, 'tile', pair_over(n))]
    ppermute x1, waiting for transfers between devices: 0.87 us -> 0.01 us  [body(): got = lax.ppermute(send.reshape(-1, columns), 'tile', pair_up(n))]
    unnamed x20, local copies, waits for them, and re-layouts: 0.67 us -> 0.05 us
    pallas_call x3 -> x5, Pallas kernels: 2.58 us -> 2.99 us  [the longest x1 1 us: body(): pl.pallas_call(functools.partial(finish_kernel, bands, fields, levels), o...]
    ppermute x2, waiting for transfers between devices: 2.4 us -> 2 us  [body(): came = lax.ppermute(send, 'tile', [(i, i ^ bit) for i in range(n)])]
  transfers between devices with their start and end apart: 6 -> 6, of which waited for: 3 -> 3; matrix products, arithmetic and copies ran while one was open for 0% -> 0% of each run, Pallas kernels for 1% -> 6%
where the time goes in v3:
time: 18.6 us; the launch traced here: 18.4 us
  starting transfers between devices  9.97 us (54%)
  Pallas kernels  4.65 us (25%)
  waiting for transfers between devices  2.83 us (15%)
  between operations  0.85 us (5%)
    ppermute x1, starting transfers between devices, body(): far = lax.ppermute(far_out, 'tile', pair_over(n))  3.56 us
    ppermute x1, starting transfers between devices, body(): second = lax.ppermute(second_out, 'comp', pair_over(bands))  2.47 us
    ppermute x2, waiting for transfers between devices, body(): came = lax.ppermute(send, 'tile', [(i, i ^ bit) for i in range(n)])  2 us
    ppermute x1, starting transfers between devices, body(): first = lax.ppermute(first_out, 'comp', pair_up(bands))  1.76 us
    pallas_call x1, Pallas kernels, body(): pl.pallas_call(functools.partial(edge_kernel, fields, levels, olev, oy),...  1.66 us
    ppermute x2, starting transfers between devices, body(): came = lax.ppermute(send, 'tile', [(i, i ^ bit) for i in range(n)])  1.65 us
    pallas_call x1, Pallas kernels, body(): pl.pallas_call(functools.partial(finish_kernel, bands, fields, levels), o...  1 us
    pallas_call x1, Pallas kernels, body(): pl.pallas_call(functools.partial(share_kernel, n, fields), out_shape=(jax...  0.89 us
  transfers between devices with their start and end apart: 6, of which 3 were waited for; matrix products, arithmetic and copies ran while one was open for 0% of the time, Pallas kernels for 6%

profile of v3, /device:TPU:0, one launch (start us, length us, event | category | flops | bytes accessed | tf_op | source)
XLA Modules:
  0.0 18.4 jit_solution(6489784908960431376)
XLA Ops:
  0.6 0.0 copy-start.1
  0.6 0.0 copy-start.4
  0.7 0.0 copy-start.5
  0.7 0.0 copy-start.6
  0.7 0.0 copy-start.7
  0.7 0.0 copy-start
  0.7 1.7 %edges.1 = (f32[16,128]{1,0:T(8,128)S(1)}, f32[16,128]{1,0:T(8,128)S(1)}, f32[32,128]{1,0:T(8,128)S(1)}) custom-call(f32[1024,128]{1,0:T(8,128)} %bitcast.16, f32[512,128]{1,0:T(8,128)} %bitcast.18, bf16[128,1536]{1,0:T(8,128)(2,1)} %constant.13.edge_at), custom_call_target="tpu_custom_call" | custom-call | tf_op jit(solution)/shard_map/edges/pallas_call | solution.py:376
  2.4 0.0 copy-start.2
  2.4 0.0 copy-done.1
  2.4 0.0 copy-done.4
  2.4 0.0 copy-done.5
  2.4 0.0 copy-start.8
  2.4 0.9 %shares.1 = (f32[16,4,128]{2,1,0:T(4,128)S(1)}, f32[20,4,128]{2,1,0:T(4,128)S(1)}) custom-call(f32[4]{0:T(128)S(1)} %copy-done.4, s32[12]{0:T(128)S(1)} %copy-done.5, s32[12]{0:T(128)S(1)} %bitcast.25, s32[12]{0:T(128)S(1)} %copy-done.7, f32[32,128]{1,0:T(8,128)S(1)} %get-tuple-element.17.ground, bf16[12,128,128]{2,1,0:T(8,128)(2,1)S(1)} %copy-done.1, ...), custom_call_target="tpu_custom_call" | custom-call | tf_op jit(solution)/shard_map/shares/pallas_call | solution.py:396
  3.3 0.5 %collective-permute-start = (f32[80,128]{1,0:T(8,128)S(1)}, f32[80,128]{1,0:T(8,128)S(1)}, u32[]{:S(2)}, u32[]{:S(2)}) collective-permute-start(f32[80,128]{1,0:T(8,128)S(1)} %bitcast.26), channel_id=1, source_target_pairs={{0,1},{1,0},{2,3},{3,2},{4,5},{5,4},{6,7},{7,6},{8,9},{9,8},{10,11... | collective-permute-start | bytes 122888 | tf_op jit(solution)/shard_map/ppermute | solution.py:417
  3.8 3.6 %collective-permute-start.1 = (f32[16,128]{1,0:T(8,128)S(1)}, f32[16,128]{1,0:T(8,128)S(1)}, u32[]{:S(2)}, u32[]{:S(2)}) collective-permute-start(f32[16,128]{1,0:T(8,128)S(1)} %get-tuple-element.20), channel_id=1, source_target_pairs={{0,7},{1,2},{2,1},{3,4},{4,3},{5,6},{6,5},{7,0},{8,15},{9,10},{10,... | collective-permute-start | bytes 24584 | tf_op jit(solution)/shard_map/ppermute | solution.py:394
  7.4 0.0 copy-done
  7.4 0.0 copy-done.8
  7.4 0.5 %inner.1 = (f32[1024,128]{1,0:T(8,128)S(1)}, f32[256,128]{1,0:T(8,128)S(1)}, f32[512,128]{1,0:T(8,128)S(1)}) custom-call(f32[1024,128]{1,0:T(8,128)S(1)} %bitcast.17, f32[512,128]{1,0:T(8,128)S(1)} %bitcast.19, bf16[256,128]{1,0:T(8,128)(2,1)S(1)} %copy-done.8), custom_call_target="tpu_custom_call" | custom-call | flops 1000000000 | bytes 1000000 | tf_op jit(solution)/shard_map/inner/pallas_call | solution.py:421
  7.9 0.0 collective-permute-done
  8.0 0.0 copy-start.3
  8.0 0.1 collective-permute-start.4
  8.1 0.7 %collective-permute-done.1.far = f32[16,128]{1,0:T(8,128)S(1)} collective-permute-done((f32[16,128]{1,0:T(8,128)S(1)}, f32[16,128]{1,0:T(8,128)S(1)}, u32[]{:S(2)}, u32[]{:S(2)}) %collective-permute-start.1) | collective-permute-done | bytes 8224 | tf_op jit(solution)/shard_map/ppermute | solution.py:394
  8.8 0.2 %corners.1 = (f32[160,128]{1,0:T(8,128)S(1)}, f32[160,128]{1,0:T(8,128)S(1)}, f32[64,128]{1,0:T(8,128)S(1)}) custom-call(f32[512,128]{1,0:T(8,128)S(1)} %bitcast.20, f32[16,128]{1,0:T(8,128)S(1)} %slice.24.near, f32[16,128]{1,0:T(8,128)S(1)} %collective-permute-done.1.far, f32[256,128]{1,0:T(8,128)S(1)} %get-tuple-element.21.ends, ...), custom_call_target="tpu_custom_call" | custom-call | flops 1000000000 | bytes 1000000 | tf_op jit(solution)/shard_map/corners/pallas_call | solution.py:439
  9.0 1.8 %collective-permute-start.2 = (f32[160,128]{1,0:T(8,128)S(1)}, f32[160,128]{1,0:T(8,128)S(1)}, u32[]{:S(2)}, u32[]{:S(2)}) collective-permute-start(f32[160,128]{1,0:T(8,128)S(1)} %get-tuple-element.23), channel_id=1, source_target_pairs={{0,8},{8,0},{16,24},{24,16},{1,9},{9,1},{17,25},{25,17},{2,10},{10... | collective-permute-start | bytes 245768 | tf_op jit(solution)/shard_map/ppermute | solution.py:453
  10.7 2.5 %collective-permute-start.3 = (f32[160,128]{1,0:T(8,128)S(1)}, f32[160,128]{1,0:T(8,128)S(1)}, u32[]{:S(2)}, u32[]{:S(2)}) collective-permute-start(f32[160,128]{1,0:T(8,128)S(1)} %get-tuple-element.24), channel_id=1, source_target_pairs={{0,24},{8,16},{16,8},{24,0},{1,25},{9,17},{17,9},{25,1},{2,26},{10... | collective-permute-start | bytes 245768 | tf_op jit(solution)/shard_map/ppermute | solution.py:452
  13.2 0.0 collective-permute-done.4
  13.2 1.6 %collective-permute-start.5 = (f32[64,128]{1,0:T(8,128)S(1)}, f32[64,128]{1,0:T(8,128)S(1)}, u32[]{:S(2)}, u32[]{:S(2)}) collective-permute-start(f32[64,128]{1,0:T(8,128)S(1)} %bitcast.30), channel_id=1, source_target_pairs={{0,4},{1,5},{2,6},{3,7},{4,0},{5,1},{6,2},{7,3},{8,12},{9,13},{10,... | collective-permute-start | bytes 98312 | tf_op jit(solution)/shard_map/ppermute | solution.py:437
  14.8 0.4 %sides.1 = (f32[1024,128]{1,0:T(8,128)S(1)}, f32[512,128]{1,0:T(8,128)S(1)}) custom-call(f32[16,128]{1,0:T(8,128)S(1)} %slice.24.near, f32[16,128]{1,0:T(8,128)S(1)} %collective-permute-done.1.far, f32[1024,128]{1,0:T(8,128)S(1)} %get-tuple-element.26.atmos_in, f32[512,128]{1,0:T(8,128)S(1)} %get-tuple-element.27.ocean_in, ...), custom_call_target="tpu_custom_call", output_to_operand_aliasing={{0}: (2, {})} | custom-call | flops 100000000 | bytes 1000000 | tf_op jit(solution)/shard_map/sides/pallas_call | solution.py:454
  15.2 2.0 %collective-permute-done.5.came = f32[64,128]{1,0:T(8,128)S(1)} collective-permute-done((f32[64,128]{1,0:T(8,128)S(1)}, f32[64,128]{1,0:T(8,128)S(1)}, u32[]{:S(2)}, u32[]{:S(2)}) %collective-permute-start.5) | collective-permute-done | bytes 32800 | tf_op jit(solution)/shard_map/ppermute | solution.py:437
  17.2 0.0 collective-permute-done.2.first
  17.2 0.1 collective-permute-done.3.second
  17.4 1.0 %finish.1 = (f32[128,8,128]{2,1,0:T(8,128)}, f32[512,128]{1,0:T(8,128)}) custom-call(f32[160,128]{1,0:T(8,128)S(1)} %collective-permute-done.2.first, f32[160,128]{1,0:T(8,128)S(1)} %collective-permute-done.3.second, f32[64,128]{1,0:T(8,128)S(1)} %bitcast.21, f32[64,128]{1,0:T(8,128)S(1)} %collective-permute-done.5.came, ...), custom_call_target="tpu_custom_call" | custom-call | tf_op jit(solution)/shard_map/finish/pallas_call | solution.py:469
  (11 shorter events, 0.0 us)
Async XLA Ops:
  0.6 1.7 %copy-start.1 = (bf16[12,128,128]{2,1,0:T(8,128)(2,1)S(1)}, bf16[12,128,128]{2,1,0:T(8,128)(2,1)}, u32[]{:S(2)}) copy-start(bf16[12,128,128]{2,1,0:T(8,128)(2,1)} %weight.1) | copy-start | bytes 1179652
  0.6 1.7 %copy-start.4 = (f32[4]{0:T(128)S(1)}, f32[4]{0:T(128)}, u32[]{:S(2)}) copy-start(f32[4]{0:T(128)} %coef_in.1) | copy-start | bytes 52
  0.7 1.7 %copy-start.5 = (s32[12]{0:T(128)S(1)}, s32[12]{0:T(128)}, u32[]{:S(2)}) copy-start(s32[12]{0:T(128)} %source_in.1) | copy-start | bytes 148
  0.7 1.7 %copy-start.6 = (s32[12,1]{0,1:T(1,128)S(1)}, s32[12,1]{0,1:T(1,128)}, u32[]{:S(2)}) copy-start(s32[12,1]{0,1:T(1,128)} %param.15) | copy-start | bytes 148
  0.7 1.7 %copy-start.7 = (s32[12]{0:T(128)S(1)}, s32[12]{0:T(128)}, u32[]{:S(2)}) copy-start(s32[12]{0:T(128)} %target_row_in.1) | copy-start | bytes 148
  0.7 6.7 %copy-start = (f32[4,32,8,128]{3,2,1,0:T(8,128)S(1)}, f32[4,32,8,128]{3,2,1,0:T(8,128)}, u32[]{:S(2)}) copy-start(f32[4,32,8,128]{3,2,1,0:T(8,128)} %param.10) | copy-start | bytes 1572868
  2.4 5.0 %copy-start.2 = (f32[4,8,16,128]{3,2,1,0:T(8,128)S(1)}, f32[4,8,16,128]{3,2,1,0:T(8,128)}, u32[]{:S(2)}) copy-start(f32[4,8,16,128]{3,2,1,0:T(8,128)} %param.11) | copy-start | bytes 786436
  2.4 5.0 %copy-start.8 = (bf16[256,128]{1,0:T(8,128)(2,1)S(1)}, bf16[256,128]{1,0:T(8,128)(2,1)}, u32[]{:S(2)}) copy-start(bf16[256,128]{1,0:T(8,128)(2,1)} %constant.14.mix) | copy-start | bytes 196612
  3.3 4.6 %collective-permute-start = (f32[80,128]{1,0:T(8,128)S(1)}, f32[80,128]{1,0:T(8,128)S(1)}, u32[]{:S(2)}, u32[]{:S(2)}) collective-permute-start(f32[80,128]{1,0:T(8,128)S(1)} %bitcast.26), channel_id=1, source_target_pairs={{0,1},{1,0},{2,3},{3,2},{4,5},{5,4},{6,7},{7,6},{8,9},{9,8},{10,11... | collective-permute-start | bytes 122888 | tf_op jit(solution)/shard_map/ppermute | solution.py:417
  3.8 4.9 %collective-permute-start.1 = (f32[16,128]{1,0:T(8,128)S(1)}, f32[16,128]{1,0:T(8,128)S(1)}, u32[]{:S(2)}, u32[]{:S(2)}) collective-permute-start(f32[16,128]{1,0:T(8,128)S(1)} %get-tuple-element.20), channel_id=1, source_target_pairs={{0,7},{1,2},{2,1},{3,4},{4,3},{5,6},{6,5},{7,0},{8,15},{9,10},{10,... | collective-permute-start | bytes 24584 | tf_op jit(solution)/shard_map/ppermute | solution.py:394
  8.0 0.8 %copy-start.3 = (bf16[192,128]{1,0:T(8,128)(2,1)S(1)}, bf16[192,128]{1,0:T(8,128)(2,1)}, u32[]{:S(2)}) copy-start(bf16[192,128]{1,0:T(8,128)(2,1)} %constant.15.place) | copy-start | bytes 147460
  8.0 5.2 %collective-permute-start.4 = (f32[64,128]{1,0:T(8,128)S(1)}, f32[64,128]{1,0:T(8,128)S(1)}, u32[]{:S(2)}, u32[]{:S(2)}) collective-permute-start(f32[64,128]{1,0:T(8,128)S(1)} %bitcast.28), channel_id=1, source_target_pairs={{0,2},{1,3},{2,0},{3,1},{4,6},{5,7},{6,4},{7,5},{8,10},{9,11},{10,... | collective-permute-start | bytes 98312 | tf_op jit(solution)/shard_map/ppermute | solution.py:437
  9.0 8.2 %collective-permute-start.2 = (f32[160,128]{1,0:T(8,128)S(1)}, f32[160,128]{1,0:T(8,128)S(1)}, u32[]{:S(2)}, u32[]{:S(2)}) collective-permute-start(f32[160,128]{1,0:T(8,128)S(1)} %get-tuple-element.23), channel_id=1, source_target_pairs={{0,8},{8,0},{16,24},{24,16},{1,9},{9,1},{17,25},{25,17},{2,10},{10... | collective-permute-start | bytes 245768 | tf_op jit(solution)/shard_map/ppermute | solution.py:453
  10.7 6.6 %collective-permute-start.3 = (f32[160,128]{1,0:T(8,128)S(1)}, f32[160,128]{1,0:T(8,128)S(1)}, u32[]{:S(2)}, u32[]{:S(2)}) collective-permute-start(f32[160,128]{1,0:T(8,128)S(1)} %get-tuple-element.24), channel_id=1, source_target_pairs={{0,24},{8,16},{16,8},{24,0},{1,25},{9,17},{17,9},{25,1},{2,26},{10... | collective-permute-start | bytes 245768 | tf_op jit(solution)/shard_map/ppermute | solution.py:452
  13.2 4.0 %collective-permute-start.5 = (f32[64,128]{1,0:T(8,128)S(1)}, f32[64,128]{1,0:T(8,128)S(1)}, u32[]{:S(2)}, u32[]{:S(2)}) collective-permute-start(f32[64,128]{1,0:T(8,128)S(1)} %bitcast.30), channel_id=1, source_target_pairs={{0,4},{1,5},{2,6},{3,7},{4,0},{5,1},{6,2},{7,3},{8,12},{9,13},{10,... | collective-permute-start | bytes 98312 | tf_op jit(solution)/shard_map/ppermute | solution.py:437

commit v4 on v3

--- a/solution.py
+++ b/solution.py
@@ -17,6 +17,7 @@
 GROUP = 4
 BLOCK = (SLOTS + 1) * GROUP
 ROOMLESS = 55096 * 1024
+EDGES = 32
 HALO = 16
 
 
@@ -51,7 +52,7 @@
             for j in range(4):
                 m = k // 4 * 4 + j
                 edge_atmos[side + k, m * columns : (m + 1) * columns] += second[k % 4, j] * unit
-    edge_ocean = np.zeros((16, 4 * columns))
+    edge_ocean = np.zeros((8, 4 * columns))
     place_atmos = np.zeros((8, 16, columns))
     place_ocean = np.zeros((4, 16, columns))
     for c in range(4):
@@ -63,10 +64,13 @@
     for k in range(8):
         place_atmos[k, k] = 0.5 * first
         place_atmos[k, 8 + k] = 0.5 * last
+    edge = np.zeros((128, 12 * columns))
+    edge[:16, : 8 * columns] = edge_atmos
+    edge[16:24, 8 * columns :] = edge_ocean
     bf = lambda a: jnp.asarray(a.astype(np.float32)).astype(jnp.bfloat16)
     return (
         bf(np.concatenate([inner, seam.T])),
-        bf(np.pad(np.concatenate([edge_atmos, edge_ocean], axis=1), ((0, 112), (0, 0)))),
+        bf(edge),
         bf(np.concatenate([place_atmos.reshape(-1, columns), place_ocean.reshape(-1, columns)])),
     )
 
@@ -106,7 +110,7 @@
     columns = atmos.shape[1]
     copies = [
         pltpu.make_async_copy(atmos_at, atmos, sems.at[0]),
-        pltpu.make_async_copy(edge_at.at[pl.ds(0, 16), :], edge, sems.at[1]),
+        pltpu.make_async_copy(edge_at.at[pl.ds(0, EDGES), :], edge, sems.at[1]),
         pltpu.make_async_copy(ocean_at, ocean, sems.at[2]),
     ]
     for copy in copies:
@@ -116,35 +120,27 @@
     copies[0].wait()
     copies[1].wait()
     halves = [row_of(atmos, k, planes, ay).astype(jnp.bfloat16) for k in range(ay)]
-    atmos_cols = dot_nt(edge[:, :width], jnp.concatenate(halves, axis=1))
+    cols = dot_nt(jnp.concatenate(halves, axis=1), edge[:, :width])
     for f in range(fields):
         ground[f * ay : (f + 1) * ay, :] = atmos[f * levels * ay : f * levels * ay + ay, :]
     copies[2].wait()
     cell_rows = [row_of(ocean, y, cells, oy) for y in range(oy)]
     chunks = [jnp.concatenate(cell_rows[4 * c : 4 * c + 4], axis=0) for c in range(oy // 4)]
-    parts = [split(c) for c in chunks]
-    ocean_cols = dot_nt(edge[:, width:], jnp.concatenate([p[0] for p in parts], axis=1)) + dot_nt(
-        edge[:, width:], jnp.concatenate([p[1] for p in parts], axis=1)
-    )
+    for part in zip(*[split(c) for c in chunks]):
+        cols = cols + dot_nt(jnp.concatenate(part, axis=1), edge[:, width:])
+    cols = cols.T
+    atmos_cols, ocean_cols = cols[: 2 * ay], cols[2 * ay : 2 * ay + 8]
     left, right = atmos_cols[:ay], atmos_cols[ay:]
     near[:ay, :] = jnp.where(even, right, left)
     far[:ay, :] = jnp.where(even, left, right)
-    near[ay:, :] = ocean_cols[:8]
-    far[ay:, :] = ocean_cols[:8]
+    near[ay:, :] = ocean_cols
+    far[ay:, :] = ocean_cols
 
 
 def share_kernel(
     n, fields, coef_in, source_in, target_in, target_row_in, ground, weight, near,
-    keep, send, coef, source, target, target_row, surf, blocks, counts, sems,
+    keep, send, surf, blocks, counts,
 ):
-    copies = [
-        pltpu.make_async_copy(src, dst, sems.at[place])
-        for place, (src, dst) in enumerate(
-            ((coef_in, coef), (source_in, source), (target_in, target), (target_row_in, target_row))
-        )
-    ]
-    for copy in copies:
-        copy.start()
     ay = ground.shape[0] // fields
     columns = ground.shape[1]
     items = weight.shape[0]
@@ -153,10 +149,10 @@
     blocks[...] = jnp.full(blocks.shape, -1.0, jnp.float32)
     for y in range(ay):
         surf[y, fields:, :] = jnp.zeros((8 - fields, columns), jnp.float32)
-    for copy in copies:
-        copy.wait()
+    coef = coef_in[...]
+    source, target, target_row = source_in[...], target_in[...], target_row_in[...]
     for f in range(fields):
-        plane = ground[f * ay : (f + 1) * ay, :] * coef[f]
+        plane = ground[f * ay : (f + 1) * ay, :] * coef[0, f]
         for y in range(ay):
             surf[y, f : f + 1, :] = plane[y : y + 1]
 
@@ -166,29 +162,22 @@
 
     def some(first, many):
         results = [
-            dot(surf[source[first + i]].astype(jnp.bfloat16), weight[first + i]) for i in range(many)
+            dot(surf[source[0, first + i]].astype(jnp.bfloat16), weight[first + i]) for i in range(many)
         ]
         for i in range(many):
-            to = target[first + i]
+            to = target[0, first + i]
             slot = counts[to]
             counts[to] = slot + 1
             offset = to ^ me
             at = ((offset % 2) * (n // 2) + offset // 2) * (SLOTS + 1)
             blocks[at + slot] = results[i][:fields]
             blocks[at + SLOTS, pl.ds(slot, 1), :] = jnp.full(
-                (1, columns), target_row[first + i].astype(jnp.float32)
+                (1, columns), target_row[0, first + i].astype(jnp.float32)
             )
 
     many = math.gcd(items, 12)
-
-    if items == many:
-        some(0, many)
-    else:
-
-        @pl.loop(0, items // many)
-        def _(part):
-            some(part * many, many)
-
+    for part in range(items // many):
+        some(part * many, many)
     keep[...] = blocks[:half]
     send[:half] = blocks[half:]
     for g in range(HALO // GROUP):
@@ -238,21 +227,18 @@
     return [(k, 1.0)]
 
 
-def corner_kernel(fields, olev, oy, ocean, near, far, ends, place, later_in, first, second, later):
+def corner_kernel(fields, olev, oy, ocean, near, far, ends, place, later_in, low, top, later):
     cells = fields * olev
     planes = ends.shape[0] // 2
     ay = near.shape[0] - 8
     later[...] = later_in[...]
     even_tile = lax.axis_index("tile") % 2 == 0
-    even_comp = lax.axis_index("comp") % 2 == 0
     halos = side_halos(even_tile, near[:ay, :], far[:ay, :])
-    top = ends[:planes, :] + dot_tn(halos, place[:16, :])
-    low = ends[planes:, :] + dot_tn(halos, place[(ay - 1) * 16 : ay * 16, :])
-    first[:planes, :] = jnp.where(even_comp, low, top)
-    second[:planes, :] = jnp.where(even_comp, top, low)
-    top, low = row_of(ocean, 0, cells, oy), row_of(ocean, oy - 1, cells, oy)
-    first[planes:, :] = jnp.where(even_comp, low, top)
-    second[planes:, :] = jnp.where(even_comp, top, low)
+    for ref, slot, k, y in ((low, 1, ay - 1, oy - 1), (top, 0, 0, 0)):
+        ref[:planes, :] = ends[slot * planes : (slot + 1) * planes, :] + dot_tn(
+            halos, place[k * 16 : (k + 1) * 16, :]
+        )
+        ref[planes:, :] = row_of(ocean, y, cells, oy)
 
 
 def side_kernel(n, ay, oy, near, far, atmos_in, ocean_in, place, atmos_part, ocean_part):
@@ -290,17 +276,16 @@
 
 
 def finish_kernel(
-    bands, fields, levels, first, second, kept, came, atmos_part, ocean_part,
+    bands, fields, levels, up, came, down, kept, atmos_part, ocean_part,
     atmos_out, ocean_out, rims, cells_out, sems,
 ):
     columns = atmos_part.shape[1]
     planes = fields * levels
     ay = atmos_part.shape[0] // planes
-    cells = first.shape[0] - planes
+    cells = up.shape[0] - planes
     oy = ocean_part.shape[0] // cells
     olev = cells // fields
     band = lax.axis_index("comp")
-    even_comp = band % 2 == 0
     copies = []
 
     def send(src, dst):
@@ -309,15 +294,13 @@
 
     for k in range(1, ay - 1):
         send(atmos_part.at[pl.ds(k * planes, planes), :], atmos_out.at[:, k, :])
-    up = jnp.where(even_comp, second[...], first[...])
-    down = jnp.where(even_comp, first[...], second[...])
     for slot, k, beyond in ((0, 0, up), (1, ay - 1, down)):
-        rims[slot] = atmos_part[k * planes : (k + 1) * planes, :] + (0.5 * viscosity) * beyond[:planes]
+        rims[slot] = atmos_part[k * planes : (k + 1) * planes, :] + (0.5 * viscosity) * beyond[:planes, :]
         send(rims.at[slot], atmos_out.at[:, k, :])
     cells_out[...] = ocean_part[...]
     for y, beyond in (
-        (0, jnp.where(band == 0, 0.0, up[planes:])),
-        (oy - 1, jnp.where(band == bands - 1, 0.0, down[planes:])),
+        (0, jnp.where(band == 0, 0.0, up[planes:, :])),
+        (oy - 1, jnp.where(band == bands - 1, 0.0, down[planes:, :])),
     ):
         row = pl.ds(y, cells, stride=oy)
         cells_out[row, :] = cells_out[row, :] + diffusion * beyond
@@ -385,7 +368,7 @@
         scratch_shapes=[
             pltpu.VMEM(atmos.shape, f32),
             pltpu.VMEM(ocean.shape, f32),
-            pltpu.VMEM((16, edge.shape[1]), jnp.bfloat16),
+            pltpu.VMEM((EDGES, edge.shape[1]), jnp.bfloat16),
             pltpu.SemaphoreType.DMA((3,)),
         ],
         compiler_params=pltpu.CompilerParams(vmem_limit_bytes=ROOMLESS),
@@ -402,18 +385,13 @@
         in_specs=[vmem] * 7,
         out_specs=(vmem, vmem),
         scratch_shapes=[
-            pltpu.SMEM(flux_coef.shape, f32),
-            pltpu.SMEM(source_row.shape, jnp.int32),
-            pltpu.SMEM(source_row.shape, jnp.int32),
-            pltpu.SMEM(source_row.shape, jnp.int32),
             pltpu.VMEM((ay, 8, columns), f32),
             pltpu.VMEM((n * (SLOTS + 1), GROUP, columns), f32),
             pltpu.SMEM((n,), jnp.int32),
-            pltpu.SemaphoreType.DMA((4,)),
         ],
         compiler_params=params,
         name="shares",
-    )(flux_coef, source_row, target_device.reshape(-1), target_row, ground, remap_weight, near_out)
+    )(*[a.reshape(1, -1) for a in (flux_coef, source_row, target_device, target_row)], ground, remap_weight, near_out)
     got = lax.ppermute(send.reshape(-1, columns), "tile", pair_up(n))
     near = got[half:]
     row_shape = jax.ShapeDtypeStruct((planes + cells, columns), f32)
@@ -436,7 +414,7 @@
         keep, send = pairs[:, 0].reshape(-1, columns), pairs[:, 1].reshape(-1, columns)
         came = lax.ppermute(send, "tile", [(i, i ^ bit) for i in range(n)])
         if bit == 2:
-            first_out, second_out, keep = pl.pallas_call(
+            low_out, top_out, keep = pl.pallas_call(
                 functools.partial(corner_kernel, fields, olev, oy),
                 out_shape=(
                     row_shape,
@@ -449,8 +427,8 @@
                 cost_estimate=cost(10**9),
                 name="corners",
             )(ocean, near, far, ends, place, keep)
-            second = lax.ppermute(second_out, "comp", pair_over(bands))
-            first = lax.ppermute(first_out, "comp", pair_up(bands))
+            up = lax.ppermute(low_out, "comp", [(i, (i + 1) % bands) for i in range(bands)])
+            down = lax.ppermute(top_out, "comp", [(i, (i - 1) % bands) for i in range(bands)])
             atmos_part, ocean_part = pl.pallas_call(
                 functools.partial(side_kernel, n, ay, oy),
                 out_shape=part_shapes,
@@ -478,7 +456,7 @@
         ],
         compiler_params=params,
         name="finish",
-    )(first, second, keep, came, atmos_part, ocean_part)
+    )(up, came, down, keep, atmos_part, ocean_part)
     return atmos_next.reshape(atmos_state.shape), ocean_next.reshape(ocean_state.shape)
 
 

time: 18.6 us -> 17.5 us (0.941)
  Pallas kernels: 4.65 us -> 4.14 us
  waiting for transfers between devices: 2.83 us -> 2.56 us
  starting transfers between devices: 9.97 us -> 9.73 us
    pallas_call x1, Pallas kernels: 0.89 us -> 0.46 us  [body(): pl.pallas_call(functools.partial(share_kernel, n, fields), out_shape=(jax...]
    ppermute x2, starting transfers between devices: 4.24 us -> 3.87 us  [the longest x1 2.12 us: body(): lax.ppermute(top_out, 'comp', [(i, (i - 1) % bands) for i in range(bands)])]
  transfers between devices with their start and end apart: 6 -> 6, of which waited for: 3 -> 2; matrix products, arithmetic and copies ran while one was open for 0% -> 0% of each run, Pallas kernels for 6% -> 6%
where the time goes in v4:
time: 17.5 us; the launch traced here: 17.3 us
  starting transfers between devices  9.73 us (56%)
  Pallas kernels  4.14 us (24%)
  waiting for transfers between devices  2.56 us (15%)
  between operations  0.84 us (5%)
    ppermute x1, starting transfers between devices, body(): far = lax.ppermute(far_out, 'tile', pair_over(n))  3.56 us
    ppermute x1, starting transfers between devices, body(): lax.ppermute(top_out, 'comp', [(i, (i - 1) % bands) for i in range(bands)])  2.12 us
    ppermute x2, waiting for transfers between devices, body(): came = lax.ppermute(send, 'tile', [(i, i ^ bit) for i in range(n)])  1.87 us
    ppermute x2, starting transfers between devices, body(): came = lax.ppermute(send, 'tile', [(i, i ^ bit) for i in range(n)])  1.78 us
    ppermute x1, starting transfers between devices, body(): lax.ppermute(low_out, 'comp', [(i, (i + 1) % bands) for i in range(bands)])  1.75 us
    pallas_call x1, Pallas kernels, body(): pl.pallas_call(functools.partial(edge_kernel, fields, levels, olev, oy),...  1.57 us
    pallas_call x1, Pallas kernels, body(): pl.pallas_call(functools.partial(finish_kernel, bands, fields, levels), o...  1 us
    ppermute x1, waiting for transfers between devices, body(): far = lax.ppermute(far_out, 'tile', pair_over(n))  0.69 us
  transfers between devices with their start and end apart: 6, of which 2 were waited for; matrix products, arithmetic and copies ran while one was open for 0% of the time, Pallas kernels for 6%

profile of v4, /device:TPU:0, one launch (start us, length us, event | category | flops | bytes accessed | tf_op | source)
XLA Modules:
  0.0 17.3 jit_solution(2537477050417515690)
XLA Ops:
  0.6 0.0 copy-start.1
  0.6 0.0 copy-start.4
  0.7 0.0 copy-start.5
  0.7 0.0 copy-start.6
  0.7 0.0 copy-start.7
  0.7 0.0 copy-start
  0.7 1.6 %edges.1 = (f32[16,128]{1,0:T(8,128)S(1)}, f32[16,128]{1,0:T(8,128)S(1)}, f32[32,128]{1,0:T(8,128)S(1)}) custom-call(f32[1024,128]{1,0:T(8,128)} %bitcast.19, f32[512,128]{1,0:T(8,128)} %bitcast.21, bf16[128,1536]{1,0:T(8,128)(2,1)} %constant.13.edge_at), custom_call_target="tpu_custom_call" | custom-call | tf_op jit(solution)/shard_map/edges/pallas_call | solution.py:359
  2.3 0.0 copy-start.2
  2.3 0.0 copy-done.1
  2.3 0.0 copy-done.4
  2.3 0.0 copy-done.5
  2.3 0.0 copy-start.8
  2.3 0.5 %shares.1 = (f32[16,4,128]{2,1,0:T(4,128)S(1)}, f32[20,4,128]{2,1,0:T(4,128)S(1)}) custom-call(f32[1,4]{1,0:T(1,128)S(1)} %bitcast.28, s32[1,12]{1,0:T(1,128)S(1)} %bitcast.29, s32[1,12]{1,0:T(1,128)S(1)} %bitcast.30, s32[1,12]{1,0:T(1,128)S(1)} %bitcast.31, f32[32,128]{1,0:T(8,128)S(1)} %get-tuple-element.17.ground, bf16[12,128,128]{2,1,0:T(8,128)(2,1)S(1)} %copy-done.1, ...), custom_call_target="tpu_custom_call" | custom-call | tf_op jit(solution)/shard_map/shares/pallas_call | solution.py:379
  2.8 0.5 %collective-permute-start = (f32[80,128]{1,0:T(8,128)S(1)}, f32[80,128]{1,0:T(8,128)S(1)}, u32[]{:S(2)}, u32[]{:S(2)}) collective-permute-start(f32[80,128]{1,0:T(8,128)S(1)} %bitcast.32), channel_id=1, source_target_pairs={{0,1},{1,0},{2,3},{3,2},{4,5},{5,4},{6,7},{7,6},{8,9},{9,8},{10,11... | collective-permute-start | bytes 122888 | tf_op jit(solution)/shard_map/ppermute | solution.py:395
  3.3 3.6 %collective-permute-start.1 = (f32[16,128]{1,0:T(8,128)S(1)}, f32[16,128]{1,0:T(8,128)S(1)}, u32[]{:S(2)}, u32[]{:S(2)}) collective-permute-start(f32[16,128]{1,0:T(8,128)S(1)} %get-tuple-element.20), channel_id=1, source_target_pairs={{0,7},{1,2},{2,1},{3,4},{4,3},{5,6},{6,5},{7,0},{8,15},{9,10},{10,... | collective-permute-start | bytes 24584 | tf_op jit(solution)/shard_map/ppermute | solution.py:377
  6.9 0.0 copy-done
  6.9 0.0 copy-done.8
  6.9 0.5 %inner.1 = (f32[1024,128]{1,0:T(8,128)S(1)}, f32[256,128]{1,0:T(8,128)S(1)}, f32[512,128]{1,0:T(8,128)S(1)}) custom-call(f32[1024,128]{1,0:T(8,128)S(1)} %bitcast.20, f32[512,128]{1,0:T(8,128)S(1)} %bitcast.22, bf16[256,128]{1,0:T(8,128)(2,1)S(1)} %copy-done.8), custom_call_target="tpu_custom_call" | custom-call | flops 1000000000 | bytes 1000000 | tf_op jit(solution)/shard_map/inner/pallas_call | solution.py:399
  7.4 0.0 collective-permute-done
  7.4 0.0 copy-start.3
  7.5 0.1 collective-permute-start.3
  7.6 0.7 %collective-permute-done.1.far = f32[16,128]{1,0:T(8,128)S(1)} collective-permute-done((f32[16,128]{1,0:T(8,128)S(1)}, f32[16,128]{1,0:T(8,128)S(1)}, u32[]{:S(2)}, u32[]{:S(2)}) %collective-permute-start.1) | collective-permute-done | bytes 8224 | tf_op jit(solution)/shard_map/ppermute | solution.py:377
  8.2 0.2 %corners.1 = (f32[160,128]{1,0:T(8,128)S(1)}, f32[160,128]{1,0:T(8,128)S(1)}, f32[64,128]{1,0:T(8,128)S(1)}) custom-call(f32[512,128]{1,0:T(8,128)S(1)} %bitcast.23, f32[16,128]{1,0:T(8,128)S(1)} %slice.24.near, f32[16,128]{1,0:T(8,128)S(1)} %collective-permute-done.1.far, f32[256,128]{1,0:T(8,128)S(1)} %get-tuple-element.21.ends, ...), custom_call_target="tpu_custom_call" | custom-call | flops 1000000000 | bytes 1000000 | tf_op jit(solution)/shard_map/corners/pallas_call | solution.py:417
  8.5 1.7 %collective-permute-start.2 = (f32[160,128]{1,0:T(8,128)S(1)}, f32[160,128]{1,0:T(8,128)S(1)}, u32[]{:S(2)}, u32[]{:S(2)}) collective-permute-start(f32[160,128]{1,0:T(8,128)S(1)} %get-tuple-element.23), channel_id=1, source_target_pairs={{0,8},{8,16},{16,24},{24,0},{1,9},{9,17},{17,25},{25,1},{2,10},{10... | collective-permute-start | bytes 245768 | tf_op jit(solution)/shard_map/ppermute | solution.py:430
  10.2 2.1 %collective-permute-start.5 = (f32[160,128]{1,0:T(8,128)S(1)}, f32[160,128]{1,0:T(8,128)S(1)}, u32[]{:S(2)}, u32[]{:S(2)}) collective-permute-start(f32[160,128]{1,0:T(8,128)S(1)} %get-tuple-element.25), channel_id=1, source_target_pairs={{0,24},{8,0},{16,8},{24,16},{1,25},{9,1},{17,9},{25,17},{2,26},{10... | collective-permute-start | bytes 245768 | tf_op jit(solution)/shard_map/ppermute | solution.py:431
  12.3 0.0 collective-permute-done.3
  12.4 1.7 %collective-permute-start.4 = (f32[64,128]{1,0:T(8,128)S(1)}, f32[64,128]{1,0:T(8,128)S(1)}, u32[]{:S(2)}, u32[]{:S(2)}) collective-permute-start(f32[64,128]{1,0:T(8,128)S(1)} %bitcast.36), channel_id=1, source_target_pairs={{0,4},{1,5},{2,6},{3,7},{4,0},{5,1},{6,2},{7,3},{8,12},{9,13},{10,... | collective-permute-start | bytes 98312 | tf_op jit(solution)/shard_map/ppermute | solution.py:415
  14.1 0.4 %sides.1 = (f32[1024,128]{1,0:T(8,128)S(1)}, f32[512,128]{1,0:T(8,128)S(1)}) custom-call(f32[16,128]{1,0:T(8,128)S(1)} %slice.24.near, f32[16,128]{1,0:T(8,128)S(1)} %collective-permute-done.1.far, f32[1024,128]{1,0:T(8,128)S(1)} %get-tuple-element.26.atmos_in, f32[512,128]{1,0:T(8,128)S(1)} %get-tuple-element.27.ocean_in, ...), custom_call_target="tpu_custom_call", output_to_operand_aliasing={{0}: (2, {})} | custom-call | flops 100000000 | bytes 1000000 | tf_op jit(solution)/shard_map/sides/pallas_call | solution.py:432
  14.5 1.9 %collective-permute-done.4.came = f32[64,128]{1,0:T(8,128)S(1)} collective-permute-done((f32[64,128]{1,0:T(8,128)S(1)}, f32[64,128]{1,0:T(8,128)S(1)}, u32[]{:S(2)}, u32[]{:S(2)}) %collective-permute-start.4) | collective-permute-done | bytes 32800 | tf_op jit(solution)/shard_map/ppermute | solution.py:415
  16.3 0.0 collective-permute-done.2.up
  16.3 0.0 collective-permute-done.5.down
  16.3 1.0 %finish.1 = (f32[128,8,128]{2,1,0:T(8,128)}, f32[512,128]{1,0:T(8,128)}) custom-call(f32[160,128]{1,0:T(8,128)S(1)} %collective-permute-done.2.up, f32[64,128]{1,0:T(8,128)S(1)} %collective-permute-done.4.came, f32[160,128]{1,0:T(8,128)S(1)} %collective-permute-done.5.down, f32[64,128]{1,0:T(8,128)S(1)} %bitcast.24, ...), custom_call_target="tpu_custom_call" | custom-call | tf_op jit(solution)/shard_map/finish/pallas_call | solution.py:447
  (11 shorter events, 0.0 us)
Async XLA Ops:
  0.6 1.7 %copy-start.1 = (bf16[12,128,128]{2,1,0:T(8,128)(2,1)S(1)}, bf16[12,128,128]{2,1,0:T(8,128)(2,1)}, u32[]{:S(2)}) copy-start(bf16[12,128,128]{2,1,0:T(8,128)(2,1)} %weight.1) | copy-start | bytes 1179652
  0.6 1.7 %copy-start.4 = (f32[4]{0:T(128)S(1)}, f32[4]{0:T(128)}, u32[]{:S(2)}) copy-start(f32[4]{0:T(128)} %param.12) | copy-start | bytes 52
  0.7 1.7 %copy-start.5 = (s32[12]{0:T(128)S(1)}, s32[12]{0:T(128)}, u32[]{:S(2)}) copy-start(s32[12]{0:T(128)} %param.14) | copy-start | bytes 148
  0.7 1.7 %copy-start.6 = (s32[12,1]{0,1:T(1,128)S(1)}, s32[12,1]{0,1:T(1,128)}, u32[]{:S(2)}) copy-start(s32[12,1]{0,1:T(1,128)} %param.15) | copy-start | bytes 148
  0.7 1.7 %copy-start.7 = (s32[12]{0:T(128)S(1)}, s32[12]{0:T(128)}, u32[]{:S(2)}) copy-start(s32[12]{0:T(128)} %param.16) | copy-start | bytes 148
  0.7 6.2 %copy-start = (f32[4,32,8,128]{3,2,1,0:T(8,128)S(1)}, f32[4,32,8,128]{3,2,1,0:T(8,128)}, u32[]{:S(2)}) copy-start(f32[4,32,8,128]{3,2,1,0:T(8,128)} %param.10) | copy-start | bytes 1572868
  2.3 4.6 %copy-start.2 = (f32[4,8,16,128]{3,2,1,0:T(8,128)S(1)}, f32[4,8,16,128]{3,2,1,0:T(8,128)}, u32[]{:S(2)}) copy-start(f32[4,8,16,128]{3,2,1,0:T(8,128)} %param.11) | copy-start | bytes 786436
  2.3 4.6 %copy-start.8 = (bf16[256,128]{1,0:T(8,128)(2,1)S(1)}, bf16[256,128]{1,0:T(8,128)(2,1)}, u32[]{:S(2)}) copy-start(bf16[256,128]{1,0:T(8,128)(2,1)} %constant.14.mix) | copy-start | bytes 196612
  2.8 4.6 %collective-permute-start = (f32[80,128]{1,0:T(8,128)S(1)}, f32[80,128]{1,0:T(8,128)S(1)}, u32[]{:S(2)}, u32[]{:S(2)}) collective-permute-start(f32[80,128]{1,0:T(8,128)S(1)} %bitcast.32), channel_id=1, source_target_pairs={{0,1},{1,0},{2,3},{3,2},{4,5},{5,4},{6,7},{7,6},{8,9},{9,8},{10,11... | collective-permute-start | bytes 122888 | tf_op jit(solution)/shard_map/ppermute | solution.py:395
  3.3 4.9 %collective-permute-start.1 = (f32[16,128]{1,0:T(8,128)S(1)}, f32[16,128]{1,0:T(8,128)S(1)}, u32[]{:S(2)}, u32[]{:S(2)}) collective-permute-start(f32[16,128]{1,0:T(8,128)S(1)} %get-tuple-element.20), channel_id=1, source_target_pairs={{0,7},{1,2},{2,1},{3,4},{4,3},{5,6},{6,5},{7,0},{8,15},{9,10},{10,... | collective-permute-start | bytes 24584 | tf_op jit(solution)/shard_map/ppermute | solution.py:377
  7.4 0.8 %copy-start.3 = (bf16[192,128]{1,0:T(8,128)(2,1)S(1)}, bf16[192,128]{1,0:T(8,128)(2,1)}, u32[]{:S(2)}) copy-start(bf16[192,128]{1,0:T(8,128)(2,1)} %constant.15.place) | copy-start | bytes 147460
  7.5 4.9 %collective-permute-start.3 = (f32[64,128]{1,0:T(8,128)S(1)}, f32[64,128]{1,0:T(8,128)S(1)}, u32[]{:S(2)}, u32[]{:S(2)}) collective-permute-start(f32[64,128]{1,0:T(8,128)S(1)} %bitcast.34), channel_id=1, source_target_pairs={{0,2},{1,3},{2,0},{3,1},{4,6},{5,7},{6,4},{7,5},{8,10},{9,11},{10,... | collective-permute-start | bytes 98312 | tf_op jit(solution)/shard_map/ppermute | solution.py:415
  8.5 7.9 %collective-permute-start.2 = (f32[160,128]{1,0:T(8,128)S(1)}, f32[160,128]{1,0:T(8,128)S(1)}, u32[]{:S(2)}, u32[]{:S(2)}) collective-permute-start(f32[160,128]{1,0:T(8,128)S(1)} %get-tuple-element.23), channel_id=1, source_target_pairs={{0,8},{8,16},{16,24},{24,0},{1,9},{9,17},{17,25},{25,1},{2,10},{10... | collective-permute-start | bytes 245768 | tf_op jit(solution)/shard_map/ppermute | solution.py:430
  10.2 6.1 %collective-permute-start.5 = (f32[160,128]{1,0:T(8,128)S(1)}, f32[160,128]{1,0:T(8,128)S(1)}, u32[]{:S(2)}, u32[]{:S(2)}) collective-permute-start(f32[160,128]{1,0:T(8,128)S(1)} %get-tuple-element.25), channel_id=1, source_target_pairs={{0,24},{8,0},{16,8},{24,16},{1,25},{9,1},{17,9},{25,17},{2,26},{10... | collective-permute-start | bytes 245768 | tf_op jit(solution)/shard_map/ppermute | solution.py:431
  12.4 4.0 %collective-permute-start.4 = (f32[64,128]{1,0:T(8,128)S(1)}, f32[64,128]{1,0:T(8,128)S(1)}, u32[]{:S(2)}, u32[]{:S(2)}) collective-permute-start(f32[64,128]{1,0:T(8,128)S(1)} %bitcast.36), channel_id=1, source_target_pairs={{0,4},{1,5},{2,6},{3,7},{4,0},{5,1},{6,2},{7,3},{8,12},{9,13},{10,... | collective-permute-start | bytes 98312 | tf_op jit(solution)/shard_map/ppermute | solution.py:415

commit v5 on v4

--- a/solution.py
+++ b/solution.py
@@ -184,7 +184,7 @@
         send[half + g] = near[g * GROUP : (g + 1) * GROUP, :]
 
 
-def inner_kernel(fields, levels, olev, oy, atmos, ocean, mix, atmos_part, ends, ocean_part):
+def inner_kernel(fields, levels, olev, oy, atmos, ocean, mix, atmos_part, low, top, ocean_part):
     planes, cells = fields * levels, fields * olev
     ay = atmos.shape[0] // planes
     columns = atmos.shape[1]
@@ -194,14 +194,16 @@
         + dot(along_y(rows, k).astype(jnp.bfloat16), mix[columns:, :])
         for k in range(ay)
     ]
-    ends[:planes, :] = across[0]
-    ends[planes:, :] = across[ay - 1]
+    low[:planes, :] = across[ay - 1]
+    top[:planes, :] = across[0]
     for k in range(ay):
         smooth = sum(share * across[j] for j, share in seam_rows(ay, k))
         atmos_part[k * planes : (k + 1) * planes, :] = rows[k] + viscosity * smooth
     col = lax.broadcasted_iota(jnp.int32, (cells, columns), 1)
     level = lax.broadcasted_iota(jnp.int32, (cells, columns), 0) % olev
     cell_rows = [row_of(ocean, y, cells, oy) for y in range(oy)]
+    low[planes:, :] = cell_rows[oy - 1]
+    top[planes:, :] = cell_rows[0]
     for y in range(oy):
         v = cell_rows[y]
         planar = (
@@ -227,31 +229,37 @@
     return [(k, 1.0)]
 
 
-def corner_kernel(fields, olev, oy, ocean, near, far, ends, place, later_in, low, top, later):
-    cells = fields * olev
-    planes = ends.shape[0] // 2
+def corner_kernel(planes, near, far, low_in, top_in, place, later_in, low, top, later):
     ay = near.shape[0] - 8
     later[...] = later_in[...]
-    even_tile = lax.axis_index("tile") % 2 == 0
-    halos = side_halos(even_tile, near[:ay, :], far[:ay, :])
-    for ref, slot, k, y in ((low, 1, ay - 1, oy - 1), (top, 0, 0, 0)):
-        ref[:planes, :] = ends[slot * planes : (slot + 1) * planes, :] + dot_tn(
-            halos, place[k * 16 : (k + 1) * 16, :]
-        )
-        ref[planes:, :] = row_of(ocean, y, cells, oy)
-
-
-def side_kernel(n, ay, oy, near, far, atmos_in, ocean_in, place, atmos_part, ocean_part):
+    halos = side_halos(lax.axis_index("tile") % 2 == 0, near[:ay, :], far[:ay, :])
+    for ref, old, k in ((low, low_in, ay - 1), (top, top_in, 0)):
+        ref[:planes, :] = old[:planes, :] + dot_tn(halos, place[k * 16 : (k + 1) * 16, :])
+
+
+def side_kernel(
+    n, fields, near, far, atmos_in, ocean_in, blocks, place,
+    atmos_out, rims, ocean_part, remapped, inside, sem,
+):
     columns = near.shape[1]
-    planes, cells = atmos_in.shape[0] // ay, ocean_in.shape[0] // oy
+    planes, ay = atmos_out.shape[:2]
+    oy = remapped.shape[0] // fields
+    cells = ocean_in.shape[0] // oy
     me = lax.axis_index("tile")
     even_tile = me % 2 == 0
     halos = side_halos(even_tile, near[:ay, :], far[:ay, :])
     sides = [dot_tn(halos, place[k * 16 : (k + 1) * 16, :]) for k in range(ay)]
+    copies = []
     for k in range(ay):
         here = slice(k * planes, (k + 1) * planes)
         smooth = sum(share * sides[j] for j, share in seam_rows(ay, k))
-        atmos_part[here, :] = atmos_in[here, :] + viscosity * smooth
+        done = atmos_in[here, :] + viscosity * smooth
+        if k in (0, ay - 1):
+            rims[(planes if k else 0) : (2 * planes if k else planes), :] = done
+        else:
+            inside[k - 1] = done
+            copies.append(pltpu.make_async_copy(inside.at[k - 1], atmos_out.at[:, k, :], sem.at[k - 1]))
+            copies[-1].start()
     side = lax.broadcasted_iota(jnp.int32, (8, columns), 0)
     near_ocean, far_ocean = near[ay:, :], far[ay:, :]
     right_first = jnp.where(
@@ -267,6 +275,29 @@
         )
         for j in range(4):
             ocean_part[pl.ds(4 * c + j, cells, stride=oy), :] = four[j * cells : (j + 1) * cells]
+    remapped[...] = remap(blocks, fields, oy)
+    for copy in copies:
+        copy.wait()
+
+
+def remap(blocks, fields, oy):
+    rows, columns = blocks.shape
+    lane = lax.broadcasted_iota(jnp.int32, (1, columns), 1)
+    row_id = lax.broadcasted_iota(jnp.int32, (fields * oy, columns), 0)
+    total = jnp.zeros((fields * oy, columns), jnp.float32)
+    for start in range(0, rows, columns):
+        count = min(columns, rows - start)
+        ids = jnp.full((1, columns), -float(fields * oy), jnp.float32)
+        for p in range(count // BLOCK):
+            at = start + p * BLOCK + SLOTS * GROUP
+            for slot in range(SLOTS):
+                here = lane // GROUP == (p * BLOCK) // GROUP + slot
+                ids = jnp.where(here, blocks[at + slot : at + slot + 1, :], ids)
+        wanted = jnp.where(ids < 0, -1, ids.astype(jnp.int32) + lane % GROUP * oy)
+        hitting = jnp.where(row_id == wanted, forcing_step, 0.0).astype(jnp.bfloat16)[:, :count]
+        high, low = split(blocks[start : start + count, :])
+        total = total + dot(hitting, high) + dot(hitting, low)
+    return total
 
 
 def side_halos(even_tile, near, far):
@@ -276,12 +307,11 @@
 
 
 def finish_kernel(
-    bands, fields, levels, up, came, down, kept, atmos_part, ocean_part,
-    atmos_out, ocean_out, rims, cells_out, sems,
+    bands, fields, levels, up, came, down, atmos_so_far, rims, ocean_part, remapped,
+    atmos_out, ocean_out, rims_out, cells_out, sems,
 ):
-    columns = atmos_part.shape[1]
     planes = fields * levels
-    ay = atmos_part.shape[0] // planes
+    ay = atmos_out.shape[1]
     cells = up.shape[0] - planes
     oy = ocean_part.shape[0] // cells
     olev = cells // fields
@@ -292,11 +322,6 @@
         copies.append(pltpu.make_async_copy(src, dst, sems.at[len(copies)]))
         copies[-1].start()
 
-    for k in range(1, ay - 1):
-        send(atmos_part.at[pl.ds(k * planes, planes), :], atmos_out.at[:, k, :])
-    for slot, k, beyond in ((0, 0, up), (1, ay - 1, down)):
-        rims[slot] = atmos_part[k * planes : (k + 1) * planes, :] + (0.5 * viscosity) * beyond[:planes, :]
-        send(rims.at[slot], atmos_out.at[:, k, :])
     cells_out[...] = ocean_part[...]
     for y, beyond in (
         (0, jnp.where(band == 0, 0.0, up[planes:, :])),
@@ -307,26 +332,15 @@
     for f in range(fields):
         deep = pl.ds((f * olev + 1) * oy, (olev - 1) * oy)
         send(cells_out.at[deep, :], ocean_out.at[deep, :])
-    lane = lax.broadcasted_iota(jnp.int32, (1, columns), 1)
-    row_id = lax.broadcasted_iota(jnp.int32, (fields * oy, columns), 0)
-    remapped = jnp.zeros((fields * oy, columns), jnp.float32)
-    for blocks in (kept, came):
-        rows = blocks.shape[0]
-        for start in range(0, rows, columns):
-            count = min(columns, rows - start)
-            ids = jnp.full((1, columns), -float(fields * oy), jnp.float32)
-            for p in range(count // BLOCK):
-                at = start + p * BLOCK + SLOTS * GROUP
-                for slot in range(SLOTS):
-                    here = lane // GROUP == (p * BLOCK) // GROUP + slot
-                    ids = jnp.where(here, blocks[at + slot : at + slot + 1, :], ids)
-            wanted = jnp.where(ids < 0, -1, ids.astype(jnp.int32) + lane % GROUP * oy)
-            hitting = jnp.where(row_id == wanted, forcing_step, 0.0).astype(jnp.bfloat16)[:, :count]
-            high, low = split(blocks[start : start + count, :])
-            remapped = remapped + dot(hitting, high) + dot(hitting, low)
+    for slot, k, beyond in ((0, 0, up), (1, ay - 1, down)):
+        rims_out[slot] = (
+            rims[slot * planes : (slot + 1) * planes, :] + (0.5 * viscosity) * beyond[:planes, :]
+        )
+        send(rims_out.at[slot], atmos_out.at[:, k, :])
+    forcing = remapped[...] + remap(came, fields, oy)
     for f in range(fields):
         top = pl.ds(f * olev * oy, oy)
-        cells_out[top, :] = cells_out[top, :] + remapped[f * oy : (f + 1) * oy]
+        cells_out[top, :] = cells_out[top, :] + forcing[f * oy : (f + 1) * oy]
         send(cells_out.at[top, :], ocean_out.at[top, :])
     for copy in copies:
         copy.wait()
@@ -396,13 +410,13 @@
     near = got[half:]
     row_shape = jax.ShapeDtypeStruct((planes + cells, columns), f32)
     part_shapes = jax.ShapeDtypeStruct(atmos.shape, f32), jax.ShapeDtypeStruct(ocean.shape, f32)
-    atmos_part, ends, ocean_part = pl.pallas_call(
+    atmos_part, low, top, ocean_part = pl.pallas_call(
         functools.partial(inner_kernel, fields, levels, olev, oy),
-        out_shape=(part_shapes[0], jax.ShapeDtypeStruct((2 * planes, columns), f32), part_shapes[1]),
+        out_shape=(part_shapes[0], row_shape, row_shape, part_shapes[1]),
         in_specs=[vmem] * 3,
-        out_specs=(vmem,) * 3,
+        out_specs=(vmem,) * 4,
         compiler_params=params,
-        cost_estimate=cost(10**9),
+        cost_estimate=cost(10**6),
         name="inner",
     )(atmos, ocean, mix)
     state = jnp.concatenate(
@@ -414,49 +428,56 @@
         keep, send = pairs[:, 0].reshape(-1, columns), pairs[:, 1].reshape(-1, columns)
         came = lax.ppermute(send, "tile", [(i, i ^ bit) for i in range(n)])
         if bit == 2:
-            low_out, top_out, keep = pl.pallas_call(
-                functools.partial(corner_kernel, fields, olev, oy),
-                out_shape=(
-                    row_shape,
-                    row_shape,
-                    jax.ShapeDtypeStruct(keep.shape, f32),
-                ),
+            low, top, keep = pl.pallas_call(
+                functools.partial(corner_kernel, planes),
+                out_shape=(row_shape, row_shape, jax.ShapeDtypeStruct(keep.shape, f32)),
                 in_specs=[vmem] * 6,
                 out_specs=(vmem,) * 3,
+                input_output_aliases={2: 0, 3: 1},
                 compiler_params=params,
                 cost_estimate=cost(10**9),
                 name="corners",
-            )(ocean, near, far, ends, place, keep)
-            up = lax.ppermute(low_out, "comp", [(i, (i + 1) % bands) for i in range(bands)])
-            down = lax.ppermute(top_out, "comp", [(i, (i - 1) % bands) for i in range(bands)])
-            atmos_part, ocean_part = pl.pallas_call(
-                functools.partial(side_kernel, n, ay, oy),
-                out_shape=part_shapes,
-                in_specs=[vmem] * 5,
-                out_specs=(vmem,) * 2,
-                input_output_aliases={2: 0},
-                compiler_params=params,
-                cost_estimate=cost(10**8),
-                name="sides",
-            )(near, far, atmos_part, ocean_part, place)
+            )(near, far, low, top, place, keep)
+            up = lax.ppermute(low, "comp", [(i, (i + 1) % bands) for i in range(bands)])
+            down = lax.ppermute(top, "comp", [(i, (i - 1) % bands) for i in range(bands)])
         state = jnp.concatenate(
             [keep.reshape(pairs[:, 0].shape), came.reshape(pairs[:, 0].shape)], axis=1
         )
         bit *= 2
     hbm = pl.BlockSpec(memory_space=pltpu.HBM)
+    by_plane = jax.ShapeDtypeStruct((planes, ay, columns), f32)
+    atmos_so_far, rims, ocean_part, remapped = pl.pallas_call(
+        functools.partial(side_kernel, n, fields),
+        out_shape=(
+            by_plane,
+            jax.ShapeDtypeStruct((2 * planes, columns), f32),
+            part_shapes[1],
+            jax.ShapeDtypeStruct((fields * oy, columns), f32),
+        ),
+        in_specs=[vmem] * 6,
+        out_specs=(hbm, vmem, vmem, vmem),
+        scratch_shapes=[
+            pltpu.VMEM((ay - 2, planes, columns), f32),
+            pltpu.SemaphoreType.DMA((ay - 2,)),
+        ],
+        compiler_params=params,
+        cost_estimate=cost(10**8),
+        name="sides",
+    )(near, far, atmos_part, ocean_part, keep, place)
     atmos_next, ocean_next = pl.pallas_call(
         functools.partial(finish_kernel, bands, fields, levels),
-        out_shape=(jax.ShapeDtypeStruct((planes, ay, columns), f32), part_shapes[1]),
-        in_specs=[vmem] * 6,
+        out_shape=(by_plane, part_shapes[1]),
+        in_specs=[vmem] * 3 + [hbm] + [vmem] * 3,
         out_specs=(hbm, hbm),
         scratch_shapes=[
             pltpu.VMEM((2, planes, columns), f32),
             pltpu.VMEM(ocean.shape, f32),
-            pltpu.SemaphoreType.DMA((ay + 2 * fields,)),
+            pltpu.SemaphoreType.DMA((2 + 2 * fields,)),
         ],
+        input_output_aliases={3: 0},
         compiler_params=params,
         name="finish",
-    )(up, came, down, keep, atmos_part, ocean_part)
+    )(up, came, down, atmos_so_far, rims, ocean_part, remapped)
     return atmos_next.reshape(atmos_state.shape), ocean_next.reshape(ocean_state.shape)
 
 

time: 17.5 us -> 17.4 us (level)
  waiting for transfers between devices: 2.56 us -> 1.91 us
  Pallas kernels: 4.14 us -> 4.66 us
    ppermute x2, waiting for transfers between devices: 1.87 us -> 1.21 us  [body(): came = lax.ppermute(send, 'tile', [(i, i ^ bit) for i in range(n)])]
    pallas_call x2, Pallas kernels: 0.6 us -> 1.24 us  [the longest x1 1.05 us: body(): pl.pallas_call(functools.partial(side_kernel, n, fields), out_shape=(by_p...]
  transfers between devices with their start and end apart: 6 -> 6, of which waited for: 2 -> 2; matrix products, arithmetic and copies ran while one was open for 0% -> 0% of each run, Pallas kernels for 6% -> 10%
where the time goes in v5:
time: 17.4 us; the launch traced here: 17.2 us
  starting transfers between devices  9.73 us (56%)
  Pallas kernels  4.66 us (27%)
  waiting for transfers between devices  1.91 us (11%)
  between operations  0.85 us (5%)
    ppermute x1, starting transfers between devices, body(): far = lax.ppermute(far_out, 'tile', pair_over(n))  3.56 us
    ppermute x1, starting transfers between devices, body(): lax.ppermute(top, 'comp', [(i, (i - 1) % bands) for i in range(bands)])  2.12 us
    ppermute x2, starting transfers between devices, body(): came = lax.ppermute(send, 'tile', [(i, i ^ bit) for i in range(n)])  1.78 us
    ppermute x1, starting transfers between devices, body(): up = lax.ppermute(low, 'comp', [(i, (i + 1) % bands) for i in range(bands)])  1.76 us
    pallas_call x1, Pallas kernels, body(): pl.pallas_call(functools.partial(edge_kernel, fields, levels, olev, oy),...  1.57 us
    ppermute x2, waiting for transfers between devices, body(): came = lax.ppermute(send, 'tile', [(i, i ^ bit) for i in range(n)])  1.21 us
    pallas_call x1, Pallas kernels, body(): pl.pallas_call(functools.partial(side_kernel, n, fields), out_shape=(by_p...  1.05 us
    pallas_call x1, Pallas kernels, body(): pl.pallas_call(functools.partial(finish_kernel, bands, fields, levels), o...  0.88 us
  transfers between devices with their start and end apart: 6, of which 2 were waited for; matrix products, arithmetic and copies ran while one was open for 0% of the time, Pallas kernels for 10%

profile of v5, /device:TPU:0, one launch (start us, length us, event | category | flops | bytes accessed | tf_op | source)
XLA Modules:
  0.0 17.2 jit_solution(11401270583407472597)
XLA Ops:
  0.6 0.0 copy-start.2
  0.6 0.0 copy-start.5
  0.7 0.0 copy-start.6
  0.7 0.0 copy-start.7
  0.7 0.0 copy-start.8
  0.7 0.0 copy-start
  0.7 1.6 %edges.1 = (f32[16,128]{1,0:T(8,128)S(1)}, f32[16,128]{1,0:T(8,128)S(1)}, f32[32,128]{1,0:T(8,128)S(1)}) custom-call(f32[1024,128]{1,0:T(8,128)} %bitcast.19, f32[512,128]{1,0:T(8,128)} %bitcast.21, bf16[128,1536]{1,0:T(8,128)(2,1)} %constant.13.edge_at), custom_call_target="tpu_custom_call" | custom-call | tf_op jit(solution)/shard_map/edges/pallas_call | solution.py:373
  2.3 0.0 copy-start.1
  2.3 0.0 copy-done.2
  2.3 0.0 copy-done.5
  2.3 0.0 copy-done.6
  2.3 0.0 copy-done.7
  2.3 0.0 copy-start.3
  2.3 0.5 %shares.1 = (f32[16,4,128]{2,1,0:T(4,128)S(1)}, f32[20,4,128]{2,1,0:T(4,128)S(1)}) custom-call(f32[1,4]{1,0:T(1,128)S(1)} %bitcast.27, s32[1,12]{1,0:T(1,128)S(1)} %bitcast.28, s32[1,12]{1,0:T(1,128)S(1)} %bitcast.29, s32[1,12]{1,0:T(1,128)S(1)} %bitcast.30, f32[32,128]{1,0:T(8,128)S(1)} %get-tuple-element.20.ground, bf16[12,128,128]{2,1,0:T(8,128)(2,1)S(1)} %copy-done.2, ...), custom_call_target="tpu_custom_call" | custom-call | tf_op jit(solution)/shard_map/shares/pallas_call | solution.py:393
  2.8 0.5 %collective-permute-start = (f32[80,128]{1,0:T(8,128)S(1)}, f32[80,128]{1,0:T(8,128)S(1)}, u32[]{:S(2)}, u32[]{:S(2)}) collective-permute-start(f32[80,128]{1,0:T(8,128)S(1)} %bitcast.31), channel_id=1, source_target_pairs={{0,1},{1,0},{2,3},{3,2},{4,5},{5,4},{6,7},{7,6},{8,9},{9,8},{10,11... | collective-permute-start | bytes 122888 | tf_op jit(solution)/shard_map/ppermute | solution.py:409
  3.3 3.6 %collective-permute-start.1 = (f32[16,128]{1,0:T(8,128)S(1)}, f32[16,128]{1,0:T(8,128)S(1)}, u32[]{:S(2)}, u32[]{:S(2)}) collective-permute-start(f32[16,128]{1,0:T(8,128)S(1)} %get-tuple-element.23), channel_id=1, source_target_pairs={{0,7},{1,2},{2,1},{3,4},{4,3},{5,6},{6,5},{7,0},{8,15},{9,10},{10,... | collective-permute-start | bytes 24584 | tf_op jit(solution)/shard_map/ppermute | solution.py:391
  6.9 0.0 copy-done.3
  6.9 0.5 %inner.1 = (f32[1024,128]{1,0:T(8,128)S(1)}, f32[160,128]{1,0:T(8,128)S(1)}, f32[160,128]{1,0:T(8,128)S(1)}, f32[512,128]{1,0:T(8,128)S(1)}) custom-call(f32[1024,128]{1,0:T(8,128)S(1)} %bitcast.20, f32[512,128]{1,0:T(8,128)S(1)} %bitcast.22, bf16[256,128]{1,0:T(8,128)(2,1)S(1)} %copy-done.3), custom_call_target="tpu_custom_call" | custom-call | flops 1000000 | bytes 1000000 | tf_op jit(solution)/shard_map/inner/pallas_call | solution.py:413
  7.4 0.0 collective-permute-done
  7.4 0.0 copy-start.4
  7.5 0.1 collective-permute-start.3
  7.6 0.7 %collective-permute-done.1.far = f32[16,128]{1,0:T(8,128)S(1)} collective-permute-done((f32[16,128]{1,0:T(8,128)S(1)}, f32[16,128]{1,0:T(8,128)S(1)}, u32[]{:S(2)}, u32[]{:S(2)}) %collective-permute-start.1) | collective-permute-done | bytes 8224 | tf_op jit(solution)/shard_map/ppermute | solution.py:391
  8.2 0.2 %corners.1 = (f32[160,128]{1,0:T(8,128)S(1)}, f32[160,128]{1,0:T(8,128)S(1)}, f32[64,128]{1,0:T(8,128)S(1)}) custom-call(f32[16,128]{1,0:T(8,128)S(1)} %slice.24.near, f32[16,128]{1,0:T(8,128)S(1)} %collective-permute-done.1.far, f32[160,128]{1,0:T(8,128)S(1)} %get-tuple-element.24.low_in, ...), custom_call_target="tpu_custom_call", output_to_operand_aliasing={{0}: (2, {}), {1}: (3, {})} | custom-call | flops 1000000000 | bytes 1000000 | tf_op jit(solution)/shard_map/corners/pallas_call | solution.py:431
  8.4 1.8 %collective-permute-start.2 = (f32[160,128]{1,0:T(8,128)S(1)}, f32[160,128]{1,0:T(8,128)S(1)}, u32[]{:S(2)}, u32[]{:S(2)}) collective-permute-start(f32[160,128]{1,0:T(8,128)S(1)} %get-tuple-element.27), channel_id=1, source_target_pairs={{0,8},{8,16},{16,24},{24,0},{1,9},{9,17},{17,25},{25,1},{2,10},{10... | collective-permute-start | bytes 245768 | tf_op jit(solution)/shard_map/ppermute | solution.py:441
  10.2 2.1 %collective-permute-start.5 = (f32[160,128]{1,0:T(8,128)S(1)}, f32[160,128]{1,0:T(8,128)S(1)}, u32[]{:S(2)}, u32[]{:S(2)}) collective-permute-start(f32[160,128]{1,0:T(8,128)S(1)} %get-tuple-element.29), channel_id=1, source_target_pairs={{0,24},{8,0},{16,8},{24,16},{1,25},{9,1},{17,9},{25,17},{2,26},{10... | collective-permute-start | bytes 245768 | tf_op jit(solution)/shard_map/ppermute | solution.py:442
  12.3 0.0 collective-permute-done.3
  12.4 1.7 %collective-permute-start.4 = (f32[64,128]{1,0:T(8,128)S(1)}, f32[64,128]{1,0:T(8,128)S(1)}, u32[]{:S(2)}, u32[]{:S(2)}) collective-permute-start(f32[64,128]{1,0:T(8,128)S(1)} %bitcast.36), channel_id=1, source_target_pairs={{0,4},{1,5},{2,6},{3,7},{4,0},{5,1},{6,2},{7,3},{8,12},{9,13},{10,... | collective-permute-start | bytes 98312 | tf_op jit(solution)/shard_map/ppermute | solution.py:429
  14.1 1.1 %sides.1 = (f32[128,8,128]{2,1,0:T(8,128)}, f32[256,128]{1,0:T(8,128)S(1)}, f32[512,128]{1,0:T(8,128)S(1)}, f32[64,128]{1,0:T(8,128)S(1)}) custom-call(f32[16,128]{1,0:T(8,128)S(1)} %slice.24.near, f32[16,128]{1,0:T(8,128)S(1)} %collective-permute-done.1.far, f32[1024,128]{1,0:T(8,128)S(1)} %get-tuple-element.30.atmos_in, ...), custom_call_target="tpu_custom_call" | custom-call | flops 100000000 | bytes 1000000 | tf_op jit(solution)/shard_map/sides/pallas_call | solution.py:449
  15.1 1.2 %collective-permute-done.4.came = f32[64,128]{1,0:T(8,128)S(1)} collective-permute-done((f32[64,128]{1,0:T(8,128)S(1)}, f32[64,128]{1,0:T(8,128)S(1)}, u32[]{:S(2)}, u32[]{:S(2)}) %collective-permute-start.4) | collective-permute-done | bytes 32800 | tf_op jit(solution)/shard_map/ppermute | solution.py:429
  16.3 0.0 collective-permute-done.2.up
  16.3 0.0 collective-permute-done.5.down
  16.3 0.9 %finish.1 = (f32[128,8,128]{2,1,0:T(8,128)}, f32[512,128]{1,0:T(8,128)}) custom-call(f32[160,128]{1,0:T(8,128)S(1)} %collective-permute-done.2.up, f32[64,128]{1,0:T(8,128)S(1)} %collective-permute-done.4.came, f32[160,128]{1,0:T(8,128)S(1)} %collective-permute-done.5.down, ...), custom_call_target="tpu_custom_call", output_to_operand_aliasing={{0}: (3, {})} | custom-call | tf_op jit(solution)/shard_map/finish/pallas_call | solution.py:467
  (11 shorter events, 0.0 us)
Async XLA Ops:
  0.6 1.7 %copy-start.2 = (bf16[12,128,128]{2,1,0:T(8,128)(2,1)S(1)}, bf16[12,128,128]{2,1,0:T(8,128)(2,1)}, u32[]{:S(2)}) copy-start(bf16[12,128,128]{2,1,0:T(8,128)(2,1)} %weight.1) | copy-start | bytes 1179652
  0.6 1.7 %copy-start.5 = (f32[4]{0:T(128)S(1)}, f32[4]{0:T(128)}, u32[]{:S(2)}) copy-start(f32[4]{0:T(128)} %param.12) | copy-start | bytes 52
  0.7 1.7 %copy-start.6 = (s32[12]{0:T(128)S(1)}, s32[12]{0:T(128)}, u32[]{:S(2)}) copy-start(s32[12]{0:T(128)} %param.14) | copy-start | bytes 148
  0.7 1.7 %copy-start.7 = (s32[12,1]{0,1:T(1,128)S(1)}, s32[12,1]{0,1:T(1,128)}, u32[]{:S(2)}) copy-start(s32[12,1]{0,1:T(1,128)} %param.15) | copy-start | bytes 148
  0.7 1.7 %copy-start.8 = (s32[12]{0:T(128)S(1)}, s32[12]{0:T(128)}, u32[]{:S(2)}) copy-start(s32[12]{0:T(128)} %param.16) | copy-start | bytes 148
  0.7 6.2 %copy-start = (f32[4,32,8,128]{3,2,1,0:T(8,128)S(1)}, f32[4,32,8,128]{3,2,1,0:T(8,128)}, u32[]{:S(2)}) copy-start(f32[4,32,8,128]{3,2,1,0:T(8,128)} %param.10) | copy-start | bytes 1572868
  2.3 4.6 %copy-start.1 = (f32[4,8,16,128]{3,2,1,0:T(8,128)S(1)}, f32[4,8,16,128]{3,2,1,0:T(8,128)}, u32[]{:S(2)}) copy-start(f32[4,8,16,128]{3,2,1,0:T(8,128)} %param.11) | copy-start | bytes 786436
  2.3 4.6 %copy-start.3 = (bf16[256,128]{1,0:T(8,128)(2,1)S(1)}, bf16[256,128]{1,0:T(8,128)(2,1)}, u32[]{:S(2)}) copy-start(bf16[256,128]{1,0:T(8,128)(2,1)} %constant.14.mix) | copy-start | bytes 196612
  2.8 4.6 %collective-permute-start = (f32[80,128]{1,0:T(8,128)S(1)}, f32[80,128]{1,0:T(8,128)S(1)}, u32[]{:S(2)}, u32[]{:S(2)}) collective-permute-start(f32[80,128]{1,0:T(8,128)S(1)} %bitcast.31), channel_id=1, source_target_pairs={{0,1},{1,0},{2,3},{3,2},{4,5},{5,4},{6,7},{7,6},{8,9},{9,8},{10,11... | collective-permute-start | bytes 122888 | tf_op jit(solution)/shard_map/ppermute | solution.py:409
  3.3 4.9 %collective-permute-start.1 = (f32[16,128]{1,0:T(8,128)S(1)}, f32[16,128]{1,0:T(8,128)S(1)}, u32[]{:S(2)}, u32[]{:S(2)}) collective-permute-start(f32[16,128]{1,0:T(8,128)S(1)} %get-tuple-element.23), channel_id=1, source_target_pairs={{0,7},{1,2},{2,1},{3,4},{4,3},{5,6},{6,5},{7,0},{8,15},{9,10},{10,... | collective-permute-start | bytes 24584 | tf_op jit(solution)/shard_map/ppermute | solution.py:391
  7.4 0.8 %copy-start.4 = (bf16[192,128]{1,0:T(8,128)(2,1)S(1)}, bf16[192,128]{1,0:T(8,128)(2,1)}, u32[]{:S(2)}) copy-start(bf16[192,128]{1,0:T(8,128)(2,1)} %constant.15.place) | copy-start | bytes 147460
  7.5 4.9 %collective-permute-start.3 = (f32[64,128]{1,0:T(8,128)S(1)}, f32[64,128]{1,0:T(8,128)S(1)}, u32[]{:S(2)}, u32[]{:S(2)}) collective-permute-start(f32[64,128]{1,0:T(8,128)S(1)} %bitcast.34), channel_id=1, source_target_pairs={{0,2},{1,3},{2,0},{3,1},{4,6},{5,7},{6,4},{7,5},{8,10},{9,11},{10,... | collective-permute-start | bytes 98312 | tf_op jit(solution)/shard_map/ppermute | solution.py:429
  8.4 7.9 %collective-permute-start.2 = (f32[160,128]{1,0:T(8,128)S(1)}, f32[160,128]{1,0:T(8,128)S(1)}, u32[]{:S(2)}, u32[]{:S(2)}) collective-permute-start(f32[160,128]{1,0:T(8,128)S(1)} %get-tuple-element.27), channel_id=1, source_target_pairs={{0,8},{8,16},{16,24},{24,0},{1,9},{9,17},{17,25},{25,1},{2,10},{10... | collective-permute-start | bytes 245768 | tf_op jit(solution)/shard_map/ppermute | solution.py:441
  10.2 6.1 %collective-permute-start.5 = (f32[160,128]{1,0:T(8,128)S(1)}, f32[160,128]{1,0:T(8,128)S(1)}, u32[]{:S(2)}, u32[]{:S(2)}) collective-permute-start(f32[160,128]{1,0:T(8,128)S(1)} %get-tuple-element.29), channel_id=1, source_target_pairs={{0,24},{8,0},{16,8},{24,16},{1,25},{9,1},{17,9},{25,17},{2,26},{10... | collective-permute-start | bytes 245768 | tf_op jit(solution)/shard_map/ppermute | solution.py:442
  12.4 4.0 %collective-permute-start.4 = (f32[64,128]{1,0:T(8,128)S(1)}, f32[64,128]{1,0:T(8,128)S(1)}, u32[]{:S(2)}, u32[]{:S(2)}) collective-permute-start(f32[64,128]{1,0:T(8,128)S(1)} %bitcast.36), channel_id=1, source_target_pairs={{0,4},{1,5},{2,6},{3,7},{4,0},{5,1},{6,2},{7,3},{8,12},{9,13},{10,... | collective-permute-start | bytes 98312 | tf_op jit(solution)/shard_map/ppermute | solution.py:429

commit v6 on v5

--- a/solution.py
+++ b/solution.py
@@ -233,8 +233,11 @@
     ay = near.shape[0] - 8
     later[...] = later_in[...]
     halos = side_halos(lax.axis_index("tile") % 2 == 0, near[:ay, :], far[:ay, :])
-    for ref, old, k in ((low, low_in, ay - 1), (top, top_in, 0)):
-        ref[:planes, :] = old[:planes, :] + dot_tn(halos, place[k * 16 : (k + 1) * 16, :])
+    columns = place.shape[1]
+    both = jnp.concatenate([place[(ay - 1) * 16 : ay * 16, :], place[:16, :]], axis=1)
+    corners = dot_tn(halos, both)
+    low[:planes, :] = low_in[:planes, :] + corners[:, :columns]
+    top[:planes, :] = top_in[:planes, :] + corners[:, columns:]
 
 
 def side_kernel(
@@ -322,6 +325,11 @@
         copies.append(pltpu.make_async_copy(src, dst, sems.at[len(copies)]))
         copies[-1].start()
 
+    for slot, k, beyond in ((0, 0, up), (1, ay - 1, down)):
+        rims_out[slot] = (
+            rims[slot * planes : (slot + 1) * planes, :] + (0.5 * viscosity) * beyond[:planes, :]
+        )
+        send(rims_out.at[slot], atmos_out.at[:, k, :])
     cells_out[...] = ocean_part[...]
     for y, beyond in (
         (0, jnp.where(band == 0, 0.0, up[planes:, :])),
@@ -332,11 +340,6 @@
     for f in range(fields):
         deep = pl.ds((f * olev + 1) * oy, (olev - 1) * oy)
         send(cells_out.at[deep, :], ocean_out.at[deep, :])
-    for slot, k, beyond in ((0, 0, up), (1, ay - 1, down)):
-        rims_out[slot] = (
-            rims[slot * planes : (slot + 1) * planes, :] + (0.5 * viscosity) * beyond[:planes, :]
-        )
-        send(rims_out.at[slot], atmos_out.at[:, k, :])
     forcing = remapped[...] + remap(came, fields, oy)
     for f in range(fields):
         top = pl.ds(f * olev * oy, oy)

time: 17.4 us -> 17.4 us (level)
  no operation moved by 1% of the time
where the time goes in v6:
time: 17.4 us; the launch traced here: 17.2 us
  starting transfers between devices  9.74 us (56%)
  Pallas kernels  4.64 us (27%)
  waiting for transfers between devices  1.91 us (11%)
  between operations  0.85 us (5%)
    ppermute x1, starting transfers between devices, body(): far = lax.ppermute(far_out, 'tile', pair_over(n))  3.56 us
    ppermute x1, starting transfers between devices, body(): lax.ppermute(top, 'comp', [(i, (i - 1) % bands) for i in range(bands)])  2.12 us
    ppermute x2, starting transfers between devices, body(): came = lax.ppermute(send, 'tile', [(i, i ^ bit) for i in range(n)])  1.79 us
    ppermute x1, starting transfers between devices, body(): up = lax.ppermute(low, 'comp', [(i, (i + 1) % bands) for i in range(bands)])  1.76 us
    pallas_call x1, Pallas kernels, body(): pl.pallas_call(functools.partial(edge_kernel, fields, levels, olev, oy),...  1.57 us
    ppermute x2, waiting for transfers between devices, body(): came = lax.ppermute(send, 'tile', [(i, i ^ bit) for i in range(n)])  1.21 us
    pallas_call x1, Pallas kernels, body(): pl.pallas_call(functools.partial(side_kernel, n, fields), out_shape=(by_p...  1.04 us
    pallas_call x1, Pallas kernels, body(): pl.pallas_call(functools.partial(finish_kernel, bands, fields, levels), o...  0.86 us
  transfers between devices with their start and end apart: 6, of which 2 were waited for; matrix products, arithmetic and copies ran while one was open for 0% of the time, Pallas kernels for 10%

profile of v6, /device:TPU:0, one launch (start us, length us, event | category | flops | bytes accessed | tf_op | source)
XLA Modules:
  0.0 17.2 jit_solution(15514343365400088484)
XLA Ops:
  0.6 0.0 copy-start.2
  0.6 0.0 copy-start.5
  0.7 0.0 copy-start.6
  0.7 0.0 copy-start.7
  0.7 0.0 copy-start.8
  0.7 1.6 %edges.1 = (f32[16,128]{1,0:T(8,128)S(1)}, f32[16,128]{1,0:T(8,128)S(1)}, f32[32,128]{1,0:T(8,128)S(1)}) custom-call(f32[1024,128]{1,0:T(8,128)} %bitcast.19, f32[512,128]{1,0:T(8,128)} %bitcast.21, bf16[128,1536]{1,0:T(8,128)(2,1)} %constant.13.edge_at), custom_call_target="tpu_custom_call" | custom-call | tf_op jit(solution)/shard_map/edges/pallas_call | solution.py:376
  2.3 0.0 copy-start.1
  2.3 0.0 copy-done.2
  2.3 0.0 copy-done.5
  2.3 0.0 copy-done.6
  2.3 0.0 copy-done.7
  2.3 0.0 copy-done.8
  2.3 0.0 copy-start.3
  2.3 0.5 %shares.1 = (f32[16,4,128]{2,1,0:T(4,128)S(1)}, f32[20,4,128]{2,1,0:T(4,128)S(1)}) custom-call(f32[1,4]{1,0:T(1,128)S(1)} %bitcast.27, s32[1,12]{1,0:T(1,128)S(1)} %bitcast.28, s32[1,12]{1,0:T(1,128)S(1)} %bitcast.29, s32[1,12]{1,0:T(1,128)S(1)} %bitcast.30, f32[32,128]{1,0:T(8,128)S(1)} %get-tuple-element.20.ground, bf16[12,128,128]{2,1,0:T(8,128)(2,1)S(1)} %copy-done.2, ...), custom_call_target="tpu_custom_call" | custom-call | tf_op jit(solution)/shard_map/shares/pallas_call | solution.py:396
  2.8 0.5 %collective-permute-start = (f32[80,128]{1,0:T(8,128)S(1)}, f32[80,128]{1,0:T(8,128)S(1)}, u32[]{:S(2)}, u32[]{:S(2)}) collective-permute-start(f32[80,128]{1,0:T(8,128)S(1)} %bitcast.31), channel_id=1, source_target_pairs={{0,1},{1,0},{2,3},{3,2},{4,5},{5,4},{6,7},{7,6},{8,9},{9,8},{10,11... | collective-permute-start | bytes 122888 | tf_op jit(solution)/shard_map/ppermute | solution.py:412
  3.3 3.6 %collective-permute-start.1 = (f32[16,128]{1,0:T(8,128)S(1)}, f32[16,128]{1,0:T(8,128)S(1)}, u32[]{:S(2)}, u32[]{:S(2)}) collective-permute-start(f32[16,128]{1,0:T(8,128)S(1)} %get-tuple-element.23), channel_id=1, source_target_pairs={{0,7},{1,2},{2,1},{3,4},{4,3},{5,6},{6,5},{7,0},{8,15},{9,10},{10,... | collective-permute-start | bytes 24584 | tf_op jit(solution)/shard_map/ppermute | solution.py:394
  6.9 0.0 copy-done.1
  6.9 0.5 %inner.1 = (f32[1024,128]{1,0:T(8,128)S(1)}, f32[160,128]{1,0:T(8,128)S(1)}, f32[160,128]{1,0:T(8,128)S(1)}, f32[512,128]{1,0:T(8,128)S(1)}) custom-call(f32[1024,128]{1,0:T(8,128)S(1)} %bitcast.20, f32[512,128]{1,0:T(8,128)S(1)} %bitcast.22, bf16[256,128]{1,0:T(8,128)(2,1)S(1)} %copy-done.3), custom_call_target="tpu_custom_call" | custom-call | flops 1000000 | bytes 1000000 | tf_op jit(solution)/shard_map/inner/pallas_call | solution.py:416
  7.4 0.0 collective-permute-done
  7.4 0.0 copy-start.4
  7.5 0.1 collective-permute-start.3
  7.6 0.7 %collective-permute-done.1.far = f32[16,128]{1,0:T(8,128)S(1)} collective-permute-done((f32[16,128]{1,0:T(8,128)S(1)}, f32[16,128]{1,0:T(8,128)S(1)}, u32[]{:S(2)}, u32[]{:S(2)}) %collective-permute-start.1) | collective-permute-done | bytes 8224 | tf_op jit(solution)/shard_map/ppermute | solution.py:394
  8.2 0.2 %corners.1 = (f32[160,128]{1,0:T(8,128)S(1)}, f32[160,128]{1,0:T(8,128)S(1)}, f32[64,128]{1,0:T(8,128)S(1)}) custom-call(f32[16,128]{1,0:T(8,128)S(1)} %slice.24.near, f32[16,128]{1,0:T(8,128)S(1)} %collective-permute-done.1.far, f32[160,128]{1,0:T(8,128)S(1)} %get-tuple-element.24.low_in, ...), custom_call_target="tpu_custom_call", output_to_operand_aliasing={{0}: (2, {}), {1}: (3, {})} | custom-call | flops 1000000000 | bytes 1000000 | tf_op jit(solution)/shard_map/corners/pallas_call | solution.py:434
  8.5 1.8 %collective-permute-start.2 = (f32[160,128]{1,0:T(8,128)S(1)}, f32[160,128]{1,0:T(8,128)S(1)}, u32[]{:S(2)}, u32[]{:S(2)}) collective-permute-start(f32[160,128]{1,0:T(8,128)S(1)} %get-tuple-element.27), channel_id=1, source_target_pairs={{0,8},{8,16},{16,24},{24,0},{1,9},{9,17},{17,25},{25,1},{2,10},{10... | collective-permute-start | bytes 245768 | tf_op jit(solution)/shard_map/ppermute | solution.py:444
  10.2 2.1 %collective-permute-start.5 = (f32[160,128]{1,0:T(8,128)S(1)}, f32[160,128]{1,0:T(8,128)S(1)}, u32[]{:S(2)}, u32[]{:S(2)}) collective-permute-start(f32[160,128]{1,0:T(8,128)S(1)} %get-tuple-element.29), channel_id=1, source_target_pairs={{0,24},{8,0},{16,8},{24,16},{1,25},{9,1},{17,9},{25,17},{2,26},{10... | collective-permute-start | bytes 245768 | tf_op jit(solution)/shard_map/ppermute | solution.py:445
  12.3 0.0 collective-permute-done.3
  12.4 1.7 %collective-permute-start.4 = (f32[64,128]{1,0:T(8,128)S(1)}, f32[64,128]{1,0:T(8,128)S(1)}, u32[]{:S(2)}, u32[]{:S(2)}) collective-permute-start(f32[64,128]{1,0:T(8,128)S(1)} %bitcast.36), channel_id=1, source_target_pairs={{0,4},{1,5},{2,6},{3,7},{4,0},{5,1},{6,2},{7,3},{8,12},{9,13},{10,... | collective-permute-start | bytes 98312 | tf_op jit(solution)/shard_map/ppermute | solution.py:432
  14.1 1.0 %sides.1 = (f32[128,8,128]{2,1,0:T(8,128)}, f32[256,128]{1,0:T(8,128)S(1)}, f32[512,128]{1,0:T(8,128)S(1)}, f32[64,128]{1,0:T(8,128)S(1)}) custom-call(f32[16,128]{1,0:T(8,128)S(1)} %slice.24.near, f32[16,128]{1,0:T(8,128)S(1)} %collective-permute-done.1.far, f32[1024,128]{1,0:T(8,128)S(1)} %get-tuple-element.30.atmos_in, ...), custom_call_target="tpu_custom_call" | custom-call | flops 100000000 | bytes 1000000 | tf_op jit(solution)/shard_map/sides/pallas_call | solution.py:452
  15.1 1.2 %collective-permute-done.4.came = f32[64,128]{1,0:T(8,128)S(1)} collective-permute-done((f32[64,128]{1,0:T(8,128)S(1)}, f32[64,128]{1,0:T(8,128)S(1)}, u32[]{:S(2)}, u32[]{:S(2)}) %collective-permute-start.4) | collective-permute-done | bytes 32800 | tf_op jit(solution)/shard_map/ppermute | solution.py:432
  16.3 0.0 collective-permute-done.2.up
  16.3 0.0 collective-permute-done.5.down
  16.3 0.9 %finish.1 = (f32[128,8,128]{2,1,0:T(8,128)}, f32[512,128]{1,0:T(8,128)}) custom-call(f32[160,128]{1,0:T(8,128)S(1)} %collective-permute-done.2.up, f32[64,128]{1,0:T(8,128)S(1)} %collective-permute-done.4.came, f32[160,128]{1,0:T(8,128)S(1)} %collective-permute-done.5.down, ...), custom_call_target="tpu_custom_call", output_to_operand_aliasing={{0}: (3, {})} | custom-call | tf_op jit(solution)/shard_map/finish/pallas_call | solution.py:470
  (11 shorter events, 0.0 us)
Async XLA Ops:
  0.6 1.7 %copy-start.2 = (bf16[12,128,128]{2,1,0:T(8,128)(2,1)S(1)}, bf16[12,128,128]{2,1,0:T(8,128)(2,1)}, u32[]{:S(2)}) copy-start(bf16[12,128,128]{2,1,0:T(8,128)(2,1)} %weight.1) | copy-start | bytes 1179652
  0.6 1.7 %copy-start.5 = (f32[4]{0:T(128)S(1)}, f32[4]{0:T(128)}, u32[]{:S(2)}) copy-start(f32[4]{0:T(128)} %param.12) | copy-start | bytes 52
  0.7 1.7 %copy-start.6 = (s32[12]{0:T(128)S(1)}, s32[12]{0:T(128)}, u32[]{:S(2)}) copy-start(s32[12]{0:T(128)} %param.14) | copy-start | bytes 148
  0.7 1.7 %copy-start.7 = (s32[12,1]{0,1:T(1,128)S(1)}, s32[12,1]{0,1:T(1,128)}, u32[]{:S(2)}) copy-start(s32[12,1]{0,1:T(1,128)} %param.15) | copy-start | bytes 148
  0.7 1.7 %copy-start.8 = (s32[12]{0:T(128)S(1)}, s32[12]{0:T(128)}, u32[]{:S(2)}) copy-start(s32[12]{0:T(128)} %param.16) | copy-start | bytes 148
  0.7 6.2 %copy-start = (f32[4,32,8,128]{3,2,1,0:T(8,128)S(1)}, f32[4,32,8,128]{3,2,1,0:T(8,128)}, u32[]{:S(2)}) copy-start(f32[4,32,8,128]{3,2,1,0:T(8,128)} %param.10) | copy-start | bytes 1572868
  2.3 4.6 %copy-start.1 = (f32[4,8,16,128]{3,2,1,0:T(8,128)S(1)}, f32[4,8,16,128]{3,2,1,0:T(8,128)}, u32[]{:S(2)}) copy-start(f32[4,8,16,128]{3,2,1,0:T(8,128)} %param.11) | copy-start | bytes 786436
  2.3 4.6 %copy-start.3 = (bf16[256,128]{1,0:T(8,128)(2,1)S(1)}, bf16[256,128]{1,0:T(8,128)(2,1)}, u32[]{:S(2)}) copy-start(bf16[256,128]{1,0:T(8,128)(2,1)} %constant.14.mix) | copy-start | bytes 196612
  2.8 4.6 %collective-permute-start = (f32[80,128]{1,0:T(8,128)S(1)}, f32[80,128]{1,0:T(8,128)S(1)}, u32[]{:S(2)}, u32[]{:S(2)}) collective-permute-start(f32[80,128]{1,0:T(8,128)S(1)} %bitcast.31), channel_id=1, source_target_pairs={{0,1},{1,0},{2,3},{3,2},{4,5},{5,4},{6,7},{7,6},{8,9},{9,8},{10,11... | collective-permute-start | bytes 122888 | tf_op jit(solution)/shard_map/ppermute | solution.py:412
  3.3 4.9 %collective-permute-start.1 = (f32[16,128]{1,0:T(8,128)S(1)}, f32[16,128]{1,0:T(8,128)S(1)}, u32[]{:S(2)}, u32[]{:S(2)}) collective-permute-start(f32[16,128]{1,0:T(8,128)S(1)} %get-tuple-element.23), channel_id=1, source_target_pairs={{0,7},{1,2},{2,1},{3,4},{4,3},{5,6},{6,5},{7,0},{8,15},{9,10},{10,... | collective-permute-start | bytes 24584 | tf_op jit(solution)/shard_map/ppermute | solution.py:394
  7.4 0.8 %copy-start.4 = (bf16[192,128]{1,0:T(8,128)(2,1)S(1)}, bf16[192,128]{1,0:T(8,128)(2,1)}, u32[]{:S(2)}) copy-start(bf16[192,128]{1,0:T(8,128)(2,1)} %constant.15.place) | copy-start | bytes 147460
  7.5 4.9 %collective-permute-start.3 = (f32[64,128]{1,0:T(8,128)S(1)}, f32[64,128]{1,0:T(8,128)S(1)}, u32[]{:S(2)}, u32[]{:S(2)}) collective-permute-start(f32[64,128]{1,0:T(8,128)S(1)} %bitcast.34), channel_id=1, source_target_pairs={{0,2},{1,3},{2,0},{3,1},{4,6},{5,7},{6,4},{7,5},{8,10},{9,11},{10,... | collective-permute-start | bytes 98312 | tf_op jit(solution)/shard_map/ppermute | solution.py:432
  8.5 7.9 %collective-permute-start.2 = (f32[160,128]{1,0:T(8,128)S(1)}, f32[160,128]{1,0:T(8,128)S(1)}, u32[]{:S(2)}, u32[]{:S(2)}) collective-permute-start(f32[160,128]{1,0:T(8,128)S(1)} %get-tuple-element.27), channel_id=1, source_target_pairs={{0,8},{8,16},{16,24},{24,0},{1,9},{9,17},{17,25},{25,1},{2,10},{10... | collective-permute-start | bytes 245768 | tf_op jit(solution)/shard_map/ppermute | solution.py:444
  10.2 6.1 %collective-permute-start.5 = (f32[160,128]{1,0:T(8,128)S(1)}, f32[160,128]{1,0:T(8,128)S(1)}, u32[]{:S(2)}, u32[]{:S(2)}) collective-permute-start(f32[160,128]{1,0:T(8,128)S(1)} %get-tuple-element.29), channel_id=1, source_target_pairs={{0,24},{8,0},{16,8},{24,16},{1,25},{9,1},{17,9},{25,17},{2,26},{10... | collective-permute-start | bytes 245768 | tf_op jit(solution)/shard_map/ppermute | solution.py:445
  12.4 4.0 %collective-permute-start.4 = (f32[64,128]{1,0:T(8,128)S(1)}, f32[64,128]{1,0:T(8,128)S(1)}, u32[]{:S(2)}, u32[]{:S(2)}) collective-permute-start(f32[64,128]{1,0:T(8,128)S(1)} %bitcast.36), channel_id=1, source_target_pairs={{0,4},{1,5},{2,6},{3,7},{4,0},{5,1},{6,2},{7,3},{8,12},{9,13},{10,... | collective-permute-start | bytes 98312 | tf_op jit(solution)/shard_map/ppermute | solution.py:432

commit v7 on v6

--- a/solution.py
+++ b/solution.py
@@ -330,21 +330,22 @@
             rims[slot * planes : (slot + 1) * planes, :] + (0.5 * viscosity) * beyond[:planes, :]
         )
         send(rims_out.at[slot], atmos_out.at[:, k, :])
-    cells_out[...] = ocean_part[...]
+    for f in range(fields):
+        cells_out[f] = ocean_part[f * olev * oy : (f + 1) * olev * oy, :]
     for y, beyond in (
         (0, jnp.where(band == 0, 0.0, up[planes:, :])),
         (oy - 1, jnp.where(band == bands - 1, 0.0, down[planes:, :])),
     ):
-        row = pl.ds(y, cells, stride=oy)
-        cells_out[row, :] = cells_out[row, :] + diffusion * beyond
-    for f in range(fields):
-        deep = pl.ds((f * olev + 1) * oy, (olev - 1) * oy)
-        send(cells_out.at[deep, :], ocean_out.at[deep, :])
+        row = pl.ds(y, olev, stride=oy)
+        for f in range(fields):
+            cells_out[f, row, :] = cells_out[f, row, :] + diffusion * beyond[f * olev : (f + 1) * olev]
+    deep = pl.ds(oy, (olev - 1) * oy)
+    send(cells_out.at[:, deep, :], ocean_out.at[:, deep, :])
     forcing = remapped[...] + remap(came, fields, oy)
     for f in range(fields):
-        top = pl.ds(f * olev * oy, oy)
-        cells_out[top, :] = cells_out[top, :] + forcing[f * oy : (f + 1) * oy]
-        send(cells_out.at[top, :], ocean_out.at[top, :])
+        cells_out[f, :oy, :] = cells_out[f, :oy, :] + forcing[f * oy : (f + 1) * oy]
+    top = pl.ds(0, oy)
+    send(cells_out.at[:, top, :], ocean_out.at[:, top, :])
     for copy in copies:
         copy.wait()
 
@@ -469,13 +470,13 @@
     )(near, far, atmos_part, ocean_part, keep, place)
     atmos_next, ocean_next = pl.pallas_call(
         functools.partial(finish_kernel, bands, fields, levels),
-        out_shape=(by_plane, part_shapes[1]),
+        out_shape=(by_plane, jax.ShapeDtypeStruct((fields, olev * oy, columns), f32)),
         in_specs=[vmem] * 3 + [hbm] + [vmem] * 3,
         out_specs=(hbm, hbm),
         scratch_shapes=[
             pltpu.VMEM((2, planes, columns), f32),
-            pltpu.VMEM(ocean.shape, f32),
-            pltpu.SemaphoreType.DMA((2 + 2 * fields,)),
+            pltpu.VMEM((fields, olev * oy, columns), f32),
+            pltpu.SemaphoreType.DMA((4,)),
         ],
         input_output_aliases={3: 0},
         compiler_params=params,

time: 17.4 us -> 17.4 us (level)
  no operation moved by 1% of the time
where the time goes in v7:
time: 17.4 us; the launch traced here: 17.2 us
  starting transfers between devices  9.74 us (56%)
  Pallas kernels  4.61 us (26%)
  waiting for transfers between devices  1.91 us (11%)
  between operations  0.85 us (5%)
    ppermute x1, starting transfers between devices, body(): far = lax.ppermute(far_out, 'tile', pair_over(n))  3.56 us
    ppermute x1, starting transfers between devices, body(): lax.ppermute(top, 'comp', [(i, (i - 1) % bands) for i in range(bands)])  2.12 us
    ppermute x2, starting transfers between devices, body(): came = lax.ppermute(send, 'tile', [(i, i ^ bit) for i in range(n)])  1.79 us
    ppermute x1, starting transfers between devices, body(): up = lax.ppermute(low, 'comp', [(i, (i + 1) % bands) for i in range(bands)])  1.76 us
    pallas_call x1, Pallas kernels, body(): pl.pallas_call(functools.partial(edge_kernel, fields, levels, olev, oy),...  1.57 us
    ppermute x2, waiting for transfers between devices, body(): came = lax.ppermute(send, 'tile', [(i, i ^ bit) for i in range(n)])  1.21 us
    pallas_call x1, Pallas kernels, body(): pl.pallas_call(functools.partial(side_kernel, n, fields), out_shape=(by_p...  1.04 us
    pallas_call x1, Pallas kernels, body(): pl.pallas_call(functools.partial(finish_kernel, bands, fields, levels), o...  0.83 us
  transfers between devices with their start and end apart: 6, of which 2 were waited for; matrix products, arithmetic and copies ran while one was open for 0% of the time, Pallas kernels for 10%

profile of v7, /device:TPU:0, one launch (start us, length us, event | category | flops | bytes accessed | tf_op | source)
XLA Modules:
  0.0 17.2 jit_solution(8327230906025993792)
XLA Ops:
  0.6 0.0 copy-start.2
  0.6 0.0 copy-start.5
  0.7 0.0 copy-start.6
  0.7 0.0 copy-start.7
  0.7 0.0 copy-start.8
  0.7 0.0 copy-start
  0.7 1.6 %edges.1 = (f32[16,128]{1,0:T(8,128)S(1)}, f32[16,128]{1,0:T(8,128)S(1)}, f32[32,128]{1,0:T(8,128)S(1)}) custom-call(f32[1024,128]{1,0:T(8,128)} %bitcast.19, f32[512,128]{1,0:T(8,128)} %bitcast.21, bf16[128,1536]{1,0:T(8,128)(2,1)} %constant.13.edge_at), custom_call_target="tpu_custom_call" | custom-call | tf_op jit(solution)/shard_map/edges/pallas_call | solution.py:377
  2.3 0.0 copy-start.1
  2.3 0.0 copy-done.2
  2.3 0.0 copy-done.5
  2.3 0.0 copy-done.6
  2.3 0.0 copy-done.7
  2.3 0.0 copy-start.3
  2.3 0.5 %shares.1 = (f32[16,4,128]{2,1,0:T(4,128)S(1)}, f32[20,4,128]{2,1,0:T(4,128)S(1)}) custom-call(f32[1,4]{1,0:T(1,128)S(1)} %bitcast.27, s32[1,12]{1,0:T(1,128)S(1)} %bitcast.28, s32[1,12]{1,0:T(1,128)S(1)} %bitcast.29, s32[1,12]{1,0:T(1,128)S(1)} %bitcast.30, f32[32,128]{1,0:T(8,128)S(1)} %get-tuple-element.20.ground, bf16[12,128,128]{2,1,0:T(8,128)(2,1)S(1)} %copy-done.2, ...), custom_call_target="tpu_custom_call" | custom-call | tf_op jit(solution)/shard_map/shares/pallas_call | solution.py:397
  2.8 0.5 %collective-permute-start = (f32[80,128]{1,0:T(8,128)S(1)}, f32[80,128]{1,0:T(8,128)S(1)}, u32[]{:S(2)}, u32[]{:S(2)}) collective-permute-start(f32[80,128]{1,0:T(8,128)S(1)} %bitcast.31), channel_id=1, source_target_pairs={{0,1},{1,0},{2,3},{3,2},{4,5},{5,4},{6,7},{7,6},{8,9},{9,8},{10,11... | collective-permute-start | bytes 122888 | tf_op jit(solution)/shard_map/ppermute | solution.py:413
  3.3 3.6 %collective-permute-start.1 = (f32[16,128]{1,0:T(8,128)S(1)}, f32[16,128]{1,0:T(8,128)S(1)}, u32[]{:S(2)}, u32[]{:S(2)}) collective-permute-start(f32[16,128]{1,0:T(8,128)S(1)} %get-tuple-element.23), channel_id=1, source_target_pairs={{0,7},{1,2},{2,1},{3,4},{4,3},{5,6},{6,5},{7,0},{8,15},{9,10},{10,... | collective-permute-start | bytes 24584 | tf_op jit(solution)/shard_map/ppermute | solution.py:395
  6.9 0.0 copy-done
  6.9 0.5 %inner.1 = (f32[1024,128]{1,0:T(8,128)S(1)}, f32[160,128]{1,0:T(8,128)S(1)}, f32[160,128]{1,0:T(8,128)S(1)}, f32[512,128]{1,0:T(8,128)S(1)}) custom-call(f32[1024,128]{1,0:T(8,128)S(1)} %bitcast.20, f32[512,128]{1,0:T(8,128)S(1)} %bitcast.22, bf16[256,128]{1,0:T(8,128)(2,1)S(1)} %copy-done.3), custom_call_target="tpu_custom_call" | custom-call | flops 1000000 | bytes 1000000 | tf_op jit(solution)/shard_map/inner/pallas_call | solution.py:417
  7.4 0.0 collective-permute-done
  7.4 0.0 copy-start.4
  7.5 0.1 collective-permute-start.3
  7.6 0.7 %collective-permute-done.1.far = f32[16,128]{1,0:T(8,128)S(1)} collective-permute-done((f32[16,128]{1,0:T(8,128)S(1)}, f32[16,128]{1,0:T(8,128)S(1)}, u32[]{:S(2)}, u32[]{:S(2)}) %collective-permute-start.1) | collective-permute-done | bytes 8224 | tf_op jit(solution)/shard_map/ppermute | solution.py:395
  8.2 0.2 %corners.1 = (f32[160,128]{1,0:T(8,128)S(1)}, f32[160,128]{1,0:T(8,128)S(1)}, f32[64,128]{1,0:T(8,128)S(1)}) custom-call(f32[16,128]{1,0:T(8,128)S(1)} %slice.24.near, f32[16,128]{1,0:T(8,128)S(1)} %collective-permute-done.1.far, f32[160,128]{1,0:T(8,128)S(1)} %get-tuple-element.24.low_in, ...), custom_call_target="tpu_custom_call", output_to_operand_aliasing={{0}: (2, {}), {1}: (3, {})} | custom-call | flops 1000000000 | bytes 1000000 | tf_op jit(solution)/shard_map/corners/pallas_call | solution.py:435
  8.5 1.8 %collective-permute-start.2 = (f32[160,128]{1,0:T(8,128)S(1)}, f32[160,128]{1,0:T(8,128)S(1)}, u32[]{:S(2)}, u32[]{:S(2)}) collective-permute-start(f32[160,128]{1,0:T(8,128)S(1)} %get-tuple-element.27), channel_id=1, source_target_pairs={{0,8},{8,16},{16,24},{24,0},{1,9},{9,17},{17,25},{25,1},{2,10},{10... | collective-permute-start | bytes 245768 | tf_op jit(solution)/shard_map/ppermute | solution.py:445
  10.2 2.1 %collective-permute-start.5 = (f32[160,128]{1,0:T(8,128)S(1)}, f32[160,128]{1,0:T(8,128)S(1)}, u32[]{:S(2)}, u32[]{:S(2)}) collective-permute-start(f32[160,128]{1,0:T(8,128)S(1)} %get-tuple-element.29), channel_id=1, source_target_pairs={{0,24},{8,0},{16,8},{24,16},{1,25},{9,1},{17,9},{25,17},{2,26},{10... | collective-permute-start | bytes 245768 | tf_op jit(solution)/shard_map/ppermute | solution.py:446
  12.3 0.0 collective-permute-done.3
  12.4 1.7 %collective-permute-start.4 = (f32[64,128]{1,0:T(8,128)S(1)}, f32[64,128]{1,0:T(8,128)S(1)}, u32[]{:S(2)}, u32[]{:S(2)}) collective-permute-start(f32[64,128]{1,0:T(8,128)S(1)} %bitcast.36), channel_id=1, source_target_pairs={{0,4},{1,5},{2,6},{3,7},{4,0},{5,1},{6,2},{7,3},{8,12},{9,13},{10,... | collective-permute-start | bytes 98312 | tf_op jit(solution)/shard_map/ppermute | solution.py:433
  14.1 1.0 %sides.1 = (f32[128,8,128]{2,1,0:T(8,128)}, f32[256,128]{1,0:T(8,128)S(1)}, f32[512,128]{1,0:T(8,128)S(1)}, f32[64,128]{1,0:T(8,128)S(1)}) custom-call(f32[16,128]{1,0:T(8,128)S(1)} %slice.24.near, f32[16,128]{1,0:T(8,128)S(1)} %collective-permute-done.1.far, f32[1024,128]{1,0:T(8,128)S(1)} %get-tuple-element.30.atmos_in, ...), custom_call_target="tpu_custom_call" | custom-call | flops 100000000 | bytes 1000000 | tf_op jit(solution)/shard_map/sides/pallas_call | solution.py:453
  15.1 1.2 %collective-permute-done.4.came = f32[64,128]{1,0:T(8,128)S(1)} collective-permute-done((f32[64,128]{1,0:T(8,128)S(1)}, f32[64,128]{1,0:T(8,128)S(1)}, u32[]{:S(2)}, u32[]{:S(2)}) %collective-permute-start.4) | collective-permute-done | bytes 32800 | tf_op jit(solution)/shard_map/ppermute | solution.py:433
  16.3 0.0 collective-permute-done.2.up
  16.3 0.0 collective-permute-done.5.down
  16.3 0.8 %finish.1 = (f32[128,8,128]{2,1,0:T(8,128)}, f32[4,128,128]{2,1,0:T(8,128)}) custom-call(f32[160,128]{1,0:T(8,128)S(1)} %collective-permute-done.2.up, f32[64,128]{1,0:T(8,128)S(1)} %collective-permute-done.4.came, f32[160,128]{1,0:T(8,128)S(1)} %collective-permute-done.5.down, ...), custom_call_target="tpu_custom_call", output_to_operand_aliasing={{0}: (3, {})} | custom-call | tf_op jit(solution)/shard_map/finish/pallas_call | solution.py:471
  (11 shorter events, 0.0 us)
Async XLA Ops:
  0.6 1.7 %copy-start.2 = (bf16[12,128,128]{2,1,0:T(8,128)(2,1)S(1)}, bf16[12,128,128]{2,1,0:T(8,128)(2,1)}, u32[]{:S(2)}) copy-start(bf16[12,128,128]{2,1,0:T(8,128)(2,1)} %weight.1) | copy-start | bytes 1179652
  0.6 1.7 %copy-start.5 = (f32[4]{0:T(128)S(1)}, f32[4]{0:T(128)}, u32[]{:S(2)}) copy-start(f32[4]{0:T(128)} %param.12) | copy-start | bytes 52
  0.7 1.7 %copy-start.6 = (s32[12]{0:T(128)S(1)}, s32[12]{0:T(128)}, u32[]{:S(2)}) copy-start(s32[12]{0:T(128)} %param.14) | copy-start | bytes 148
  0.7 1.7 %copy-start.7 = (s32[12,1]{0,1:T(1,128)S(1)}, s32[12,1]{0,1:T(1,128)}, u32[]{:S(2)}) copy-start(s32[12,1]{0,1:T(1,128)} %param.15) | copy-start | bytes 148
  0.7 1.7 %copy-start.8 = (s32[12]{0:T(128)S(1)}, s32[12]{0:T(128)}, u32[]{:S(2)}) copy-start(s32[12]{0:T(128)} %param.16) | copy-start | bytes 148
  0.7 6.2 %copy-start = (f32[4,32,8,128]{3,2,1,0:T(8,128)S(1)}, f32[4,32,8,128]{3,2,1,0:T(8,128)}, u32[]{:S(2)}) copy-start(f32[4,32,8,128]{3,2,1,0:T(8,128)} %param.10) | copy-start | bytes 1572868
  2.3 4.6 %copy-start.1 = (f32[4,8,16,128]{3,2,1,0:T(8,128)S(1)}, f32[4,8,16,128]{3,2,1,0:T(8,128)}, u32[]{:S(2)}) copy-start(f32[4,8,16,128]{3,2,1,0:T(8,128)} %param.11) | copy-start | bytes 786436
  2.3 4.6 %copy-start.3 = (bf16[256,128]{1,0:T(8,128)(2,1)S(1)}, bf16[256,128]{1,0:T(8,128)(2,1)}, u32[]{:S(2)}) copy-start(bf16[256,128]{1,0:T(8,128)(2,1)} %constant.14.mix) | copy-start | bytes 196612
  2.8 4.6 %collective-permute-start = (f32[80,128]{1,0:T(8,128)S(1)}, f32[80,128]{1,0:T(8,128)S(1)}, u32[]{:S(2)}, u32[]{:S(2)}) collective-permute-start(f32[80,128]{1,0:T(8,128)S(1)} %bitcast.31), channel_id=1, source_target_pairs={{0,1},{1,0},{2,3},{3,2},{4,5},{5,4},{6,7},{7,6},{8,9},{9,8},{10,11... | collective-permute-start | bytes 122888 | tf_op jit(solution)/shard_map/ppermute | solution.py:413
  3.3 4.9 %collective-permute-start.1 = (f32[16,128]{1,0:T(8,128)S(1)}, f32[16,128]{1,0:T(8,128)S(1)}, u32[]{:S(2)}, u32[]{:S(2)}) collective-permute-start(f32[16,128]{1,0:T(8,128)S(1)} %get-tuple-element.23), channel_id=1, source_target_pairs={{0,7},{1,2},{2,1},{3,4},{4,3},{5,6},{6,5},{7,0},{8,15},{9,10},{10,... | collective-permute-start | bytes 24584 | tf_op jit(solution)/shard_map/ppermute | solution.py:395
  7.4 0.8 %copy-start.4 = (bf16[192,128]{1,0:T(8,128)(2,1)S(1)}, bf16[192,128]{1,0:T(8,128)(2,1)}, u32[]{:S(2)}) copy-start(bf16[192,128]{1,0:T(8,128)(2,1)} %constant.15.place) | copy-start | bytes 147460
  7.5 4.9 %collective-permute-start.3 = (f32[64,128]{1,0:T(8,128)S(1)}, f32[64,128]{1,0:T(8,128)S(1)}, u32[]{:S(2)}, u32[]{:S(2)}) collective-permute-start(f32[64,128]{1,0:T(8,128)S(1)} %bitcast.34), channel_id=1, source_target_pairs={{0,2},{1,3},{2,0},{3,1},{4,6},{5,7},{6,4},{7,5},{8,10},{9,11},{10,... | collective-permute-start | bytes 98312 | tf_op jit(solution)/shard_map/ppermute | solution.py:433
  8.5 7.9 %collective-permute-start.2 = (f32[160,128]{1,0:T(8,128)S(1)}, f32[160,128]{1,0:T(8,128)S(1)}, u32[]{:S(2)}, u32[]{:S(2)}) collective-permute-start(f32[160,128]{1,0:T(8,128)S(1)} %get-tuple-element.27), channel_id=1, source_target_pairs={{0,8},{8,16},{16,24},{24,0},{1,9},{9,17},{17,25},{25,1},{2,10},{10... | collective-permute-start | bytes 245768 | tf_op jit(solution)/shard_map/ppermute | solution.py:445
  10.2 6.1 %collective-permute-start.5 = (f32[160,128]{1,0:T(8,128)S(1)}, f32[160,128]{1,0:T(8,128)S(1)}, u32[]{:S(2)}, u32[]{:S(2)}) collective-permute-start(f32[160,128]{1,0:T(8,128)S(1)} %get-tuple-element.29), channel_id=1, source_target_pairs={{0,24},{8,0},{16,8},{24,16},{1,25},{9,1},{17,9},{25,17},{2,26},{10... | collective-permute-start | bytes 245768 | tf_op jit(solution)/shard_map/ppermute | solution.py:446
  12.4 4.0 %collective-permute-start.4 = (f32[64,128]{1,0:T(8,128)S(1)}, f32[64,128]{1,0:T(8,128)S(1)}, u32[]{:S(2)}, u32[]{:S(2)}) collective-permute-start(f32[64,128]{1,0:T(8,128)S(1)} %bitcast.36), channel_id=1, source_target_pairs={{0,4},{1,5},{2,6},{3,7},{4,0},{5,1},{6,2},{7,3},{8,12},{9,13},{10,... | collective-permute-start | bytes 98312 | tf_op jit(solution)/shard_map/ppermute | solution.py:433

commit v8 on v7

--- a/solution.py
+++ b/solution.py
@@ -137,6 +137,10 @@
     far[ay:, :] = ocean_cols
 
 
+def swapped(offset):
+    return (offset & ~6) | (offset & 2) << 1 | (offset & 4) >> 1
+
+
 def share_kernel(
     n, fields, coef_in, source_in, target_in, target_row_in, ground, weight, near,
     keep, send, surf, blocks, counts,
@@ -168,7 +172,7 @@
             to = target[0, first + i]
             slot = counts[to]
             counts[to] = slot + 1
-            offset = to ^ me
+            offset = swapped(to ^ me)
             at = ((offset % 2) * (n // 2) + offset // 2) * (SLOTS + 1)
             blocks[at + slot] = results[i][:fields]
             blocks[at + SLOTS, pl.ds(slot, 1), :] = jnp.full(
@@ -430,7 +434,7 @@
     while bit < n:
         pairs = state.reshape(state.shape[0] // 2, 2, state.shape[1], BLOCK, columns)
         keep, send = pairs[:, 0].reshape(-1, columns), pairs[:, 1].reshape(-1, columns)
-        came = lax.ppermute(send, "tile", [(i, i ^ bit) for i in range(n)])
+        came = lax.ppermute(send, "tile", [(i, i ^ swapped(bit)) for i in range(n)])
         if bit == 2:
             low, top, keep = pl.pallas_call(
                 functools.partial(corner_kernel, planes),

time: 17.4 us -> 17.4 us (level)
  waiting for transfers between devices: 1.91 us -> 2.35 us
  starting transfers between devices: 9.74 us -> 9.3 us
    ppermute x2, waiting for transfers between devices: 1.21 us -> 2.14 us  [body(): came = lax.ppermute(send, 'tile', [(i, i ^ swapped(bit)) for i in range(n)])]
    ppermute x1, waiting for transfers between devices: 0.69 us -> 0.2 us  [body(): far = lax.ppermute(far_out, 'tile', pair_over(n))]
    ppermute x2, starting transfers between devices: 1.79 us -> 1.36 us  [body(): came = lax.ppermute(send, 'tile', [(i, i ^ swapped(bit)) for i in range(n)])]
where the time goes in v8:
time: 17.4 us; the launch traced here: 17.2 us
  starting transfers between devices  9.3 us (53%)
  Pallas kernels  4.62 us (27%)
  waiting for transfers between devices  2.35 us (14%)
  between operations  0.83 us (5%)
    ppermute x1, starting transfers between devices, body(): far = lax.ppermute(far_out, 'tile', pair_over(n))  3.56 us
    ppermute x2, waiting for transfers between devices, body(): came = lax.ppermute(send, 'tile', [(i, i ^ swapped(bit)) for i in range(n)])  2.14 us
    ppermute x1, starting transfers between devices, body(): lax.ppermute(top, 'comp', [(i, (i - 1) % bands) for i in range(bands)])  2.12 us
    ppermute x1, starting transfers between devices, body(): up = lax.ppermute(low, 'comp', [(i, (i + 1) % bands) for i in range(bands)])  1.76 us
    pallas_call x1, Pallas kernels, body(): pl.pallas_call(functools.partial(edge_kernel, fields, levels, olev, oy),...  1.57 us
    ppermute x2, starting transfers between devices, body(): came = lax.ppermute(send, 'tile', [(i, i ^ swapped(bit)) for i in range(n)])  1.36 us
    pallas_call x1, Pallas kernels, body(): pl.pallas_call(functools.partial(side_kernel, n, fields), out_shape=(by_p...  1.05 us
    pallas_call x1, Pallas kernels, body(): pl.pallas_call(functools.partial(finish_kernel, bands, fields, levels), o...  0.83 us
  transfers between devices with their start and end apart: 6, of which 2 were waited for; matrix products, arithmetic and copies ran while one was open for 0% of the time, Pallas kernels for 10%

profile of v8, /device:TPU:0, one launch (start us, length us, event | category | flops | bytes accessed | tf_op | source)
XLA Modules:
  0.0 17.2 jit_solution(2507040100846969701)
XLA Ops:
  0.6 0.0 copy-start.2
  0.6 0.0 copy-start.5
  0.7 0.0 copy-start.6
  0.7 0.0 copy-start.7
  0.7 0.0 copy-start.8
  0.7 0.0 copy-start
  0.7 1.6 %edges.1 = (f32[16,128]{1,0:T(8,128)S(1)}, f32[16,128]{1,0:T(8,128)S(1)}, f32[32,128]{1,0:T(8,128)S(1)}) custom-call(f32[1024,128]{1,0:T(8,128)} %bitcast.19, f32[512,128]{1,0:T(8,128)} %bitcast.21, bf16[128,1536]{1,0:T(8,128)(2,1)} %constant.13.edge_at), custom_call_target="tpu_custom_call" | custom-call | tf_op jit(solution)/shard_map/edges/pallas_call | solution.py:381
  2.3 0.0 copy-start.1
  2.3 0.0 copy-done.2
  2.3 0.0 copy-done.5
  2.3 0.0 copy-done.6
  2.3 0.0 copy-done.7
  2.3 0.0 copy-start.3
  2.3 0.5 %shares.1 = (f32[16,4,128]{2,1,0:T(4,128)S(1)}, f32[20,4,128]{2,1,0:T(4,128)S(1)}) custom-call(f32[1,4]{1,0:T(1,128)S(1)} %bitcast.27, s32[1,12]{1,0:T(1,128)S(1)} %bitcast.28, s32[1,12]{1,0:T(1,128)S(1)} %bitcast.29, s32[1,12]{1,0:T(1,128)S(1)} %bitcast.30, f32[32,128]{1,0:T(8,128)S(1)} %get-tuple-element.20.ground, bf16[12,128,128]{2,1,0:T(8,128)(2,1)S(1)} %copy-done.2, ...), custom_call_target="tpu_custom_call" | custom-call | tf_op jit(solution)/shard_map/shares/pallas_call | solution.py:401
  2.8 0.5 %collective-permute-start = (f32[80,128]{1,0:T(8,128)S(1)}, f32[80,128]{1,0:T(8,128)S(1)}, u32[]{:S(2)}, u32[]{:S(2)}) collective-permute-start(f32[80,128]{1,0:T(8,128)S(1)} %bitcast.31), channel_id=1, source_target_pairs={{0,1},{1,0},{2,3},{3,2},{4,5},{5,4},{6,7},{7,6},{8,9},{9,8},{10,11... | collective-permute-start | bytes 122888 | tf_op jit(solution)/shard_map/ppermute | solution.py:417
  3.3 3.6 %collective-permute-start.1 = (f32[16,128]{1,0:T(8,128)S(1)}, f32[16,128]{1,0:T(8,128)S(1)}, u32[]{:S(2)}, u32[]{:S(2)}) collective-permute-start(f32[16,128]{1,0:T(8,128)S(1)} %get-tuple-element.23), channel_id=1, source_target_pairs={{0,7},{1,2},{2,1},{3,4},{4,3},{5,6},{6,5},{7,0},{8,15},{9,10},{10,... | collective-permute-start | bytes 24584 | tf_op jit(solution)/shard_map/ppermute | solution.py:399
  6.9 0.0 copy-done
  6.9 0.5 %inner.1 = (f32[1024,128]{1,0:T(8,128)S(1)}, f32[160,128]{1,0:T(8,128)S(1)}, f32[160,128]{1,0:T(8,128)S(1)}, f32[512,128]{1,0:T(8,128)S(1)}) custom-call(f32[1024,128]{1,0:T(8,128)S(1)} %bitcast.20, f32[512,128]{1,0:T(8,128)S(1)} %bitcast.22, bf16[256,128]{1,0:T(8,128)(2,1)S(1)} %copy-done.3), custom_call_target="tpu_custom_call" | custom-call | flops 1000000 | bytes 1000000 | tf_op jit(solution)/shard_map/inner/pallas_call | solution.py:421
  7.4 0.0 collective-permute-done
  7.4 0.0 copy-start.4
  7.5 0.6 %collective-permute-start.3 = (f32[64,128]{1,0:T(8,128)S(1)}, f32[64,128]{1,0:T(8,128)S(1)}, u32[]{:S(2)}, u32[]{:S(2)}) collective-permute-start(f32[64,128]{1,0:T(8,128)S(1)} %bitcast.34), channel_id=1, source_target_pairs={{0,4},{1,5},{2,6},{3,7},{4,0},{5,1},{6,2},{7,3},{8,12},{9,13},{10,... | collective-permute-start | bytes 98312 | tf_op jit(solution)/shard_map/ppermute | solution.py:437
  8.0 0.2 %collective-permute-done.1.far = f32[16,128]{1,0:T(8,128)S(1)} collective-permute-done((f32[16,128]{1,0:T(8,128)S(1)}, f32[16,128]{1,0:T(8,128)S(1)}, u32[]{:S(2)}, u32[]{:S(2)}) %collective-permute-start.1) | collective-permute-done | bytes 8224 | tf_op jit(solution)/shard_map/ppermute | solution.py:399
  8.2 0.2 %corners.1 = (f32[160,128]{1,0:T(8,128)S(1)}, f32[160,128]{1,0:T(8,128)S(1)}, f32[64,128]{1,0:T(8,128)S(1)}) custom-call(f32[16,128]{1,0:T(8,128)S(1)} %slice.24.near, f32[16,128]{1,0:T(8,128)S(1)} %collective-permute-done.1.far, f32[160,128]{1,0:T(8,128)S(1)} %get-tuple-element.24.low_in, ...), custom_call_target="tpu_custom_call", output_to_operand_aliasing={{0}: (2, {}), {1}: (3, {})} | custom-call | flops 1000000000 | bytes 1000000 | tf_op jit(solution)/shard_map/corners/pallas_call | solution.py:439
  8.5 1.8 %collective-permute-start.2 = (f32[160,128]{1,0:T(8,128)S(1)}, f32[160,128]{1,0:T(8,128)S(1)}, u32[]{:S(2)}, u32[]{:S(2)}) collective-permute-start(f32[160,128]{1,0:T(8,128)S(1)} %get-tuple-element.27), channel_id=1, source_target_pairs={{0,8},{8,16},{16,24},{24,0},{1,9},{9,17},{17,25},{25,1},{2,10},{10... | collective-permute-start | bytes 245768 | tf_op jit(solution)/shard_map/ppermute | solution.py:449
  10.2 2.1 %collective-permute-start.5 = (f32[160,128]{1,0:T(8,128)S(1)}, f32[160,128]{1,0:T(8,128)S(1)}, u32[]{:S(2)}, u32[]{:S(2)}) collective-permute-start(f32[160,128]{1,0:T(8,128)S(1)} %get-tuple-element.29), channel_id=1, source_target_pairs={{0,24},{8,0},{16,8},{24,16},{1,25},{9,1},{17,9},{25,17},{2,26},{10... | collective-permute-start | bytes 245768 | tf_op jit(solution)/shard_map/ppermute | solution.py:450
  12.3 0.0 collective-permute-done.3
  12.4 0.8 %collective-permute-start.4 = (f32[64,128]{1,0:T(8,128)S(1)}, f32[64,128]{1,0:T(8,128)S(1)}, u32[]{:S(2)}, u32[]{:S(2)}) collective-permute-start(f32[64,128]{1,0:T(8,128)S(1)} %bitcast.36), channel_id=1, source_target_pairs={{0,2},{1,3},{2,0},{3,1},{4,6},{5,7},{6,4},{7,5},{8,10},{9,11},{10,... | collective-permute-start | bytes 98312 | tf_op jit(solution)/shard_map/ppermute | solution.py:437
  13.2 1.0 %sides.1 = (f32[128,8,128]{2,1,0:T(8,128)}, f32[256,128]{1,0:T(8,128)S(1)}, f32[512,128]{1,0:T(8,128)S(1)}, f32[64,128]{1,0:T(8,128)S(1)}) custom-call(f32[16,128]{1,0:T(8,128)S(1)} %slice.24.near, f32[16,128]{1,0:T(8,128)S(1)} %collective-permute-done.1.far, f32[1024,128]{1,0:T(8,128)S(1)} %get-tuple-element.30.atmos_in, ...), custom_call_target="tpu_custom_call" | custom-call | flops 100000000 | bytes 1000000 | tf_op jit(solution)/shard_map/sides/pallas_call | solution.py:457
  14.2 2.1 %collective-permute-done.4.came = f32[64,128]{1,0:T(8,128)S(1)} collective-permute-done((f32[64,128]{1,0:T(8,128)S(1)}, f32[64,128]{1,0:T(8,128)S(1)}, u32[]{:S(2)}, u32[]{:S(2)}) %collective-permute-start.4) | collective-permute-done | bytes 32800 | tf_op jit(solution)/shard_map/ppermute | solution.py:437
  16.3 0.0 collective-permute-done.2.up
  16.3 0.0 collective-permute-done.5.down
  16.3 0.8 %finish.1 = (f32[128,8,128]{2,1,0:T(8,128)}, f32[4,128,128]{2,1,0:T(8,128)}) custom-call(f32[160,128]{1,0:T(8,128)S(1)} %collective-permute-done.2.up, f32[64,128]{1,0:T(8,128)S(1)} %collective-permute-done.4.came, f32[160,128]{1,0:T(8,128)S(1)} %collective-permute-done.5.down, ...), custom_call_target="tpu_custom_call", output_to_operand_aliasing={{0}: (3, {})} | custom-call | tf_op jit(solution)/shard_map/finish/pallas_call | solution.py:475
  (11 shorter events, 0.0 us)
Async XLA Ops:
  0.6 1.7 %copy-start.2 = (bf16[12,128,128]{2,1,0:T(8,128)(2,1)S(1)}, bf16[12,128,128]{2,1,0:T(8,128)(2,1)}, u32[]{:S(2)}) copy-start(bf16[12,128,128]{2,1,0:T(8,128)(2,1)} %weight.1) | copy-start | bytes 1179652
  0.6 1.7 %copy-start.5 = (f32[4]{0:T(128)S(1)}, f32[4]{0:T(128)}, u32[]{:S(2)}) copy-start(f32[4]{0:T(128)} %param.12) | copy-start | bytes 52
  0.7 1.7 %copy-start.6 = (s32[12]{0:T(128)S(1)}, s32[12]{0:T(128)}, u32[]{:S(2)}) copy-start(s32[12]{0:T(128)} %param.14) | copy-start | bytes 148
  0.7 1.7 %copy-start.7 = (s32[12,1]{0,1:T(1,128)S(1)}, s32[12,1]{0,1:T(1,128)}, u32[]{:S(2)}) copy-start(s32[12,1]{0,1:T(1,128)} %param.15) | copy-start | bytes 148
  0.7 1.7 %copy-start.8 = (s32[12]{0:T(128)S(1)}, s32[12]{0:T(128)}, u32[]{:S(2)}) copy-start(s32[12]{0:T(128)} %param.16) | copy-start | bytes 148
  0.7 6.2 %copy-start = (f32[4,32,8,128]{3,2,1,0:T(8,128)S(1)}, f32[4,32,8,128]{3,2,1,0:T(8,128)}, u32[]{:S(2)}) copy-start(f32[4,32,8,128]{3,2,1,0:T(8,128)} %param.10) | copy-start | bytes 1572868
  2.3 4.6 %copy-start.1 = (f32[4,8,16,128]{3,2,1,0:T(8,128)S(1)}, f32[4,8,16,128]{3,2,1,0:T(8,128)}, u32[]{:S(2)}) copy-start(f32[4,8,16,128]{3,2,1,0:T(8,128)} %param.11) | copy-start | bytes 786436
  2.3 4.6 %copy-start.3 = (bf16[256,128]{1,0:T(8,128)(2,1)S(1)}, bf16[256,128]{1,0:T(8,128)(2,1)}, u32[]{:S(2)}) copy-start(bf16[256,128]{1,0:T(8,128)(2,1)} %constant.14.mix) | copy-start | bytes 196612
  2.8 4.6 %collective-permute-start = (f32[80,128]{1,0:T(8,128)S(1)}, f32[80,128]{1,0:T(8,128)S(1)}, u32[]{:S(2)}, u32[]{:S(2)}) collective-permute-start(f32[80,128]{1,0:T(8,128)S(1)} %bitcast.31), channel_id=1, source_target_pairs={{0,1},{1,0},{2,3},{3,2},{4,5},{5,4},{6,7},{7,6},{8,9},{9,8},{10,11... | collective-permute-start | bytes 122888 | tf_op jit(solution)/shard_map/ppermute | solution.py:417
  3.3 4.9 %collective-permute-start.1 = (f32[16,128]{1,0:T(8,128)S(1)}, f32[16,128]{1,0:T(8,128)S(1)}, u32[]{:S(2)}, u32[]{:S(2)}) collective-permute-start(f32[16,128]{1,0:T(8,128)S(1)} %get-tuple-element.23), channel_id=1, source_target_pairs={{0,7},{1,2},{2,1},{3,4},{4,3},{5,6},{6,5},{7,0},{8,15},{9,10},{10,... | collective-permute-start | bytes 24584 | tf_op jit(solution)/shard_map/ppermute | solution.py:399
  7.4 0.8 %copy-start.4 = (bf16[192,128]{1,0:T(8,128)(2,1)S(1)}, bf16[192,128]{1,0:T(8,128)(2,1)}, u32[]{:S(2)}) copy-start(bf16[192,128]{1,0:T(8,128)(2,1)} %constant.15.place) | copy-start | bytes 147460
  7.5 4.9 %collective-permute-start.3 = (f32[64,128]{1,0:T(8,128)S(1)}, f32[64,128]{1,0:T(8,128)S(1)}, u32[]{:S(2)}, u32[]{:S(2)}) collective-permute-start(f32[64,128]{1,0:T(8,128)S(1)} %bitcast.34), channel_id=1, source_target_pairs={{0,4},{1,5},{2,6},{3,7},{4,0},{5,1},{6,2},{7,3},{8,12},{9,13},{10,... | collective-permute-start | bytes 98312 | tf_op jit(solution)/shard_map/ppermute | solution.py:437
  8.5 7.9 %collective-permute-start.2 = (f32[160,128]{1,0:T(8,128)S(1)}, f32[160,128]{1,0:T(8,128)S(1)}, u32[]{:S(2)}, u32[]{:S(2)}) collective-permute-start(f32[160,128]{1,0:T(8,128)S(1)} %get-tuple-element.27), channel_id=1, source_target_pairs={{0,8},{8,16},{16,24},{24,0},{1,9},{9,17},{17,25},{25,1},{2,10},{10... | collective-permute-start | bytes 245768 | tf_op jit(solution)/shard_map/ppermute | solution.py:449
  10.2 6.1 %collective-permute-start.5 = (f32[160,128]{1,0:T(8,128)S(1)}, f32[160,128]{1,0:T(8,128)S(1)}, u32[]{:S(2)}, u32[]{:S(2)}) collective-permute-start(f32[160,128]{1,0:T(8,128)S(1)} %get-tuple-element.29), channel_id=1, source_target_pairs={{0,24},{8,0},{16,8},{24,16},{1,25},{9,1},{17,9},{25,17},{2,26},{10... | collective-permute-start | bytes 245768 | tf_op jit(solution)/shard_map/ppermute | solution.py:450
  12.4 4.0 %collective-permute-start.4 = (f32[64,128]{1,0:T(8,128)S(1)}, f32[64,128]{1,0:T(8,128)S(1)}, u32[]{:S(2)}, u32[]{:S(2)}) collective-permute-start(f32[64,128]{1,0:T(8,128)S(1)} %bitcast.36), channel_id=1, source_target_pairs={{0,2},{1,3},{2,0},{3,1},{4,6},{5,7},{6,4},{7,5},{8,10},{9,11},{10,... | collective-permute-start | bytes 98312 | tf_op jit(solution)/shard_map/ppermute | solution.py:437
